TPU v7x, 512 devices: a whole 4x8x8 slice. The times are simulated.
512 devices in a mesh: dp: 32 (over z, x_hi, core), dap: 16 (over x_lo, y).
Axes of the slice: x: 4 (x_hi: 2, x_lo: 2; x = x_hi * 2 + x_lo), y: 8, z: 8, core: 2. Of those that a mesh axis runs over, the one named last changes fastest.
Arguments:
- pair_act: bfloat16 [32, 128, 128, 128], P('dp', 'dap'), may hold values from -6 to 6
- lengths: int32 [32], P('dp'), may hold values from 42 to 128, as said below
- cotangent: bfloat16 [32, 128, 128, 128], P('dp', 'dap'), may hold values from -6 to 6
- proj_weight: bfloat16 [128, 512], replicated, may hold values from -0.5 to 0.5
- gate_shift: float32 [128], replicated, may hold values from -4 to 4
- out_weight: bfloat16 [128, 128], replicated, may hold values from -3 to 3
- bias_weight: bfloat16 [128, 4], replicated, may hold values from -0.5 to 0.5
- norm_gain: float32 [128], replicated, may hold values from 0.5 to 1.5
Outputs:
- updated_pair: bfloat16 [32, 128, 128, 128], P('dp', 'dap')
- pair_grad: bfloat16 [32, 128, 128, 128], P('dp', 'dap')
- grad_proj: float32 [128, 512], replicated
- grad_shift: float32 [128], replicated
- grad_out: float32 [128, 128], replicated
- grad_bias: float32 [128, 4], replicated
- grad_gain: float32 [128], replicated
Inputs may be any that keep to these rules, and one draw needn't show every extreme that they name: `lengths`: residue count of each crop; in every draw some crop has exactly 128.
All inputs are finite; a program needn't handle non-finite values.
Results may differ from a plain program's by a relative error of at most 0.023.
Values may be sent and summed in bfloat16 or wider, within the bound.
No kernel may reach another device: no remote copies, remote signals or barrier semaphores. Data moves between devices by JAX's collectives and lax.ppermute only.
A program may use at most 64 MiB of HBM per device.

v0:
```python
import jax
import jax.numpy as jnp
from jax import lax
from jax.sharding import PartitionSpec as P

EPS = 1e-05


def normalize(pair_rows, norm_gain):
    as_float = pair_rows.astype(jnp.float32)
    centered = as_float - jnp.mean(as_float, -1, keepdims=True)
    inv_std = lax.rsqrt(jnp.mean(centered * centered, -1, keepdims=True) + EPS)
    x_hat = centered * inv_std
    return (x_hat, inv_std, (x_hat * norm_gain).astype(jnp.bfloat16))


def per_device(
    pair_act, lengths, cotangent, proj_weight, gate_shift, out_weight, bias_weight, norm_gain
):
    f32 = jnp.float32
    bf16 = jnp.bfloat16
    local_pair = pair_act[0]
    local_cot = cotangent[0]
    length = lengths[0]
    row_count, full_width, channels = local_pair.shape
    head_count = bias_weight.shape[1]
    head_size = channels // head_count
    scaling = head_size ** (-0.5)
    key_live = (jnp.arange(full_width) < length).astype(f32)
    own_rows = lax.axis_index("dap") * row_count + jnp.arange(row_count)
    row_live = (own_rows < length).astype(f32)
    pair_mask = row_live[:, None] * key_live[None, :]
    x_hat, inv_std, normed = normalize(local_pair, norm_gain)
    flat_rows = normed.reshape(row_count * full_width, channels)
    bias_local = jnp.dot(flat_rows, bias_weight, preferred_element_type=f32).reshape(
        row_count, full_width, head_count
    )
    bias_local = bias_local.transpose(0, 2, 1).astype(bf16)
    projected = jnp.dot(flat_rows, proj_weight, preferred_element_type=f32).reshape(
        row_count, full_width, 4 * channels
    )
    split_shape = (row_count, full_width, head_count, head_size)
    queries = (projected[..., :channels] * scaling).astype(bf16).reshape(split_shape)
    key_heads = projected[..., channels : 2 * channels].astype(bf16).reshape(split_shape)
    value_heads = projected[..., 2 * channels : 3 * channels].astype(bf16).reshape(split_shape)
    gating = jax.nn.sigmoid(projected[..., 3 * channels :] + gate_shift)

    def softmax_rows(query_block, bias_piece):
        scores = jnp.einsum("rjhd,rkhd->rjhk", query_block, key_heads, preferred_element_type=f32)
        scores = scores + bias_piece.astype(f32)[None]
        expo = jnp.exp(scores) * key_live
        return expo / jnp.sum(expo, -1, keepdims=True)

    bias_piece = lax.all_gather(bias_local, "dap", axis=0, tiled=True)
    piece_rows = bias_piece.shape[0]
    query_block = queries
    weights = softmax_rows(query_block, bias_piece).astype(bf16)
    result = jnp.einsum("rjhk,rkhd->rjhd", weights, value_heads, preferred_element_type=f32)
    attended = result.reshape(row_count, piece_rows, channels).astype(bf16)
    mixed = (gating * attended.astype(f32)).astype(bf16)
    output = jnp.dot(mixed.reshape(-1, channels), out_weight, preferred_element_type=f32)
    output = output.reshape(row_count, full_width, channels)
    updated = (local_pair.astype(f32) + output * pair_mask[..., None]).astype(bf16)
    d_output = (local_cot.astype(f32) * pair_mask[..., None]).astype(bf16)
    flat_output = d_output.reshape(-1, channels)
    grad_out = jnp.einsum(
        "nc,ne->ce", mixed.reshape(-1, channels), flat_output, preferred_element_type=f32
    )
    d_mixed = jnp.einsum("ne,ce->nc", flat_output, out_weight, preferred_element_type=f32)
    d_mixed = d_mixed.reshape(row_count, full_width, channels)
    d_attend = (d_mixed * gating).astype(bf16).reshape(split_shape)
    d_gating = d_mixed * attended.astype(f32) * gating * (1.0 - gating)
    bias_piece = lax.all_gather(bias_local, "dap", axis=0, tiled=True)
    query_block = queries
    probs = softmax_rows(query_block, bias_piece)
    weights = probs.astype(bf16)
    grad_probs = jnp.einsum("rjhd,rkhd->rjhk", d_attend, value_heads, preferred_element_type=f32)
    d_value_all = jnp.einsum("rjhk,rjhd->rkhd", weights, d_attend, preferred_element_type=f32)
    d_scores = probs * (grad_probs - jnp.sum(probs * grad_probs, -1, keepdims=True))
    scores_low = d_scores.astype(bf16)
    d_query = jnp.einsum("rjhk,rkhd->rjhd", scores_low, key_heads, preferred_element_type=f32)
    d_query_all = d_query
    d_key_all = jnp.einsum("rjhk,rjhd->rkhd", scores_low, query_block, preferred_element_type=f32)
    bias_part = jnp.sum(d_scores, 0)
    carried = (d_query_all, d_key_all, d_value_all, bias_part)
    d_query_all, d_key_all, d_value_all, bias_part = carried
    flat_shape = (row_count, full_width, channels)
    d_proj = jnp.concatenate(
        [
            d_query_all.reshape(flat_shape) * scaling,
            d_key_all.reshape(flat_shape),
            d_value_all.reshape(flat_shape),
            d_gating,
        ],
        -1,
    ).astype(bf16)
    flat_grad = d_proj.reshape(-1, 4 * channels)
    grad_proj = jnp.einsum("nc,ne->ce", flat_rows, flat_grad, preferred_element_type=f32)
    grad_shift = jnp.sum(d_proj[..., 3 * channels :].astype(f32), (0, 1))
    normed_proj = jnp.einsum(
        "ne,ce->nc", flat_grad, proj_weight, preferred_element_type=f32
    ).reshape(flat_shape)
    bias_sum = lax.psum_scatter(
        bias_part.astype(jnp.bfloat16), "dap", scatter_dimension=0, tiled=True
    ).astype(jnp.float32)
    bias_grad = bias_sum.astype(bf16)
    grad_bias = jnp.einsum("jkc,jhk->ch", normed, bias_grad, preferred_element_type=f32)
    d_normed = normed_proj + jnp.einsum(
        "jhk,ch->jkc", bias_grad, bias_weight, preferred_element_type=f32
    )
    grad_gain = jnp.sum(d_normed * x_hat, (0, 1))
    d_x_hat = d_normed * norm_gain
    d_pair = inv_std * (
        d_x_hat
        - jnp.mean(d_x_hat, -1, keepdims=True)
        - x_hat * jnp.mean(d_x_hat * x_hat, -1, keepdims=True)
    )
    pair_grad = (local_cot.astype(f32) + d_pair).astype(bf16)
    packed = jnp.concatenate(
        [grad_proj, grad_out, grad_bias, grad_shift[:, None], grad_gain[:, None]], 1
    )
    summed = lax.psum(packed, ("dp", "dap")) / full_width
    grad_proj_all = summed[:, : 4 * channels]
    grad_out_all = summed[:, 4 * channels : 5 * channels]
    grad_bias_all = summed[:, 5 * channels : 5 * channels + head_count]
    grad_shift_all = summed[:, 5 * channels + head_count]
    grad_gain_all = summed[:, 5 * channels + head_count + 1]
    return (
        updated[None],
        pair_grad[None],
        grad_proj_all,
        grad_shift_all,
        grad_out_all,
        grad_bias_all,
        grad_gain_all,
    )


def solution(mesh):
    in_specs = (
        P("dp", "dap", None, None),
        P("dp"),
        P("dp", "dap", None, None),
        P(),
        P(),
        P(),
        P(),
        P(),
    )
    out_specs = (P("dp", "dap", None, None), P("dp", "dap", None, None), P(), P(), P(), P(), P())
    return jax.shard_map(
        per_device, mesh=mesh, in_specs=in_specs, out_specs=out_specs, check_vma=False
    )
```

profile of v0, /device:TPU:1, one launch (start us, length us, event | category | flops | bytes accessed | tf_op | source)
XLA Modules:
  0.0 484.8 jit_solution(5046009006499561191)
XLA Ops:
  7.3 1.2 convert_reduce_fusion
  8.4 1.3 fusion.26
  9.8 1.4 fusion.11
  11.2 28.5 %all_gather.4 = bf16[128,4,128]{2,1,0:T(4,128)(2,1)S(1)} all-gather(bf16[8,4,128]{2,1,0:T(4,128)(2,1)S(1)} %fusion.11), channel_id=1, replica_groups=mesh['dp'=32,'dap'=16] {'dap'}, dimensions={0}, use_global_device_ids=true | all-gather | bytes 139264 | tf_op jit(solution)/shard_map/all_gather | solution.py:54
  40.5 1.0 fusion.60
  43.1 1.1 copy.94
  44.3 1.4 fusion.5
  45.7 1.3 fusion.9
  47.0 1.2 copy.100
  48.3 0.7 broadcast_multiply_fusion.1
  49.0 2.9 convert_reduce_fusion.1
  51.9 1.1 copy.102
  53.1 1.8 fusion
  54.9 2.5 fusion.13
  57.4 1.7 copy.111
  59.2 2.1 fusion.7
  61.3 2.3 convolution_convert_fusion.1
  63.6 0.7 convolution_convert_fusion
  65.1 0.8 copy.118
  65.9 1.7 fusion.10
  67.6 1.3 dynamic-slice
  69.6 0.7 convolution_bitcast_fusion
  70.9 122.9 %all-reduce.6.cloned.1.call-done = bf16[128,4,128]{2,1,0:T(4,128)(2,1)} async-done(((bf16[128,4,128]{2,1,0:T(4,128)(2,1)}), bf16[128,4,128]{2,1,0:T(4,128)(2,1)}) %all-reduce.6.cloned.1.call-update) | async-done | bytes 131088
  193.8 1.0 fusion.46
  194.8 0.7 fusion.25
  195.6 1.2 convolution_bitcast_fusion.1
  196.9 0.9 concatenate.16
  197.7 1.3 fusion.36
  199.1 275.2 %all-reduce.4.cloned.1.call-done = f32[128,646]{1,0:T(8,128)} async-done(((f32[128,646]{1,0:T(8,128)}), f32[128,646]{1,0:T(8,128)}) %all-reduce.4.cloned.1.call-update) | async-done | bytes 330768 | tf_op jit(solution)/shard_map/psum | solution.py:122
  474.2 1.0 broadcast_multiply_fusion
  475.3 0.7 slice.46
  476.6 0.7 slice_reduce_fusion
  (79 shorter events, 4.6 us)
Async XLA Ops:
  7.2 32.7 %copy-start = (bf16[128,512]{1,0:T(8,128)(2,1)S(1)}, bf16[128,512]{1,0:T(8,128)(2,1)}, u32[]{:S(2)}) copy-start(bf16[128,512]{1,0:T(8,128)(2,1)} %param.11) | copy-start | bytes 393220
  7.2 32.7 %copy-start.1 = (bf16[1,8,128,128]{3,2,1,0:T(8,128)(2,1)S(1)}, bf16[1,8,128,128]{3,2,1,0:T(8,128)(2,1)}, u32[]{:S(2)}) copy-start(bf16[1,8,128,128]{3,2,1,0:T(8,128)(2,1)} %param.8) | copy-start | bytes 786436
  7.2 32.7 %copy-start.24 = (f32[128]{0:T(128)S(1)}, f32[128]{0:T(128)}, u32[]{:S(2)}) copy-start(f32[128]{0:T(128)} %param.15) | copy-start | bytes 1540
  7.2 186.6 %all-reduce.6.cloned.1.call-start = ((), (), s32[]{:S(2)}) async-start(), calls=%async_computation.1 | async-start | bytes 262144
  8.4 32.0 %copy-start.15 = (f32[8,128]{1,0:T(8,128)}, f32[8,128]{1,0:T(8,128)S(1)}, u32[]{:S(2)}) copy-start(f32[8,128]{1,0:T(8,128)S(1)} %broadcast_multiply_fusion.4) | copy-start | bytes 12292
  9.8 30.7 %copy-start.19 = (f32[8,128]{1,0:T(8,128)}, f32[8,128]{1,0:T(8,128)S(1)}, u32[]{:S(2)}) copy-start(f32[8,128]{1,0:T(8,128)S(1)} %add_rsqrt_fusion) | copy-start | bytes 12292
  39.9 13.1 %copy-start.3 = (f32[128,4,128]{0,2,1:T(8,128)}, f32[128,4,128]{0,2,1:T(8,128)S(1)}, u32[]{:S(2)}) copy-start(f32[128,4,128]{0,2,1:T(8,128)S(1)} %copy.98) | copy-start | bytes 786436
  40.5 3.8 copy-start.2
  41.7 4.0 copy-start.5
  41.9 5.1 %copy-start.6 = (bf16[8,128,128]{1,2,0:T(8,128)(2,1)}, bf16[8,128,128]{1,2,0:T(8,128)(2,1)S(1)}, u32[]{:S(2)}) copy-start(bf16[8,128,128]{1,2,0:T(8,128)(2,1)S(1)} %copy.96) | copy-start | bytes 786436
  44.2 2.8 copy-start.14
  44.2 1.4 copy-start.21
  45.7 3.3 copy-start.7
  49.0 2.9 copy-start.17
  53.0 1.8 copy-start.12
  53.1 1.8 copy-start.22
  59.1 415.1 %all-reduce.4.cloned.1.call-start = ((), (), s32[]{:S(2)}) async-start(), calls=%async_computation | async-start | bytes 786432 | tf_op jit(solution)/shard_map/psum | solution.py:122
  59.2 4.4 copy-start.4
  59.2 4.4 copy-start.13
  59.2 4.4 copy-start.23
  63.6 1.0 copy-start.10
  63.6 1.1 copy-start.11
  63.6 2.3 copy-start.9
  64.3 5.2 %copy-start.16 = (f32[8,128]{1,0:T(8,128)S(1)}, f32[8,128]{1,0:T(8,128)}, u32[]{:S(2)}) copy-start(f32[8,128]{1,0:T(8,128)} %copy-done.15) | copy-start | bytes 12292
  64.3 5.2 %copy-start.20 = (f32[8,128]{1,0:T(8,128)S(1)}, f32[8,128]{1,0:T(8,128)}, u32[]{:S(2)}) copy-start(f32[8,128]{1,0:T(8,128)} %copy-done.19) | copy-start | bytes 12292
  64.3 5.2 %copy-start.25 = (f32[128]{0:T(128)S(1)}, f32[128]{0:T(128)}, u32[]{:S(2)}) copy-start(f32[128]{0:T(128)} %param.15) | copy-start | bytes 1540
  64.4 5.2 %copy-start.27 = (bf16[8,128,128]{2,1,0:T(8,128)(2,1)S(1)}, bf16[8,128,128]{2,1,0:T(8,128)(2,1)}, u32[]{:S(2)}) copy-start(bf16[8,128,128]{2,1,0:T(8,128)(2,1)} %get-tuple-element.41) | copy-start | bytes 786436
  69.5 1.0 copy-start.8
  69.5 0.9 copy-start.18
  69.6 124.3 %copy-start.26 = (bf16[128,4]{0,1:T(4,128)(2,1)S(1)}, bf16[128,4]{0,1:T(4,128)(2,1)}, u32[]{:S(2)}) copy-start(bf16[128,4]{0,1:T(4,128)(2,1)} %param.14) | copy-start | bytes 3076
Sparse Core Ops, SparseCore 0:
  59.2 134.5 all-reduce.5
  199.6 274.5 all-reduce.3
where the time goes:
time: 486 us; the launch traced here: 485 us
  waiting for transfers between devices  398 us (82%)
  blocking collectives  28.5 us (6%)
  matrix products  20.1 us (4%)
  between operations  15.9 us (3%)
  local copies, waits for them, and re-layouts  13.4 us (3%)
  other arithmetic  8.71 us (2%)
    psum x1, waiting for transfers between devices, per_device(): summed = lax.psum(packed, ('dp', 'dap')) / full_width  275 us
    unnamed x3, waiting for transfers between devices  123 us
    all_gather x1, blocking collectives, per_device(): bias_piece = lax.all_gather(bias_local, 'dap', axis=0, tiled=True)  28.5 us
  transfers between devices with their start and end apart: 2, of which 2 were waited for; matrix products, arithmetic and copies ran while one was open for 2% of the time, Pallas kernels for 0%

commit v1 on v0

v1 whole, which is shorter than its diff:
```python
import functools

import jax
import jax.numpy as jnp
from jax import lax
from jax.experimental import pallas as pl
from jax.experimental.pallas import tpu as pltpu
from jax.sharding import PartitionSpec as P

EPS = 1e-05
DEAD = -1e30
F32 = jnp.float32
BF16 = jnp.bfloat16
VMEM_LIMIT = 40 * 1024 * 1024


def contract(a, b, a_axis, b_axis):
    return lax.dot_general(
        a, b, (((a_axis,), (b_axis,)), ((), ())), preferred_element_type=F32
    )


def standardize(rows):
    rows = rows.astype(F32)
    centered = rows - jnp.mean(rows, -1, keepdims=True)
    inv_std = lax.rsqrt(jnp.mean(centered * centered, -1, keepdims=True) + EPS)
    return centered * inv_std, inv_std


def head_masks(shape, axis, heads):
    size = shape[axis] // heads
    position = lax.broadcasted_iota(jnp.int32, shape, axis)
    return [(position >= h * size) & (position < (h + 1) * size) for h in range(heads)]


def stack_heads(block, masks):
    return jnp.concatenate([jnp.where(m, block, jnp.zeros_like(block)) for m in masks], 0)


def pick_heads(stacked, masks):
    size = stacked.shape[0] // len(masks)
    picked = stacked[:size]
    for h in range(1, len(masks)):
        picked = jnp.where(masks[h], stacked[h * size : (h + 1) * size], picked)
    return picked


def norm_kernel(pair_ref, gain_ref, bias_weight_ref, normed_ref, bias_ref, held):
    row_count = pair_ref.shape[0]
    heads = bias_weight_ref.shape[1]
    for row in range(row_count):
        x_hat, _ = standardize(pair_ref[row])
        normed = (x_hat * gain_ref[...]).astype(BF16)
        normed_ref[row] = normed
        held[pl.ds(row, heads, stride=row_count), :] = contract(
            bias_weight_ref[...], normed, 0, 1
        )
    bias_ref[...] = held[...].astype(BF16)


def attend_kernel(
    place_ref,
    pair_ref,
    cot_ref,
    normed_ref,
    bias_ref,
    proj_weight_ref,
    gate_shift_ref,
    out_weight_ref,
    updated_ref,
    normed_proj_ref,
    bias_part_ref,
    grad_proj_ref,
    grad_out_ref,
    grad_small_ref,
    bias_t,
    bias_sum,
    d_proj,
    mixed_all,
    d_output_all,
):
    row_count, width, channels = pair_ref.shape
    heads = bias_t.shape[0] // width
    head_size = channels // heads
    scaling = head_size ** (-0.5)
    length, first_row = place_ref[0], place_ref[1]
    devices = bias_ref.shape[0]
    key_live = lax.broadcasted_iota(jnp.int32, (width, width), 0) < length
    for h in range(heads):
        rows = [
            bias_ref[d].astype(F32)[h * row_count : (h + 1) * row_count]
            for d in range(devices)
        ]
        turned = jnp.concatenate(rows, 0).T
        bias_t[h * width : (h + 1) * width] = jnp.where(key_live, turned, DEAD)
    bias_sum[...] = jnp.zeros_like(bias_sum)
    lane_masks = head_masks((width, channels), 1, heads)
    weight_t = proj_weight_ref[...].T
    token_live = lax.broadcasted_iota(jnp.int32, (width, channels), 0)

    def one_row(row, carry):
        shift_sum, gain_sum = carry
        normed = normed_ref[row]
        projected = dot(normed, proj_weight_ref[...])
        queries = (projected[:, :channels] * scaling).astype(BF16)
        keys = projected[:, channels : 2 * channels].astype(BF16)
        values = projected[:, 2 * channels : 3 * channels].astype(BF16)
        gating = jax.nn.sigmoid(projected[:, 3 * channels :] + gate_shift_ref[...])
        turned = contract(weight_t[channels : 3 * channels], normed, 1, 1).astype(BF16)
        keys_t, values_t = turned[:channels], turned[channels:]
        live = token_live < jnp.where(first_row + row < length, length, 0)
        d_output = jnp.where(live, cot_ref[row].astype(F32), 0.0).astype(BF16)
        d_output_all[row] = d_output
        d_mixed = contract(d_output, out_weight_ref[...], 1, 1)
        d_attend = (d_mixed * gating).astype(BF16)
        scores = contract(stack_heads(keys, lane_masks), queries, 1, 1)
        grads = contract(stack_heads(values, lane_masks), d_attend, 1, 1)
        weights, lows, attended_t, d_query_t = [], [], [], []
        for h in range(heads):
            part = slice(h * width, (h + 1) * width)
            expo = jnp.exp(scores[part] + bias_t[part])
            probs = expo * (1.0 / jnp.sum(expo, 0, keepdims=True))
            weight = probs.astype(BF16)
            g = grads[part]
            d_scores = probs * (g - jnp.sum(probs * g, 0, keepdims=True))
            bias_sum[part] += d_scores
            low = d_scores.astype(BF16)
            weights.append(weight)
            lows.append(low)
            own = slice(h * head_size, (h + 1) * head_size)
            attended_t.append(dot(values_t[own], weight))
            d_query_t.append(dot(keys_t[own], low))
        attended = jnp.concatenate(attended_t, 0).T.astype(BF16).astype(F32)
        d_query = jnp.concatenate(d_query_t, 0).T
        d_value = pick_heads(dot(jnp.concatenate(weights, 0), d_attend), lane_masks)
        d_key = pick_heads(dot(jnp.concatenate(lows, 0), queries), lane_masks)
        mixed = (gating * attended).astype(BF16)
        mixed_all[row] = mixed
        output = dot(mixed, out_weight_ref[...])
        updated_ref[row] = (
            pair_ref[row].astype(F32) + jnp.where(live, output, 0.0)
        ).astype(BF16)
        d_gating = (d_mixed * attended * gating * (1.0 - gating)).astype(BF16)
        d_row = jnp.concatenate(
            [
                (d_query * scaling).astype(BF16),
                d_key.astype(BF16),
                d_value.astype(BF16),
                d_gating,
            ],
            1,
        )
        d_proj[row] = d_row
        normed_proj = dot(d_row, weight_t)
        normed_proj_ref[row] = normed_proj
        x_hat, _ = standardize(pair_ref[row])
        shift_sum = shift_sum + jnp.sum(d_gating.astype(F32), 0, keepdims=True)
        gain_sum = gain_sum + jnp.sum(normed_proj * x_hat, 0, keepdims=True)
        return shift_sum, gain_sum

    zero = jnp.zeros((1, channels), F32)
    shift_sum, gain_sum = lax.fori_loop(0, row_count, one_row, (zero, zero))
    for h in range(heads):
        turned = bias_sum[h * width : (h + 1) * width].T
        for d in range(devices):
            bias_t[pl.ds(d * heads * row_count + h * row_count, row_count), :] = turned[
                d * row_count : (d + 1) * row_count
            ]
    bias_part_ref[...] = bias_t[...].astype(BF16).reshape(bias_part_ref.shape)
    tokens = row_count * width
    normed = normed_ref[...].reshape(tokens, channels)
    grad_proj_ref[...] = contract(normed, d_proj[...].reshape(tokens, 4 * channels), 0, 0)
    grad_out_ref[...] = contract(
        mixed_all[...].reshape(tokens, channels),
        d_output_all[...].reshape(tokens, channels),
        0,
        0,
    )
    grad_small_ref[0:1] = shift_sum
    grad_small_ref[1:2] = gain_sum


def dot(a, b):
    return jnp.dot(a, b, preferred_element_type=F32)


def finish_kernel(
    pair_ref,
    cot_ref,
    normed_ref,
    normed_proj_ref,
    bias_grad_ref,
    gain_ref,
    bias_weight_ref,
    pair_grad_ref,
    grad_bias_ref,
    grad_gain_ref,
):
    row_count, width, channels = pair_ref.shape
    heads = bias_weight_ref.shape[1]
    bias_grad = bias_grad_ref[...].astype(F32)
    of_row = lax.broadcasted_iota(jnp.int32, bias_grad.shape, 0) % row_count
    weight_t = bias_weight_ref[...].astype(F32).T
    spread = jnp.concatenate(
        [jnp.broadcast_to(weight_t[h : h + 1], (row_count, channels)) for h in range(heads)], 0
    )
    grad_bias = jnp.zeros((heads * row_count, channels), F32)
    gain_sum = jnp.zeros((1, channels), F32)
    for row in range(row_count):
        own = jnp.where(of_row == row, bias_grad, 0.0)
        grad_bias = grad_bias + dot(own.astype(BF16), normed_ref[row])
        added = dot(own.T.astype(BF16), spread.astype(BF16))
        x_hat, inv_std = standardize(pair_ref[row])
        gain_sum = gain_sum + jnp.sum(added * x_hat, 0, keepdims=True)
        d_x_hat = (normed_proj_ref[row] + added) * gain_ref[...]
        d_pair = inv_std * (
            d_x_hat
            - jnp.mean(d_x_hat, -1, keepdims=True)
            - x_hat * jnp.mean(d_x_hat * x_hat, -1, keepdims=True)
        )
        pair_grad_ref[row] = (cot_ref[row].astype(F32) + d_pair).astype(BF16)
    for h in range(heads):
        grad_bias_ref[h : h + 1] = jnp.sum(
            grad_bias[h * row_count : (h + 1) * row_count], 0, keepdims=True
        )
    grad_gain_ref[...] = gain_sum


def per_device(
    pair_act, lengths, cotangent, proj_weight, gate_shift, out_weight, bias_weight, norm_gain
):
    pair, cot = pair_act[0], cotangent[0]
    row_count, width, channels = pair.shape
    heads = bias_weight.shape[1]
    gain = norm_gain[None]
    devices = width // row_count
    vmem = pl.BlockSpec(memory_space=pltpu.VMEM)
    smem = pl.BlockSpec(memory_space=pltpu.SMEM)
    params = pltpu.CompilerParams(vmem_limit_bytes=VMEM_LIMIT)
    rows_shape = (row_count, width, channels)
    normed, bias_local = pl.pallas_call(
        norm_kernel,
        out_shape=(
            jax.ShapeDtypeStruct(rows_shape, BF16),
            jax.ShapeDtypeStruct((heads * row_count, width), BF16),
        ),
        in_specs=[vmem] * 3,
        out_specs=(vmem, vmem),
        scratch_shapes=[pltpu.VMEM((heads * row_count, width), F32)],
        compiler_params=params,
        name="norm",
    )(pair, gain, bias_weight)
    bias_all = lax.all_gather(bias_local, "dap", axis=0)
    place = jnp.stack([lengths[0], lax.axis_index("dap") * row_count]).astype(jnp.int32)
    updated, normed_proj, bias_part, grad_proj, grad_out, grad_small = pl.pallas_call(
        attend_kernel,
        out_shape=(
            jax.ShapeDtypeStruct(rows_shape, BF16),
            jax.ShapeDtypeStruct(rows_shape, F32),
            jax.ShapeDtypeStruct((devices, heads * row_count, width), BF16),
            jax.ShapeDtypeStruct((channels, 4 * channels), F32),
            jax.ShapeDtypeStruct((channels, channels), F32),
            jax.ShapeDtypeStruct((2, channels), F32),
        ),
        in_specs=[smem] + [vmem] * 7,
        out_specs=(vmem,) * 6,
        scratch_shapes=[
            pltpu.VMEM((heads * width, width), F32),
            pltpu.VMEM((heads * width, width), F32),
            pltpu.VMEM((row_count, width, 4 * channels), BF16),
            pltpu.VMEM(rows_shape, BF16),
            pltpu.VMEM(rows_shape, BF16),
        ],
        compiler_params=params,
        name="attend",
    )(place, pair, cot, normed, bias_all, proj_weight, gate_shift[None], out_weight)
    bias_grad = lax.psum_scatter(bias_part, "dap", scatter_dimension=0)
    pair_grad, grad_bias, grad_gain = pl.pallas_call(
        finish_kernel,
        out_shape=(
            jax.ShapeDtypeStruct(rows_shape, BF16),
            jax.ShapeDtypeStruct((heads, channels), F32),
            jax.ShapeDtypeStruct((1, channels), F32),
        ),
        in_specs=[vmem] * 7,
        out_specs=(vmem,) * 3,
        compiler_params=params,
        name="finish",
    )(pair, cot, normed, normed_proj, bias_grad, gain, bias_weight)
    packed = jnp.concatenate(
        [grad_proj, grad_out, grad_bias.T, grad_small[0][:, None], (grad_small[1] + grad_gain[0])[:, None]], 1
    )
    summed = lax.psum(packed, ("dp", "dap")) / width
    return (
        updated[None],
        pair_grad[None],
        summed[:, : 4 * channels],
        summed[:, 5 * channels + heads],
        summed[:, 4 * channels : 5 * channels],
        summed[:, 5 * channels : 5 * channels + heads],
        summed[:, 5 * channels + heads + 1],
    )


def solution(mesh):
    rows = P("dp", "dap", None, None)
    return jax.shard_map(
        per_device,
        mesh=mesh,
        in_specs=(rows, P("dp"), rows, P(), P(), P(), P(), P()),
        out_specs=(rows, rows, P(), P(), P(), P(), P()),
        check_vma=False,
    )
```

time: 486 us -> 408 us (0.84)
  waiting for transfers between devices: 398 us -> 344 us
  matrix products: 20.1 us -> 0 us
  Pallas kernels: 0 us -> 11.2 us
  other arithmetic: 8.71 us -> 1.1 us
  local copies, waits for them, and re-layouts: 13.4 us -> 7.96 us
    unnamed x3 -> x2, waiting for transfers between devices: 123 us -> 0.03 us
    reduce_scatter x0 -> x1, waiting for transfers between devices: none -> 66 us  [per_device(): bias_grad = lax.psum_scatter(bias_part, 'dap', scatter_dimension=0)]
    dot_general x15 -> x0, matrix products: 20.1 us -> none  [the longest x1 2.89 us: per_device(): jnp.einsum('ne,ce->nc', flat_output, out_weight, preferred_element_type=f32)]
    pallas_call x0 -> x3, Pallas kernels: none -> 11.2 us  [the longest x1 8.23 us: per_device(): pl.pallas_call(attend_kernel, out_shape=(jax.ShapeDtypeStruct(rows_shape,...]
  transfers between devices with their start and end apart: 2 -> 2, of which waited for: 2 -> 2; matrix products, arithmetic and copies ran while one was open for 2% -> 0% of each run, Pallas kernels for 0% -> 0%
where the time goes in v1:
time: 408 us; the launch traced here: 407 us
  waiting for transfers between devices  344 us (84%)
  blocking collectives  28.7 us (7%)
  between operations  14.7 us (4%)
  Pallas kernels  11.2 us (3%)
  local copies, waits for them, and re-layouts  7.96 us (2%)
    psum x1, waiting for transfers between devices, per_device(): summed = lax.psum(packed, ('dp', 'dap')) / width  278 us
    reduce_scatter x1, waiting for transfers between devices, per_device(): bias_grad = lax.psum_scatter(bias_part, 'dap', scatter_dimension=0)  66 us
    all_gather x1, blocking collectives, per_device(): bias_all = lax.all_gather(bias_local, 'dap', axis=0)  28.7 us
    pallas_call x1, Pallas kernels, per_device(): pl.pallas_call(attend_kernel, out_shape=(jax.ShapeDtypeStruct(rows_shape,...  8.23 us
  transfers between devices with their start and end apart: 2, of which 2 were waited for; matrix products, arithmetic and copies ran while one was open for 0% of the time, Pallas kernels for 0%

profile of v1, /device:TPU:1, one launch (start us, length us, event | category | flops | bytes accessed | tf_op | source)
XLA Modules:
  0.0 407.4 jit_solution(10017343365418806566)
XLA Ops:
  7.2 0.0 reduce-scatter.2.cloned.1.call-start
  7.2 0.0 copy-start.9
  7.9 0.0 copy-done.9
  7.9 0.1 copy.21.bias_weight_ref
  8.0 0.7 copy-done.7
  8.7 0.9 copy-done
  9.6 0.8 norm.1
  10.4 28.7 %all-gather = bf16[512,128]{1,0:T(8,128)(2,1)S(1)} all-gather(bf16[32,128]{1,0:T(8,128)(2,1)S(1)} %get-tuple-element.19), channel_id=2, replica_groups=mesh['dp'=32,'dap'=16] {'dap'}, dimensions={0}, use_global_device_ids=true | all-gather | bytes 139264 | tf_op jit(solution)/shard_map/all_gather | solution.py:253
  39.1 0.1 pad_add_fusion.place_ref
  39.2 0.0 copy-done.1
  39.2 0.0 copy-done.5
  39.2 0.0 copy-done.4
  39.2 0.6 copy-done.8
  39.8 0.9 copy-done.2
  40.8 8.2 %attend.1 = (bf16[8,128,128]{2,1,0:T(8,128)(2,1)}, f32[8,128,128]{2,1,0:T(8,128)S(1)}, bf16[16,32,128]{2,1,0:T(8,128)(2,1)}, f32[128,512]{1,0:T(8,128)S(1)}, f32...) custom-call(s32[2]{0:T(128)S(1)} %pad_add_fusion.place_ref, bf16[8,128,128]{2,1,0:T(8,128)(2,1)S(1)} %bitcast.15, ...), custom_call_target="tpu_custom_call" | custom-call | tf_op jit(solution)/shard_map/attend/pallas_call | solution.py:255
  49.0 0.0 reduce-scatter.2.cloned.1.call-update
  49.0 0.0 all-reduce.2.cloned.1.call-start
  49.1 66.0 %reduce-scatter.2.cloned.1.call-done = bf16[1,32,128]{2,1,0:T(8,128)(2,1)} async-done(((bf16[16,32,128]{2,1,0:T(8,128)(2,1)}), bf16[1,32,128]{2,1,0:T(8,128)(2,1)}) %reduce-scatter.2.cloned.1.call-update) | async-done | bytes 8208 | tf_op jit(solution)/shard_map/reduce_scatter | solution.py:277
  115.1 0.0 copy-done.3
  115.2 0.7 copy-done.6
  115.8 2.2 finish.1
  118.0 0.1 copy.23
  118.2 0.1 copy.25
  118.3 0.1 copy.24
  118.4 0.8 concatenate.3
  119.2 0.0 all-reduce.2.cloned.1.call-update
  119.3 277.5 %all-reduce.2.cloned.1.call-done = f32[128,646]{1,0:T(8,128)} async-done(((f32[128,646]{1,0:T(8,128)}), f32[128,646]{1,0:T(8,128)}) %all-reduce.2.cloned.1.call-update) | async-done | bytes 330768 | tf_op jit(solution)/shard_map/psum | solution.py:293
  396.8 1.0 broadcast_multiply_fusion
  397.8 0.7 slice_reduce_fusion
  398.5 0.6 slice.30
  399.2 0.7 slice.28
  399.9 0.7 copy.26
  (11 shorter events, 0.0 us)
Async XLA Ops:
  7.2 108.0 %reduce-scatter.2.cloned.1.call-start = ((), (), s32[]{:S(2)}) async-start(), calls=%async_computation.1 | async-start | bytes 139264 | tf_op jit(solution)/shard_map/reduce_scatter | solution.py:277
  7.2 0.7 copy-start.9
  8.0 0.7 copy-start.7
  8.7 0.9 copy-start
  9.6 29.5 %copy-start.1 = (bf16[1,8,128,128]{3,2,1,0:T(8,128)(2,1)S(1)}, bf16[1,8,128,128]{3,2,1,0:T(8,128)(2,1)}, u32[]{:S(2)}) copy-start(bf16[1,8,128,128]{3,2,1,0:T(8,128)(2,1)} %param.8) | copy-start | bytes 786436
  9.6 29.5 %copy-start.5 = (bf16[128,128]{1,0:T(8,128)(2,1)S(1)}, bf16[128,128]{1,0:T(8,128)(2,1)}, u32[]{:S(2)}) copy-start(bf16[128,128]{1,0:T(8,128)(2,1)} %out_weight_ref.1) | copy-start | bytes 98308
  10.4 28.8 %copy-start.4 = (bf16[128,512]{1,0:T(8,128)(2,1)S(1)}, bf16[128,512]{1,0:T(8,128)(2,1)}, u32[]{:S(2)}) copy-start(bf16[128,512]{1,0:T(8,128)(2,1)} %proj_weight_ref.1) | copy-start | bytes 393220
  39.2 0.7 copy-start.8
  39.8 0.9 copy-start.2
  40.8 74.4 %copy-start.3 = (bf16[1,8,128,128]{3,2,1,0:T(8,128)(2,1)S(1)}, bf16[1,8,128,128]{3,2,1,0:T(8,128)(2,1)}, u32[]{:S(2)}) copy-start(bf16[1,8,128,128]{3,2,1,0:T(8,128)(2,1)} %param.10) | copy-start | bytes 786436
  49.0 347.7 %all-reduce.2.cloned.1.call-start = ((), (), s32[]{:S(2)}) async-start(), calls=%async_computation.2 | async-start | bytes 786432 | tf_op jit(solution)/shard_map/psum | solution.py:293
  115.1 0.7 copy-start.6
Sparse Core Ops, SparseCore 0:
  49.2 65.9 reduce-scatter.1
  120.9 275.8 all-reduce.1

commit v2 on v1

--- a/solution.py
+++ b/solution.py
@@ -47,15 +47,17 @@
 
 def norm_kernel(pair_ref, gain_ref, bias_weight_ref, normed_ref, bias_ref, held):
     row_count = pair_ref.shape[0]
-    heads = bias_weight_ref.shape[1]
+    heads = bias_weight_ref.shape[0]
     for row in range(row_count):
         x_hat, _ = standardize(pair_ref[row])
         normed = (x_hat * gain_ref[...]).astype(BF16)
         normed_ref[row] = normed
         held[pl.ds(row, heads, stride=row_count), :] = contract(
-            bias_weight_ref[...], normed, 0, 1
+            bias_weight_ref[...], normed, 1, 1
         )
-    bias_ref[...] = held[...].astype(BF16)
+    block = held[...].astype(BF16)
+    for peer in range(bias_ref.shape[0]):
+        bias_ref[peer] = block
 
 
 def attend_kernel(
@@ -69,15 +71,14 @@
     out_weight_ref,
     updated_ref,
     normed_proj_ref,
-    bias_part_ref,
-    grad_proj_ref,
-    grad_out_ref,
-    grad_small_ref,
+    parts_ref,
+    small_ref,
     bias_t,
     bias_sum,
     d_proj,
     mixed_all,
     d_output_all,
+    parts,
 ):
     row_count, width, channels = pair_ref.shape
     heads = bias_t.shape[0] // width
@@ -160,24 +161,32 @@
 
     zero = jnp.zeros((1, channels), F32)
     shift_sum, gain_sum = lax.fori_loop(0, row_count, one_row, (zero, zero))
+    shared = heads * row_count
     for h in range(heads):
         turned = bias_sum[h * width : (h + 1) * width].T
         for d in range(devices):
-            bias_t[pl.ds(d * heads * row_count + h * row_count, row_count), :] = turned[
+            parts[d, h * row_count : (h + 1) * row_count] = turned[
                 d * row_count : (d + 1) * row_count
             ]
-    bias_part_ref[...] = bias_t[...].astype(BF16).reshape(bias_part_ref.shape)
     tokens = row_count * width
     normed = normed_ref[...].reshape(tokens, channels)
-    grad_proj_ref[...] = contract(normed, d_proj[...].reshape(tokens, 4 * channels), 0, 0)
-    grad_out_ref[...] = contract(
+    grad_proj = contract(normed, d_proj[...].reshape(tokens, 4 * channels), 0, 0)
+    grad_out = contract(
         mixed_all[...].reshape(tokens, channels),
         d_output_all[...].reshape(tokens, channels),
         0,
         0,
     )
-    grad_small_ref[0:1] = shift_sum
-    grad_small_ref[1:2] = gain_sum
+    pieces = [grad_proj[:, i * channels : (i + 1) * channels] for i in range(4)] + [grad_out]
+    for d in range(devices):
+        for i, piece in enumerate(pieces):
+            start = shared + i * row_count
+            parts[d, start : start + row_count] = piece[d * row_count : (d + 1) * row_count]
+    unused = shared + len(pieces) * row_count
+    parts[:, unused:] = jnp.zeros((devices, parts.shape[1] - unused, width), F32)
+    parts_ref[...] = parts[...].astype(BF16)
+    small_ref[0:1] = gain_sum
+    small_ref[1:2] = shift_sum
 
 
 def dot(a, b):
@@ -189,27 +198,32 @@
     cot_ref,
     normed_ref,
     normed_proj_ref,
-    bias_grad_ref,
+    parts_ref,
+    small_ref,
     gain_ref,
     bias_weight_ref,
     pair_grad_ref,
-    grad_bias_ref,
-    grad_gain_ref,
+    sums_ref,
+    held,
 ):
     row_count, width, channels = pair_ref.shape
-    heads = bias_weight_ref.shape[1]
-    bias_grad = bias_grad_ref[...].astype(F32)
+    heads = bias_weight_ref.shape[0]
+    shared = heads * row_count
+    total = parts_ref[0].astype(F32)
+    for d in range(1, parts_ref.shape[0]):
+        total = total + parts_ref[d].astype(F32)
+    bias_grad = total[:shared].astype(BF16).astype(F32)
     of_row = lax.broadcasted_iota(jnp.int32, bias_grad.shape, 0) % row_count
-    weight_t = bias_weight_ref[...].astype(F32).T
+    weight_t = bias_weight_ref[...].astype(F32)
     spread = jnp.concatenate(
         [jnp.broadcast_to(weight_t[h : h + 1], (row_count, channels)) for h in range(heads)], 0
-    )
-    grad_bias = jnp.zeros((heads * row_count, channels), F32)
-    gain_sum = jnp.zeros((1, channels), F32)
+    ).astype(BF16)
+    grad_bias = jnp.zeros((shared, channels), F32)
+    gain_sum = small_ref[0:1]
     for row in range(row_count):
         own = jnp.where(of_row == row, bias_grad, 0.0)
         grad_bias = grad_bias + dot(own.astype(BF16), normed_ref[row])
-        added = dot(own.T.astype(BF16), spread.astype(BF16))
+        added = dot(own.T.astype(BF16), spread)
         x_hat, inv_std = standardize(pair_ref[row])
         gain_sum = gain_sum + jnp.sum(added * x_hat, 0, keepdims=True)
         d_x_hat = (normed_proj_ref[row] + added) * gain_ref[...]
@@ -219,11 +233,49 @@
             - x_hat * jnp.mean(d_x_hat * x_hat, -1, keepdims=True)
         )
         pair_grad_ref[row] = (cot_ref[row].astype(F32) + d_pair).astype(BF16)
+    grads = 5 * row_count
+    held[:grads] = total[shared : shared + grads]
+    held[grads:] = jnp.zeros((held.shape[0] - grads, channels), F32)
     for h in range(heads):
-        grad_bias_ref[h : h + 1] = jnp.sum(
+        held[grads + h : grads + h + 1] = jnp.sum(
             grad_bias[h * row_count : (h + 1) * row_count], 0, keepdims=True
         )
-    grad_gain_ref[...] = gain_sum
+    held[grads + heads : grads + heads + 1] = gain_sum
+    held[grads + heads + 1 : grads + heads + 2] = small_ref[1:2]
+    block = held[...].astype(BF16)
+    for peer in range(sums_ref.shape[0]):
+        sums_ref[peer] = block
+
+
+def sum_kernel(sums_ref, out_ref):
+    total = sums_ref[0].astype(F32)
+    for d in range(1, sums_ref.shape[0]):
+        total = total + sums_ref[d].astype(F32)
+    block = total.astype(BF16)
+    for peer in range(out_ref.shape[0]):
+        out_ref[peer] = block
+
+
+def assemble_kernel(
+    heads, scale, blocks_ref, grad_proj_ref, grad_shift_ref, grad_out_ref, grad_bias_ref, grad_gain_ref
+):
+    devices = blocks_ref.shape[0]
+    channels = grad_out_ref.shape[0]
+    row_count = channels // devices
+    grads = 5 * row_count
+    small = None
+    for d in range(devices):
+        block = blocks_ref[d].astype(F32) * scale
+        own = slice(d * row_count, (d + 1) * row_count)
+        for i in range(4):
+            grad_proj_ref[own, i * channels : (i + 1) * channels] = block[
+                i * row_count : (i + 1) * row_count
+            ]
+        grad_out_ref[own] = block[4 * row_count : grads]
+        small = block[grads:] if small is None else small + block[grads:]
+    grad_bias_ref[...] = small[:heads]
+    grad_gain_ref[...] = small[heads : heads + 1]
+    grad_shift_ref[...] = small[heads + 1 : heads + 2]
 
 
 def per_device(
@@ -232,73 +284,98 @@
     pair, cot = pair_act[0], cotangent[0]
     row_count, width, channels = pair.shape
     heads = bias_weight.shape[1]
-    gain = norm_gain[None]
-    devices = width // row_count
+    gain, bias_weight_t = norm_gain[None], bias_weight.T
+    devices, samples = lax.axis_size("dap"), lax.axis_size("dp")
+    shared = heads * row_count
+    chunk = -(-(5 * row_count + heads + 2) // 16) * 16
     vmem = pl.BlockSpec(memory_space=pltpu.VMEM)
     smem = pl.BlockSpec(memory_space=pltpu.SMEM)
     params = pltpu.CompilerParams(vmem_limit_bytes=VMEM_LIMIT)
     rows_shape = (row_count, width, channels)
-    normed, bias_local = pl.pallas_call(
+
+    def exchange(blocks, axis):
+        return lax.all_to_all(blocks, axis, 0, 0, tiled=True)
+
+    normed, bias_copies = pl.pallas_call(
         norm_kernel,
         out_shape=(
             jax.ShapeDtypeStruct(rows_shape, BF16),
-            jax.ShapeDtypeStruct((heads * row_count, width), BF16),
+            jax.ShapeDtypeStruct((devices, shared, width), BF16),
         ),
         in_specs=[vmem] * 3,
         out_specs=(vmem, vmem),
-        scratch_shapes=[pltpu.VMEM((heads * row_count, width), F32)],
+        scratch_shapes=[pltpu.VMEM((shared, width), F32)],
         compiler_params=params,
         name="norm",
-    )(pair, gain, bias_weight)
-    bias_all = lax.all_gather(bias_local, "dap", axis=0)
+    )(pair, gain, bias_weight_t)
+    bias_all = exchange(bias_copies, "dap")
     place = jnp.stack([lengths[0], lax.axis_index("dap") * row_count]).astype(jnp.int32)
-    updated, normed_proj, bias_part, grad_proj, grad_out, grad_small = pl.pallas_call(
+    updated, normed_proj, parts, small = pl.pallas_call(
         attend_kernel,
         out_shape=(
             jax.ShapeDtypeStruct(rows_shape, BF16),
             jax.ShapeDtypeStruct(rows_shape, F32),
-            jax.ShapeDtypeStruct((devices, heads * row_count, width), BF16),
-            jax.ShapeDtypeStruct((channels, 4 * channels), F32),
-            jax.ShapeDtypeStruct((channels, channels), F32),
+            jax.ShapeDtypeStruct((devices, shared + chunk, width), BF16),
             jax.ShapeDtypeStruct((2, channels), F32),
         ),
         in_specs=[smem] + [vmem] * 7,
-        out_specs=(vmem,) * 6,
+        out_specs=(vmem,) * 4,
         scratch_shapes=[
             pltpu.VMEM((heads * width, width), F32),
             pltpu.VMEM((heads * width, width), F32),
             pltpu.VMEM((row_count, width, 4 * channels), BF16),
             pltpu.VMEM(rows_shape, BF16),
             pltpu.VMEM(rows_shape, BF16),
+            pltpu.VMEM((devices, shared + chunk, width), F32),
         ],
         compiler_params=params,
         name="attend",
     )(place, pair, cot, normed, bias_all, proj_weight, gate_shift[None], out_weight)
-    bias_grad = lax.psum_scatter(bias_part, "dap", scatter_dimension=0)
-    pair_grad, grad_bias, grad_gain = pl.pallas_call(
+    parts = exchange(parts, "dap")
+    pair_grad, sums = pl.pallas_call(
         finish_kernel,
         out_shape=(
             jax.ShapeDtypeStruct(rows_shape, BF16),
+            jax.ShapeDtypeStruct((samples, chunk, channels), BF16),
+        ),
+        in_specs=[vmem] * 8,
+        out_specs=(vmem,) * 2,
+        scratch_shapes=[pltpu.VMEM((chunk, channels), F32)],
+        compiler_params=params,
+        name="finish",
+    )(pair, cot, normed, normed_proj, parts, small, gain, bias_weight_t)
+    sums = exchange(sums, "dp")
+    blocks = pl.pallas_call(
+        sum_kernel,
+        out_shape=jax.ShapeDtypeStruct((devices, chunk, channels), BF16),
+        in_specs=[vmem],
+        out_specs=vmem,
+        compiler_params=params,
+        name="sum",
+    )(sums)
+    blocks = exchange(blocks, "dap")
+    grad_proj, grad_shift, grad_out, grad_bias, grad_gain = pl.pallas_call(
+        functools.partial(assemble_kernel, heads, 1.0 / width),
+        out_shape=(
+            jax.ShapeDtypeStruct((channels, 4 * channels), F32),
+            jax.ShapeDtypeStruct((1, channels), F32),
+            jax.ShapeDtypeStruct((channels, channels), F32),
             jax.ShapeDtypeStruct((heads, channels), F32),
             jax.ShapeDtypeStruct((1, channels), F32),
         ),
-        in_specs=[vmem] * 7,
-        out_specs=(vmem,) * 3,
-        compiler_params=params,
-        name="finish",
-    )(pair, cot, normed, normed_proj, bias_grad, gain, bias_weight)
-    packed = jnp.concatenate(
-        [grad_proj, grad_out, grad_bias.T, grad_small[0][:, None], (grad_small[1] + grad_gain[0])[:, None]], 1
-    )
-    summed = lax.psum(packed, ("dp", "dap")) / width
+        in_specs=[vmem],
+        out_specs=(vmem,) * 5,
+        compiler_params=params,
+        name="assemble",
+    )(blocks)
     return (
         updated[None],
         pair_grad[None],
-        summed[:, : 4 * channels],
-        summed[:, 5 * channels + heads],
-        summed[:, 4 * channels : 5 * channels],
-        summed[:, 5 * channels : 5 * channels + heads],
-        summed[:, 5 * channels + heads + 1],
+        grad_proj,
+        grad_shift[0],
+        grad_out,
+        grad_bias.T,
+        grad_gain[0],
     )
 
 

time: 408 us -> 88.3 us (0.22)
  the two profiles are of different devices: /device:TPU:1 before, /device:TPU:8 now
where the time goes in v2:
time: 88.3 us; the launch traced here: 87.8 us
  blocking collectives  54.2 us (61%)
  Pallas kernels  11.9 us (13%)
  starting transfers between devices  9.12 us (10%)
  waiting for transfers between devices  7.26 us (8%)
  local copies, waits for them, and re-layouts  3.93 us (4%)
  between operations  1.32 us (1%)
    all_to_all x3, blocking collectives, exchange(): return lax.all_to_all(blocks, axis, 0, 0, tiled=True)  54.2 us
    all_to_all x1, starting transfers between devices, exchange(): return lax.all_to_all(blocks, axis, 0, 0, tiled=True)  9.12 us
    pallas_call x1, Pallas kernels, per_device(): pl.pallas_call(attend_kernel, out_shape=(jax.ShapeDtypeStruct(rows_shape,...  7.85 us
    all_to_all x1, waiting for transfers between devices, exchange(): return lax.all_to_all(blocks, axis, 0, 0, tiled=True)  7.26 us
    unnamed x16, local copies, waits for them, and re-layouts  3.93 us
    pallas_call x1, Pallas kernels, per_device(): pl.pallas_call(finish_kernel, out_shape=(jax.ShapeDtypeStruct(rows_shape,...  2.03 us
  transfers between devices with their start and end apart: 1, of which 1 were waited for; matrix products, arithmetic and copies ran while one was open for 0% of the time, Pallas kernels for 0%

profile of v2, /device:TPU:8, one launch (start us, length us, event | category | flops | bytes accessed | tf_op | source)
XLA Modules:
  0.0 87.8 jit_solution(15224582268440798879)
XLA Ops:
  0.6 0.0 copy-start.5
  0.6 0.0 copy-start.6
  0.7 0.7 copy-done.5
  1.3 0.0 copy-done.6
  1.3 0.0 copy-start
  1.3 0.9 %copy-done = bf16[1,8,128,128]{3,2,1,0:T(8,128)(2,1)S(1)} copy-done((bf16[1,8,128,128]{3,2,1,0:T(8,128)(2,1)S(1)}, bf16[1,8,128,128]{3,2,1,0:T(8,128)(2,1)}, u32[]{:S(2)}) %copy-start) | copy-done | bytes 262168
  2.3 0.0 copy-start.1
  2.3 0.0 copy-start.2
  2.3 1.2 %norm.1 = (bf16[8,128,128]{2,1,0:T(8,128)(2,1)S(1)}, bf16[16,32,128]{2,1,0:T(8,128)(2,1)}) custom-call(bf16[8,128,128]{2,1,0:T(8,128)(2,1)S(1)} %bitcast.11, f32[1,128]{1,0:T(1,128)S(1)} %bitcast.18, bf16[4,128]{1,0:T(4,128)(2,1)S(1)} %bitcast.16), custom_call_target="tpu_custom_call" | custom-call | tf_op jit(solution)/shard_map/norm/pallas_call | solution.py:299
  3.5 9.1 %all-to-all-start = ((bf16[16,32,128]{2,1,0:T(8,128)(2,1)}), bf16[16,32,128]{2,1,0:T(8,128)(2,1)S(1)}, u32[]{:S(2)}, u32[]{:S(2)}) async-start(bf16[16,32,128]{2,1,0:T(8,128)(2,1)} %get-tuple-element.21), calls=%async_computation | async-start | bytes 262144 | tf_op jit(solution)/shard_map/all_to_all | solution.py:297
  13.2 0.1 pad_add_fusion.place_ref
  13.3 7.3 %all-to-all-done.bias_ref = bf16[16,32,128]{2,1,0:T(8,128)(2,1)S(1)} async-done(((bf16[16,32,128]{2,1,0:T(8,128)(2,1)}), bf16[16,32,128]{2,1,0:T(8,128)(2,1)S(1)}, u32[]{:S(2)}, u32[]{:S(2)}) %all-to-all-start) | async-done | bytes 131104 | tf_op jit(solution)/shard_map/all_to_all | solution.py:297
  20.6 0.0 copy-start.7
  20.6 0.0 copy-done.1
  20.6 0.0 copy-done.2
  20.6 0.6 copy-done.7
  21.2 0.0 copy-start.3
  21.2 0.9 %copy-done.3 = bf16[128,512]{1,0:T(8,128)(2,1)S(1)} copy-done((bf16[128,512]{1,0:T(8,128)(2,1)S(1)}, bf16[128,512]{1,0:T(8,128)(2,1)}, u32[]{:S(2)}) %copy-start.3) | copy-done | bytes 131096
  22.1 0.0 copy-start.4
  22.1 0.8 copy-done.4
  22.9 7.8 %attend.1 = (bf16[8,128,128]{2,1,0:T(8,128)(2,1)}, f32[8,128,128]{2,1,0:T(8,128)S(1)}, bf16[16,80,128]{2,1,0:T(8,128)(2,1)S(1)}, f32[2,128]{1,0:T(2,128)S(1)}) custom-call(s32[2]{0:T(128)S(1)} %pad_add_fusion.place_ref, bf16[8,128,128]{2,1,0:T(8,128)(2,1)S(1)} %bitcast.12, bf16[8,128,128]{2,1,0:T(8,128)(2,1)S(1)} %bitcast.14, ...), custom_call_target="tpu_custom_call" | custom-call | tf_op jit(solution)/shard_map/attend/pallas_call | solution.py:313
  30.8 13.3 %all_to_all.20.parts_ref = bf16[16,80,128]{2,1,0:T(8,128)(2,1)S(1)} all-to-all(bf16[16,80,128]{2,1,0:T(8,128)(2,1)S(1)} %get-tuple-element.24), channel_id=1, replica_groups=mesh['dp'=32,'dap'=16] {'dap'}, dimensions={0} | all-to-all | bytes 655360 | tf_op jit(solution)/shard_map/all_to_all | solution.py:297
  44.1 2.0 %finish.1 = (bf16[8,128,128]{2,1,0:T(8,128)(2,1)}, bf16[32,48,128]{2,1,0:T(8,128)(2,1)S(1)}) custom-call(bf16[8,128,128]{2,1,0:T(8,128)(2,1)S(1)} %bitcast.13, bf16[8,128,128]{2,1,0:T(8,128)(2,1)S(1)} %bitcast.15, bf16[8,128,128]{2,1,0:T(8,128)(2,1)S(1)} %get-tuple-element.20.normed_ref, f32[8,128,128]{2,1,0:T(8,128)S(1)} %get-tuple-element.23.normed_proj_ref, ...), custom_call_target="tpu_custom_call" | custom-call | tf_op jit(solution)/shard_map/finish/pallas_call | solution.py:335
  46.1 28.1 %all_to_all.21.sums_ref = bf16[32,48,128]{2,1,0:T(8,128)(2,1)S(1)} all-to-all(bf16[32,48,128]{2,1,0:T(8,128)(2,1)S(1)} %get-tuple-element.27), channel_id=1, replica_groups=mesh['dp'=32,'dap'=16] {'dp'}, dimensions={0} | all-to-all | bytes 786432 | tf_op jit(solution)/shard_map/all_to_all | solution.py:297
  74.2 0.1 sum.1
  74.3 12.8 %all_to_all.22.blocks_ref = bf16[16,48,128]{2,1,0:T(8,128)(2,1)S(1)} all-to-all(bf16[16,48,128]{2,1,0:T(8,128)(2,1)S(1)} %sum.1), channel_id=1, replica_groups=mesh['dp'=32,'dap'=16] {'dap'}, dimensions={0} | all-to-all | bytes 393216 | tf_op jit(solution)/shard_map/all_to_all | solution.py:297
  87.1 0.7 assemble.1
Async XLA Ops:
  0.6 0.7 copy-start.5
  0.6 0.7 copy-start.6
  1.3 1.0 %copy-start = (bf16[1,8,128,128]{3,2,1,0:T(8,128)(2,1)S(1)}, bf16[1,8,128,128]{3,2,1,0:T(8,128)(2,1)}, u32[]{:S(2)}) copy-start(bf16[1,8,128,128]{3,2,1,0:T(8,128)(2,1)} %param.8) | copy-start | bytes 786436
  2.3 18.3 %copy-start.1 = (bf16[1,8,128,128]{3,2,1,0:T(8,128)(2,1)S(1)}, bf16[1,8,128,128]{3,2,1,0:T(8,128)(2,1)}, u32[]{:S(2)}) copy-start(bf16[1,8,128,128]{3,2,1,0:T(8,128)(2,1)} %param.8) | copy-start | bytes 786436
  2.3 18.3 %copy-start.2 = (bf16[1,8,128,128]{3,2,1,0:T(8,128)(2,1)S(1)}, bf16[1,8,128,128]{3,2,1,0:T(8,128)(2,1)}, u32[]{:S(2)}) copy-start(bf16[1,8,128,128]{3,2,1,0:T(8,128)(2,1)} %param.10) | copy-start | bytes 786436
  3.5 17.1 %all-to-all-start = ((bf16[16,32,128]{2,1,0:T(8,128)(2,1)}), bf16[16,32,128]{2,1,0:T(8,128)(2,1)S(1)}, u32[]{:S(2)}, u32[]{:S(2)}) async-start(bf16[16,32,128]{2,1,0:T(8,128)(2,1)} %get-tuple-element.21), calls=%async_computation | async-start | bytes 262144 | tf_op jit(solution)/shard_map/all_to_all | solution.py:297
  20.6 0.7 copy-start.7
  21.2 0.9 %copy-start.3 = (bf16[128,512]{1,0:T(8,128)(2,1)S(1)}, bf16[128,512]{1,0:T(8,128)(2,1)}, u32[]{:S(2)}) copy-start(bf16[128,512]{1,0:T(8,128)(2,1)} %proj_weight_ref.1) | copy-start | bytes 393220
  22.1 0.8 copy-start.4

commit v3 on v2

v3 whole, which is shorter than its diff:
```python
import functools

import jax
import jax.numpy as jnp
from jax import lax
from jax.experimental import pallas as pl
from jax.experimental.pallas import tpu as pltpu
from jax.sharding import PartitionSpec as P

EPS = 1e-05
DEAD = -1e30
F32 = jnp.float32
BF16 = jnp.bfloat16
VMEM_LIMIT = 40 * 1024 * 1024
UNROLL_PROJECT = 4
UNROLL_ATTEND = 4


def contract(a, b, a_axis, b_axis):
    return lax.dot_general(
        a, b, (((a_axis,), (b_axis,)), ((), ())), preferred_element_type=F32
    )


def standardize(rows):
    rows = rows.astype(F32)
    centered = rows - jnp.mean(rows, -1, keepdims=True)
    inv_std = lax.rsqrt(jnp.mean(centered * centered, -1, keepdims=True) + EPS)
    return centered * inv_std, inv_std


def head_masks(shape, axis, heads):
    size = shape[axis] // heads
    position = lax.broadcasted_iota(jnp.int32, shape, axis)
    return [(position >= h * size) & (position < (h + 1) * size) for h in range(heads)]


def stack_heads(block, masks):
    return jnp.concatenate([jnp.where(m, block, jnp.zeros_like(block)) for m in masks], 0)


def pick_heads(stacked, masks):
    size = stacked.shape[0] // len(masks)
    picked = stacked[:size]
    for h in range(1, len(masks)):
        picked = jnp.where(masks[h], stacked[h * size : (h + 1) * size], picked)
    return picked


def norm_kernel(pair_ref, gain_ref, bias_weight_ref, normed_ref, bias_ref, held):
    row_count = pair_ref.shape[0]
    heads = bias_weight_ref.shape[0]
    for row in range(row_count):
        x_hat, _ = standardize(pair_ref[row])
        normed = (x_hat * gain_ref[...]).astype(BF16)
        normed_ref[row] = normed
        held[pl.ds(row, heads, stride=row_count), :] = contract(
            bias_weight_ref[...], normed, 1, 1
        )
    block = held[...].astype(BF16)
    for peer in range(bias_ref.shape[0]):
        bias_ref[peer] = block


def dot(a, b):
    return jnp.dot(a, b, preferred_element_type=F32)


def project_kernel(
    place_ref,
    cot_ref,
    normed_ref,
    proj_weight_ref,
    gate_shift_ref,
    out_weight_ref,
    queries_ref,
    turned_ref,
    gating_ref,
    d_output_ref,
    d_mixed_ref,
    d_attend_ref,
    scores_ref,
    grads_ref,
):
    row_count, width, channels = cot_ref.shape
    heads = scores_ref.shape[1] // width
    scaling = (channels // heads) ** (-0.5)
    length, first_row = place_ref[0], place_ref[1]
    lane_masks = head_masks((width, channels), 1, heads)
    weight_t = proj_weight_ref[:, channels : 3 * channels].T
    token = lax.broadcasted_iota(jnp.int32, (width, channels), 0)

    def one_row(row, carry):
        normed = normed_ref[row]
        projected = dot(normed, proj_weight_ref[...])
        queries = (projected[:, :channels] * scaling).astype(BF16)
        keys = projected[:, channels : 2 * channels].astype(BF16)
        values = projected[:, 2 * channels : 3 * channels].astype(BF16)
        gating = jax.nn.sigmoid(projected[:, 3 * channels :] + gate_shift_ref[...])
        live = token < jnp.where(first_row + row < length, length, 0)
        d_output = jnp.where(live, cot_ref[row].astype(F32), 0.0).astype(BF16)
        d_mixed = contract(d_output, out_weight_ref[...], 1, 1)
        d_attend = (d_mixed * gating).astype(BF16)
        queries_ref[row] = queries
        turned_ref[row] = contract(weight_t, normed, 1, 1).astype(BF16)
        gating_ref[row] = gating
        d_output_ref[row] = d_output
        d_mixed_ref[row] = d_mixed
        d_attend_ref[row] = d_attend
        scores_ref[row] = contract(stack_heads(keys, lane_masks), queries, 1, 1)
        grads_ref[row] = contract(stack_heads(values, lane_masks), d_attend, 1, 1)
        return carry

    lax.fori_loop(0, row_count, one_row, 0, unroll=UNROLL_PROJECT)


def attend_kernel(
    place_ref,
    bias_ref,
    normed_ref,
    queries_ref,
    turned_ref,
    gating_ref,
    d_output_ref,
    d_mixed_ref,
    d_attend_ref,
    scores_ref,
    grads_ref,
    parts_ref,
    mixed_ref,
    d_proj_ref,
    shift_ref,
    bias_t,
    bias_sum,
    parts,
):
    row_count, width, channels = normed_ref.shape
    heads = bias_t.shape[0] // width
    head_size = channels // heads
    scaling = head_size ** (-0.5)
    length = place_ref[0]
    devices = bias_ref.shape[0]
    key_live = lax.broadcasted_iota(jnp.int32, (width, width), 0) < length
    for h in range(heads):
        rows = [
            bias_ref[d].astype(F32)[h * row_count : (h + 1) * row_count]
            for d in range(devices)
        ]
        turned = jnp.concatenate(rows, 0).T
        bias_t[h * width : (h + 1) * width] = jnp.where(key_live, turned, DEAD)
    bias_sum[...] = jnp.zeros_like(bias_sum)
    lane_masks = head_masks((width, channels), 1, heads)

    def one_row(row, shift_sum):
        weights, lows, attended_t, d_query_t = [], [], [], []
        for h in range(heads):
            part = slice(h * width, (h + 1) * width)
            own = slice(h * head_size, (h + 1) * head_size)
            expo = jnp.exp(scores_ref[row, part] + bias_t[part])
            probs = expo * (1.0 / jnp.sum(expo, 0, keepdims=True))
            weight = probs.astype(BF16)
            g = grads_ref[row, part]
            d_scores = probs * (g - jnp.sum(probs * g, 0, keepdims=True))
            bias_sum[part] += d_scores
            low = d_scores.astype(BF16)
            weights.append(weight)
            lows.append(low)
            attended_t.append(
                dot(turned_ref[row, channels + own.start : channels + own.stop], weight)
            )
            d_query_t.append(dot(turned_ref[row, own], low))
        attended = jnp.concatenate(attended_t, 0).T.astype(BF16).astype(F32)
        d_query = jnp.concatenate(d_query_t, 0).T
        d_value = pick_heads(dot(jnp.concatenate(weights, 0), d_attend_ref[row]), lane_masks)
        d_key = pick_heads(dot(jnp.concatenate(lows, 0), queries_ref[row]), lane_masks)
        gating = gating_ref[row]
        mixed = gating * attended
        mixed_ref[row] = mixed.astype(BF16)
        d_gating = (d_mixed_ref[row] * mixed * (1.0 - gating)).astype(BF16)
        d_proj_ref[row, :, :channels] = (d_query * scaling).astype(BF16)
        d_proj_ref[row, :, channels : 2 * channels] = d_key.astype(BF16)
        d_proj_ref[row, :, 2 * channels : 3 * channels] = d_value.astype(BF16)
        d_proj_ref[row, :, 3 * channels :] = d_gating
        return shift_sum + jnp.sum(d_gating.astype(F32), 0, keepdims=True)

    zero = jnp.zeros((1, channels), F32)
    shift_ref[...] = lax.fori_loop(0, row_count, one_row, zero, unroll=UNROLL_ATTEND)
    shared = heads * row_count
    for h in range(heads):
        turned = bias_sum[h * width : (h + 1) * width].T
        for d in range(devices):
            parts[d, h * row_count : (h + 1) * row_count] = turned[
                d * row_count : (d + 1) * row_count
            ]
    tokens = row_count * width
    normed = normed_ref[...].reshape(tokens, channels)
    grad_proj = contract(normed, d_proj_ref[...].reshape(tokens, 4 * channels), 0, 0)
    grad_out = contract(
        mixed_ref[...].reshape(tokens, channels),
        d_output_ref[...].reshape(tokens, channels),
        0,
        0,
    )
    pieces = [grad_proj[:, i * channels : (i + 1) * channels] for i in range(4)] + [grad_out]
    for d in range(devices):
        for i, piece in enumerate(pieces):
            start = shared + i * row_count
            parts[d, start : start + row_count] = piece[d * row_count : (d + 1) * row_count]
    unused = shared + len(pieces) * row_count
    parts[:, unused:] = jnp.zeros((devices, parts.shape[1] - unused, width), F32)
    parts_ref[...] = parts[...].astype(BF16)


def update_kernel(
    place_ref,
    pair_ref,
    mixed_ref,
    d_proj_ref,
    proj_weight_ref,
    out_weight_ref,
    updated_ref,
    normed_proj_ref,
    gain_ref,
):
    row_count, width, channels = pair_ref.shape
    length, first_row = place_ref[0], place_ref[1]
    token = lax.broadcasted_iota(jnp.int32, (width, channels), 0)
    gain_sum = jnp.zeros((1, channels), F32)
    for row in range(row_count):
        live = token < jnp.where(first_row + row < length, length, 0)
        output = dot(mixed_ref[row], out_weight_ref[...])
        updated_ref[row] = (
            pair_ref[row].astype(F32) + jnp.where(live, output, 0.0)
        ).astype(BF16)
        normed_proj = contract(d_proj_ref[row], proj_weight_ref[...], 1, 1)
        normed_proj_ref[row] = normed_proj
        x_hat, _ = standardize(pair_ref[row])
        gain_sum = gain_sum + jnp.sum(normed_proj * x_hat, 0, keepdims=True)
    gain_ref[...] = gain_sum


def bias_kernel(
    parts_ref,
    normed_ref,
    gain_sum_ref,
    shift_ref,
    gain_ref,
    bias_weight_ref,
    bias_grad_ref,
    sums_ref,
    held,
):
    row_count, width, channels = normed_ref.shape
    heads = bias_weight_ref.shape[0]
    shared = heads * row_count
    total = parts_ref[0].astype(F32)
    for d in range(1, parts_ref.shape[0]):
        total = total + parts_ref[d].astype(F32)
    bias_grad = total[:shared].astype(BF16)
    bias_grad_ref[...] = bias_grad
    bias_grad = bias_grad.astype(F32)
    of_row = lax.broadcasted_iota(jnp.int32, bias_grad.shape, 0) % row_count
    grad_bias = jnp.zeros((shared, channels), F32)
    for row in range(row_count):
        own = jnp.where(of_row == row, bias_grad, 0.0).astype(BF16)
        grad_bias = grad_bias + dot(own, normed_ref[row])
    grads = 5 * row_count
    held[:grads] = total[shared : shared + grads]
    held[grads:] = jnp.zeros((held.shape[0] - grads, channels), F32)
    weight = bias_weight_ref[...].astype(F32)
    added = jnp.zeros((1, channels), F32)
    for h in range(heads):
        summed = jnp.sum(grad_bias[h * row_count : (h + 1) * row_count], 0, keepdims=True)
        held[grads + h : grads + h + 1] = summed
        added = added + summed * weight[h : h + 1]
    held[grads + heads : grads + heads + 1] = gain_sum_ref[...] + added / gain_ref[...]
    held[grads + heads + 1 : grads + heads + 2] = shift_ref[...]
    block = held[...].astype(BF16)
    for peer in range(sums_ref.shape[0]):
        sums_ref[peer] = block


def finish_kernel(
    pair_ref,
    cot_ref,
    normed_proj_ref,
    bias_grad_ref,
    gain_ref,
    bias_weight_ref,
    pair_grad_ref,
):
    row_count, width, channels = pair_ref.shape
    heads = bias_weight_ref.shape[0]
    bias_grad = bias_grad_ref[...].astype(F32)
    of_row = lax.broadcasted_iota(jnp.int32, bias_grad.shape, 0) % row_count
    weight = bias_weight_ref[...].astype(F32)
    spread = jnp.concatenate(
        [jnp.broadcast_to(weight[h : h + 1], (row_count, channels)) for h in range(heads)], 0
    ).astype(BF16)
    for row in range(row_count):
        own = jnp.where(of_row == row, bias_grad, 0.0)
        added = dot(own.T.astype(BF16), spread)
        x_hat, inv_std = standardize(pair_ref[row])
        d_x_hat = (normed_proj_ref[row] + added) * gain_ref[...]
        d_pair = inv_std * (
            d_x_hat
            - jnp.mean(d_x_hat, -1, keepdims=True)
            - x_hat * jnp.mean(d_x_hat * x_hat, -1, keepdims=True)
        )
        pair_grad_ref[row] = (cot_ref[row].astype(F32) + d_pair).astype(BF16)


def sum_kernel(sums_ref, out_ref):
    total = sums_ref[0].astype(F32)
    for d in range(1, sums_ref.shape[0]):
        total = total + sums_ref[d].astype(F32)
    block = total.astype(BF16)
    for peer in range(out_ref.shape[0]):
        out_ref[peer] = block


def assemble_kernel(
    heads, scale, blocks_ref, grad_proj_ref, grad_shift_ref, grad_out_ref, grad_bias_ref, grad_gain_ref
):
    devices = blocks_ref.shape[0]
    channels = grad_out_ref.shape[0]
    row_count = channels // devices
    grads = 5 * row_count
    small = None
    for d in range(devices):
        block = blocks_ref[d].astype(F32) * scale
        own = slice(d * row_count, (d + 1) * row_count)
        for i in range(4):
            grad_proj_ref[own, i * channels : (i + 1) * channels] = block[
                i * row_count : (i + 1) * row_count
            ]
        grad_out_ref[own] = block[4 * row_count : grads]
        small = block[grads:] if small is None else small + block[grads:]
    grad_bias_ref[...] = small[:heads]
    grad_gain_ref[...] = small[heads : heads + 1]
    grad_shift_ref[...] = small[heads + 1 : heads + 2]


def per_device(
    pair_act, lengths, cotangent, proj_weight, gate_shift, out_weight, bias_weight, norm_gain
):
    pair, cot = pair_act[0], cotangent[0]
    row_count, width, channels = pair.shape
    heads = bias_weight.shape[1]
    gain, bias_weight_t = norm_gain[None], bias_weight.T
    devices, samples = lax.axis_size("dap"), lax.axis_size("dp")
    shared = heads * row_count
    chunk = -(-(5 * row_count + heads + 2) // 16) * 16
    vmem = pl.BlockSpec(memory_space=pltpu.VMEM)
    smem = pl.BlockSpec(memory_space=pltpu.SMEM)
    rows_shape = (row_count, width, channels)
    heads_shape = (row_count, heads * width, width)
    line = ((1, channels), F32)

    def call(kernel, name, args, outs, scratch=(), placed=False, flops=0, moved=0):
        return pl.pallas_call(
            kernel,
            out_shape=tuple(jax.ShapeDtypeStruct(shape, dtype) for shape, dtype in outs),
            in_specs=[smem] * placed + [vmem] * (len(args) - placed),
            out_specs=(vmem,) * len(outs),
            scratch_shapes=[pltpu.VMEM(shape, dtype) for shape, dtype in scratch],
            compiler_params=pltpu.CompilerParams(vmem_limit_bytes=VMEM_LIMIT),
            cost_estimate=pl.CostEstimate(flops=flops, bytes_accessed=moved, transcendentals=0),
            name=name,
        )(*args)

    def exchange(blocks, axis):
        return lax.all_to_all(blocks, axis, 0, 0, tiled=True)

    normed, bias_copies = call(
        norm_kernel,
        "norm",
        (pair, gain, bias_weight_t),
        [(rows_shape, BF16), ((devices, shared, width), BF16)],
        [((shared, width), F32)],
    )
    bias_all = exchange(bias_copies, "dap")
    place = jnp.stack([lengths[0], lax.axis_index("dap") * row_count]).astype(jnp.int32)
    projected = call(
        project_kernel,
        "project",
        (place, cot, normed, proj_weight, gate_shift[None], out_weight),
        [
            (rows_shape, BF16),
            ((row_count, 2 * channels, width), BF16),
            (rows_shape, F32),
            (rows_shape, BF16),
            (rows_shape, F32),
            (rows_shape, BF16),
            (heads_shape, F32),
            (heads_shape, F32),
        ],
        placed=True,
        flops=3 * 10**9,
        moved=10**7,
    )
    parts, mixed, d_proj, shift = call(
        attend_kernel,
        "attend",
        (place, bias_all, normed, *projected),
        [
            ((devices, shared + chunk, width), BF16),
            (rows_shape, BF16),
            ((row_count, width, 4 * channels), BF16),
            line,
        ],
        [
            ((heads * width, width), F32),
            ((heads * width, width), F32),
            ((devices, shared + chunk, width), F32),
        ],
        placed=True,
    )
    parts = exchange(parts, "dap")
    updated, normed_proj, gain_sum = call(
        update_kernel,
        "update",
        (place, pair, mixed, d_proj, proj_weight, out_weight),
        [(rows_shape, BF16), (rows_shape, F32), line],
        placed=True,
        flops=2 * 10**9,
        moved=6 * 10**6,
    )
    bias_grad, sums = call(
        bias_kernel,
        "bias_grad",
        (parts, normed, gain_sum, shift, gain, bias_weight_t),
        [((shared, width), BF16), ((samples, chunk, channels), BF16)],
        [((chunk, channels), F32)],
    )
    sums = exchange(sums, "dp")
    (pair_grad,) = call(
        finish_kernel,
        "finish",
        (pair, cot, normed_proj, bias_grad, gain, bias_weight_t),
        [(rows_shape, BF16)],
        flops=2 * 10**9,
        moved=6 * 10**6,
    )
    (blocks,) = call(sum_kernel, "sum", (sums,), [((devices, chunk, channels), BF16)])
    blocks = exchange(blocks, "dap")
    grad_proj, grad_shift, grad_out, grad_bias, grad_gain = call(
        functools.partial(assemble_kernel, heads, 1.0 / width),
        "assemble",
        (blocks,),
        [
            ((channels, 4 * channels), F32),
            line,
            ((channels, channels), F32),
            ((heads, channels), F32),
            line,
        ],
    )
    return (
        updated[None],
        pair_grad[None],
        grad_proj,
        grad_shift[0],
        grad_out,
        grad_bias.T,
        grad_gain[0],
    )


def solution(mesh):
    rows = P("dp", "dap", None, None)
    return jax.shard_map(
        per_device,
        mesh=mesh,
        in_specs=(rows, P("dp"), rows, P(), P(), P(), P(), P()),
        out_specs=(rows, rows, P(), P(), P(), P(), P()),
        check_vma=False,
    )
```

time: 88.3 us -> 97 us (1.099)
  blocking collectives: 54.2 us -> 27.7 us
  local copies, waits for them, and re-layouts: 3.93 us -> 22.5 us
  starting transfers between devices: 9.12 us -> 22 us
  waiting for transfers between devices: 7.26 us -> 10.3 us
    all_to_all x3 -> x1, blocking collectives: 54.2 us -> 27.7 us  [exchange(): return lax.all_to_all(blocks, axis, 0, 0, tiled=True)]
    unnamed x16 -> x56, local copies, waits for them, and re-layouts: 3.93 us -> 22.5 us
    all_to_all x1 -> x3, starting transfers between devices: 9.12 us -> 22 us  [exchange(): return lax.all_to_all(blocks, axis, 0, 0, tiled=True)]
    all_to_all x1 -> x3, waiting for transfers between devices: 7.26 us -> 10.3 us  [exchange(): return lax.all_to_all(blocks, axis, 0, 0, tiled=True)]
    pallas_call x5 -> x8, Pallas kernels: 11.9 us -> 12.2 us  [call(): pl.pallas_call(kernel, out_shape=tuple((jax.ShapeDtypeStruct(shape, dtype...]
  transfers between devices with their start and end apart: 1 -> 3, of which waited for: 1 -> 2; matrix products, arithmetic and copies ran while one was open for 0% -> 0% of each run, Pallas kernels for 0% -> 7%
where the time goes in v3:
time: 97 us; the launch traced here: 96.1 us
  blocking collectives  27.7 us (29%)
  local copies, waits for them, and re-layouts  22.5 us (23%)
  starting transfers between devices  22 us (23%)
  Pallas kernels  12.2 us (13%)
  waiting for transfers between devices  10.3 us (11%)
  between operations  1.36 us (1%)
    all_to_all x1, blocking collectives, exchange(): return lax.all_to_all(blocks, axis, 0, 0, tiled=True)  27.7 us
    unnamed x56, local copies, waits for them, and re-layouts  22.5 us
    all_to_all x3, starting transfers between devices, exchange(): return lax.all_to_all(blocks, axis, 0, 0, tiled=True)  22 us
    pallas_call x8, Pallas kernels, call(): pl.pallas_call(kernel, out_shape=tuple((jax.ShapeDtypeStruct(shape, dtype...  12.2 us
    all_to_all x3, waiting for transfers between devices, exchange(): return lax.all_to_all(blocks, axis, 0, 0, tiled=True)  10.3 us
  transfers between devices with their start and end apart: 3, of which 2 were waited for; matrix products, arithmetic and copies ran while one was open for 0% of the time, Pallas kernels for 7%

profile of v3, /device:TPU:8, one launch (start us, length us, event | category | flops | bytes accessed | tf_op | source)
XLA Modules:
  0.0 96.1 jit_solution(12845812521033851831)
XLA Ops:
  0.6 0.9 copy-done.11
  2.9 1.2 %norm.1 = (bf16[8,128,128]{2,1,0:T(8,128)(2,1)S(1)}, bf16[16,32,128]{2,1,0:T(8,128)(2,1)}) custom-call(bf16[8,128,128]{2,1,0:T(8,128)(2,1)S(1)} %bitcast.11, f32[1,128]{1,0:T(1,128)S(1)} %bitcast.17, bf16[4,128]{1,0:T(4,128)(2,1)S(1)} %bitcast.14), custom_call_target="tpu_custom_call" | custom-call | tf_op jit(solution)/shard_map/norm/pallas_call | solution.py:361
  4.1 9.1 %all-to-all-start = ((bf16[16,32,128]{2,1,0:T(8,128)(2,1)}), bf16[16,32,128]{2,1,0:T(8,128)(2,1)S(1)}, u32[]{:S(2)}, u32[]{:S(2)}) async-start(bf16[16,32,128]{2,1,0:T(8,128)(2,1)} %get-tuple-element.31), calls=%async_computation | async-start | bytes 262144 | tf_op jit(solution)/shard_map/all_to_all | solution.py:373
  14.0 0.9 copy-done.19
  14.9 0.9 copy-done.23
  15.8 0.8 copy-done.25
  17.2 2.8 %project.1 = (bf16[8,128,128]{2,1,0:T(8,128)(2,1)S(1)}, bf16[8,256,128]{2,1,0:T(8,128)(2,1)S(1)}, f32[8,128,128]{2,1,0:T(8,128)S(1)}, bf16[8,128,128]{2,1,0:T(8,...) custom-call(s32[2]{0:T(128)S(1)} %pad_add_fusion.place_ref, ...), custom_call_target="tpu_custom_call" | custom-call | flops 3000000000 | bytes 10000000 | tf_op jit(solution)/shard_map/project/pallas_call | solution.py:361
  20.0 1.4 %copy-done = f32[8,512,128]{2,1,0:T(8,128)} copy-done((f32[8,512,128]{2,1,0:T(8,128)}, f32[8,512,128]{2,1,0:T(8,128)S(1)}, u32[]{:S(2)}) %copy-start) | copy-done | bytes 2097176
  21.4 0.8 copy-done.2
  22.2 0.7 copy-done.5
  24.3 1.6 %copy-done.1 = f32[8,512,128]{2,1,0:T(8,128)S(1)} copy-done((f32[8,512,128]{2,1,0:T(8,128)S(1)}, f32[8,512,128]{2,1,0:T(8,128)}, u32[]{:S(2)}) %copy-start.1) | copy-done | bytes 2097176
  25.9 1.0 %copy-done.3 = f32[8,128,128]{2,1,0:T(8,128)S(1)} copy-done((f32[8,128,128]{2,1,0:T(8,128)S(1)}, f32[8,128,128]{2,1,0:T(8,128)}, u32[]{:S(2)}) %copy-start.3) | copy-done | bytes 524312
  27.0 0.9 copy-done.6
  27.9 0.9 copy-done.8
  28.9 0.9 copy-done.10
  29.8 2.7 %attend.1 = (bf16[16,80,128]{2,1,0:T(8,128)(2,1)S(1)}, bf16[8,128,128]{2,1,0:T(8,128)(2,1)S(1)}, bf16[8,128,512]{2,1,0:T(8,128)(2,1)S(1)}, f32[1,128]{1,0:T(1,128)S(1)}) custom-call(s32[2]{0:T(128)S(1)} %pad_add_fusion.place_ref, bf16[16,32,128]{2,1,0:T(8,128)(2,1)S(1)} %all-to-all-done.bias_ref, bf16[8,128,128]{2,1,0:T(8,128)(2,1)S(1)} %get-tuple-element.32.normed_ref, ...), custom_call_target="tpu_custom_call" | custom-call | tf_op jit(solution)/shard_map/attend/pallas_call | solution.py:361
  32.5 0.7 copy-done.4
  33.2 1.0 %copy-done.17 = bf16[8,128,512]{2,1,0:T(8,128)(2,1)} copy-done((bf16[8,128,512]{2,1,0:T(8,128)(2,1)}, bf16[8,128,512]{2,1,0:T(8,128)(2,1)S(1)}, u32[]{:S(2)}) %copy-start.17) | copy-done | bytes 1048600
  34.9 8.2 %all-to-all-start.1 = ((bf16[16,80,128]{2,1,0:T(8,128)(2,1)}), bf16[16,80,128]{2,1,0:T(8,128)(2,1)S(1)}, u32[]{:S(2)}, u32[]{:S(2)}) async-start(bf16[16,80,128]{2,1,0:T(8,128)(2,1)} %copy-done.4), calls=%async_computation.1 | async-start | bytes 655360 | tf_op jit(solution)/shard_map/all_to_all | solution.py:373
  43.1 0.9 copy-done.12
  44.0 1.2 %copy-done.18 = bf16[8,128,512]{2,1,0:T(8,128)(2,1)S(1)} copy-done((bf16[8,128,512]{2,1,0:T(8,128)(2,1)S(1)}, bf16[8,128,512]{2,1,0:T(8,128)(2,1)}, u32[]{:S(2)}) %copy-start.18) | copy-done | bytes 1048600
  45.2 0.9 copy-done.22
  46.2 0.9 copy-done.24
  47.1 0.8 copy-done.26
  47.9 1.7 %update.1 = (bf16[8,128,128]{2,1,0:T(8,128)(2,1)}, f32[8,128,128]{2,1,0:T(8,128)S(1)}, f32[1,128]{1,0:T(1,128)S(1)}) custom-call(s32[2]{0:T(128)S(1)} %pad_add_fusion.place_ref, bf16[8,128,128]{2,1,0:T(8,128)(2,1)S(1)} %bitcast.12, bf16[8,128,128]{2,1,0:T(8,128)(2,1)S(1)} %copy-done.22, bf16[8,128,512]{2,1,0:T(8,128)(2,1)S(1)} %copy-done.18, ...), custom_call_target="tpu_custom_call" | custom-call | flops 2000000000 | bytes 6000000 | tf_op jit(solution)/shard_map/update/pallas_call | solution.py:361
  49.6 3.7 %all-to-all-done.1.parts_ref = bf16[16,80,128]{2,1,0:T(8,128)(2,1)S(1)} async-done(((bf16[16,80,128]{2,1,0:T(8,128)(2,1)}), bf16[16,80,128]{2,1,0:T(8,128)(2,1)S(1)}, u32[]{:S(2)}, u32[]{:S(2)}) %all-to-all-start.1) | async-done | bytes 327712 | tf_op jit(solution)/shard_map/all_to_all | solution.py:373
  53.5 27.7 %all_to_all.20.sums_ref = bf16[32,48,128]{2,1,0:T(8,128)(2,1)S(1)} all-to-all(bf16[32,48,128]{2,1,0:T(8,128)(2,1)S(1)} %get-tuple-element.49), channel_id=1, replica_groups=mesh['dp'=32,'dap'=16] {'dp'}, dimensions={0} | all-to-all | bytes 786432 | tf_op jit(solution)/shard_map/all_to_all | solution.py:373
  81.2 0.7 sum.1
  82.0 4.7 %all-to-all-start.3 = ((bf16[16,48,128]{2,1,0:T(8,128)(2,1)}), bf16[16,48,128]{2,1,0:T(8,128)(2,1)S(1)}, u32[]{:S(2)}, u32[]{:S(2)}) async-start(bf16[16,48,128]{2,1,0:T(8,128)(2,1)} %sum.1), calls=%async_computation.3 | async-start | bytes 393216 | tf_op jit(solution)/shard_map/all_to_all | solution.py:373
  86.6 2.0 %finish.1 = bf16[8,128,128]{2,1,0:T(8,128)(2,1)} custom-call(bf16[8,128,128]{2,1,0:T(8,128)(2,1)S(1)} %bitcast.13, bf16[8,128,128]{2,1,0:T(8,128)(2,1)S(1)} %bitcast.21, f32[8,128,128]{2,1,0:T(8,128)S(1)} %get-tuple-element.44.normed_proj_ref, bf16[32,128]{1,0:T(8,128)(2,1)S(1)} %get-tuple-element.48.bias_grad_ref, f32[1,128]{1,0:T(1,128)S(1)} %bitcast.19, ...), custom_call_target="tpu_custom_call" | custom-call | flops 2000000000 | bytes 6000000 | tf_op jit(solution)/shard_map/finish/pallas_call | solution.py:361
  88.7 6.6 %all-to-all-done.3.blocks_ref = bf16[16,48,128]{2,1,0:T(8,128)(2,1)S(1)} async-done(((bf16[16,48,128]{2,1,0:T(8,128)(2,1)}), bf16[16,48,128]{2,1,0:T(8,128)(2,1)S(1)}, u32[]{:S(2)}, u32[]{:S(2)}) %all-to-all-start.3) | async-done | bytes 196640 | tf_op jit(solution)/shard_map/all_to_all | solution.py:373
  95.3 0.7 assemble.1
  (40 shorter events, 4.5 us)
Async XLA Ops:
  0.6 1.0 copy-start.11
  1.6 0.7 copy-start.13
  2.3 0.7 copy-start.15
  4.1 20.2 %all-to-all-start = ((bf16[16,32,128]{2,1,0:T(8,128)(2,1)}), bf16[16,32,128]{2,1,0:T(8,128)(2,1)S(1)}, u32[]{:S(2)}, u32[]{:S(2)}) async-start(bf16[16,32,128]{2,1,0:T(8,128)(2,1)} %get-tuple-element.31), calls=%async_computation | async-start | bytes 262144 | tf_op jit(solution)/shard_map/all_to_all | solution.py:373
  14.0 1.0 copy-start.19
  14.9 0.9 copy-start.23
  15.8 0.8 copy-start.25
  16.6 0.7 copy-start.27
  20.0 1.4 %copy-start = (f32[8,512,128]{2,1,0:T(8,128)}, f32[8,512,128]{2,1,0:T(8,128)S(1)}, u32[]{:S(2)}) copy-start(f32[8,512,128]{2,1,0:T(8,128)S(1)} %get-tuple-element.40.grads_ref) | copy-start | bytes 6291460
  21.4 0.8 copy-start.2
  22.2 0.7 copy-start.5
  22.9 0.7 copy-start.7
  23.6 0.7 copy-start.9
  24.3 1.6 %copy-start.1 = (f32[8,512,128]{2,1,0:T(8,128)S(1)}, f32[8,512,128]{2,1,0:T(8,128)}, u32[]{:S(2)}) copy-start(f32[8,512,128]{2,1,0:T(8,128)} %copy-done) | copy-start | bytes 6291460
  25.9 1.0 %copy-start.3 = (f32[8,128,128]{2,1,0:T(8,128)S(1)}, f32[8,128,128]{2,1,0:T(8,128)}, u32[]{:S(2)}) copy-start(f32[8,128,128]{2,1,0:T(8,128)} %copy-done.2) | copy-start | bytes 1572868
  27.0 0.9 copy-start.6
  27.9 0.9 copy-start.8
  28.9 0.9 copy-start.10
  32.5 0.7 copy-start.4
  33.2 1.0 %copy-start.17 = (bf16[8,128,512]{2,1,0:T(8,128)(2,1)}, bf16[8,128,512]{2,1,0:T(8,128)(2,1)S(1)}, u32[]{:S(2)}) copy-start(bf16[8,128,512]{2,1,0:T(8,128)(2,1)S(1)} %get-tuple-element.42.d_proj_ref) | copy-start | bytes 3145732
  34.2 0.7 copy-start.21
  34.9 18.4 %all-to-all-start.1 = ((bf16[16,80,128]{2,1,0:T(8,128)(2,1)}), bf16[16,80,128]{2,1,0:T(8,128)(2,1)S(1)}, u32[]{:S(2)}, u32[]{:S(2)}) async-start(bf16[16,80,128]{2,1,0:T(8,128)(2,1)} %copy-done.4), calls=%async_computation.1 | async-start | bytes 655360 | tf_op jit(solution)/shard_map/all_to_all | solution.py:373
  43.1 0.9 copy-start.12
  44.0 1.2 %copy-start.18 = (bf16[8,128,512]{2,1,0:T(8,128)(2,1)S(1)}, bf16[8,128,512]{2,1,0:T(8,128)(2,1)}, u32[]{:S(2)}) copy-start(bf16[8,128,512]{2,1,0:T(8,128)(2,1)} %copy-done.17) | copy-start | bytes 3145732
  45.2 0.9 copy-start.22
  46.2 0.9 copy-start.24
  47.1 0.8 copy-start.26
  47.9 5.4 %copy-start.14 = (bf16[128,4]{0,1:T(4,128)(2,1)S(1)}, bf16[128,4]{0,1:T(4,128)(2,1)}, u32[]{:S(2)}) copy-start(bf16[128,4]{0,1:T(4,128)(2,1)} %param.14) | copy-start | bytes 3076
  47.9 5.4 %copy-start.16 = (f32[128]{0:T(128)S(1)}, f32[128]{0:T(128)}, u32[]{:S(2)}) copy-start(f32[128]{0:T(128)} %param.15) | copy-start | bytes 1540
  49.6 37.0 %copy-start.20 = (bf16[1,8,128,128]{3,2,1,0:T(8,128)(2,1)S(1)}, bf16[1,8,128,128]{3,2,1,0:T(8,128)(2,1)}, u32[]{:S(2)}) copy-start(bf16[1,8,128,128]{3,2,1,0:T(8,128)(2,1)} %param.10) | copy-start | bytes 786436
  82.0 13.3 %all-to-all-start.3 = ((bf16[16,48,128]{2,1,0:T(8,128)(2,1)}), bf16[16,48,128]{2,1,0:T(8,128)(2,1)S(1)}, u32[]{:S(2)}, u32[]{:S(2)}) async-start(bf16[16,48,128]{2,1,0:T(8,128)(2,1)} %sum.1), calls=%async_computation.3 | async-start | bytes 393216 | tf_op jit(solution)/shard_map/all_to_all | solution.py:373

commit v4 on v3

--- a/solution.py
+++ b/solution.py
@@ -11,7 +11,7 @@
 DEAD = -1e30
 F32 = jnp.float32
 BF16 = jnp.bfloat16
-VMEM_LIMIT = 40 * 1024 * 1024
+VMEM_LIMIT = 16 * 1024 * 1024
 UNROLL_PROJECT = 4
 UNROLL_ATTEND = 4
 
@@ -73,20 +73,14 @@
     proj_weight_ref,
     gate_shift_ref,
     out_weight_ref,
-    queries_ref,
-    turned_ref,
-    gating_ref,
-    d_output_ref,
-    d_mixed_ref,
-    d_attend_ref,
-    scores_ref,
-    grads_ref,
+    bias_weight_ref,
+    narrow_ref,
+    wide_ref,
 ):
     row_count, width, channels = cot_ref.shape
-    heads = scores_ref.shape[1] // width
+    heads = bias_weight_ref.shape[0]
     scaling = (channels // heads) ** (-0.5)
     length, first_row = place_ref[0], place_ref[1]
-    lane_masks = head_masks((width, channels), 1, heads)
     weight_t = proj_weight_ref[:, channels : 3 * channels].T
     token = lax.broadcasted_iota(jnp.int32, (width, channels), 0)
 
@@ -101,14 +95,11 @@
         d_output = jnp.where(live, cot_ref[row].astype(F32), 0.0).astype(BF16)
         d_mixed = contract(d_output, out_weight_ref[...], 1, 1)
         d_attend = (d_mixed * gating).astype(BF16)
-        queries_ref[row] = queries
-        turned_ref[row] = contract(weight_t, normed, 1, 1).astype(BF16)
-        gating_ref[row] = gating
-        d_output_ref[row] = d_output
-        d_mixed_ref[row] = d_mixed
-        d_attend_ref[row] = d_attend
-        scores_ref[row] = contract(stack_heads(keys, lane_masks), queries, 1, 1)
-        grads_ref[row] = contract(stack_heads(values, lane_masks), d_attend, 1, 1)
+        for n, block in enumerate((queries, d_attend, d_output, keys, values)):
+            narrow_ref[row, n * width : (n + 1) * width] = block
+        narrow_ref[row, 5 * width :] = contract(weight_t, normed, 1, 1).astype(BF16)
+        wide_ref[row, :width] = gating
+        wide_ref[row, width:] = d_mixed
         return carry
 
     lax.fori_loop(0, row_count, one_row, 0, unroll=UNROLL_PROJECT)
@@ -118,21 +109,18 @@
     place_ref,
     bias_ref,
     normed_ref,
-    queries_ref,
-    turned_ref,
-    gating_ref,
-    d_output_ref,
-    d_mixed_ref,
-    d_attend_ref,
-    scores_ref,
-    grads_ref,
+    narrow_ref,
+    wide_ref,
+    proj_weight_ref,
     parts_ref,
     mixed_ref,
-    d_proj_ref,
+    normed_proj_ref,
     shift_ref,
     bias_t,
     bias_sum,
     parts,
+    d_proj,
+    weight_t,
 ):
     row_count, width, channels = normed_ref.shape
     heads = bias_t.shape[0] // width
@@ -150,37 +138,49 @@
         bias_t[h * width : (h + 1) * width] = jnp.where(key_live, turned, DEAD)
     bias_sum[...] = jnp.zeros_like(bias_sum)
     lane_masks = head_masks((width, channels), 1, heads)
+    weight_t[...] = proj_weight_ref[...].T
 
     def one_row(row, shift_sum):
         weights, lows, attended_t, d_query_t = [], [], [], []
+        queries, d_attend, _, keys, values = (
+            narrow_ref[row, n * width : (n + 1) * width] for n in range(5)
+        )
+        turned = narrow_ref.at[row, 5 * width :]
+        scores = contract(stack_heads(keys, lane_masks), queries, 1, 1)
+        grads = contract(stack_heads(values, lane_masks), d_attend, 1, 1)
         for h in range(heads):
             part = slice(h * width, (h + 1) * width)
             own = slice(h * head_size, (h + 1) * head_size)
-            expo = jnp.exp(scores_ref[row, part] + bias_t[part])
+            expo = jnp.exp(scores[part] + bias_t[part])
             probs = expo * (1.0 / jnp.sum(expo, 0, keepdims=True))
             weight = probs.astype(BF16)
-            g = grads_ref[row, part]
+            g = grads[part]
             d_scores = probs * (g - jnp.sum(probs * g, 0, keepdims=True))
             bias_sum[part] += d_scores
             low = d_scores.astype(BF16)
             weights.append(weight)
             lows.append(low)
-            attended_t.append(
-                dot(turned_ref[row, channels + own.start : channels + own.stop], weight)
-            )
-            d_query_t.append(dot(turned_ref[row, own], low))
+            attended_t.append(dot(turned[channels + own.start : channels + own.stop], weight))
+            d_query_t.append(dot(turned[own], low))
         attended = jnp.concatenate(attended_t, 0).T.astype(BF16).astype(F32)
         d_query = jnp.concatenate(d_query_t, 0).T
-        d_value = pick_heads(dot(jnp.concatenate(weights, 0), d_attend_ref[row]), lane_masks)
-        d_key = pick_heads(dot(jnp.concatenate(lows, 0), queries_ref[row]), lane_masks)
-        gating = gating_ref[row]
+        d_value = pick_heads(dot(jnp.concatenate(weights, 0), d_attend), lane_masks)
+        d_key = pick_heads(dot(jnp.concatenate(lows, 0), queries), lane_masks)
+        gating = wide_ref[row, :width]
         mixed = gating * attended
         mixed_ref[row] = mixed.astype(BF16)
-        d_gating = (d_mixed_ref[row] * mixed * (1.0 - gating)).astype(BF16)
-        d_proj_ref[row, :, :channels] = (d_query * scaling).astype(BF16)
-        d_proj_ref[row, :, channels : 2 * channels] = d_key.astype(BF16)
-        d_proj_ref[row, :, 2 * channels : 3 * channels] = d_value.astype(BF16)
-        d_proj_ref[row, :, 3 * channels :] = d_gating
+        d_gating = (wide_ref[row, width:] * mixed * (1.0 - gating)).astype(BF16)
+        d_row = jnp.concatenate(
+            [
+                (d_query * scaling).astype(BF16),
+                d_key.astype(BF16),
+                d_value.astype(BF16),
+                d_gating,
+            ],
+            1,
+        )
+        d_proj[row] = d_row
+        normed_proj_ref[row] = dot(d_row, weight_t[...])
         return shift_sum + jnp.sum(d_gating.astype(F32), 0, keepdims=True)
 
     zero = jnp.zeros((1, channels), F32)
@@ -194,10 +194,10 @@
             ]
     tokens = row_count * width
     normed = normed_ref[...].reshape(tokens, channels)
-    grad_proj = contract(normed, d_proj_ref[...].reshape(tokens, 4 * channels), 0, 0)
+    grad_proj = contract(normed, d_proj[...].reshape(tokens, 4 * channels), 0, 0)
     grad_out = contract(
         mixed_ref[...].reshape(tokens, channels),
-        d_output_ref[...].reshape(tokens, channels),
+        narrow_ref[:, 2 * width : 3 * width].reshape(tokens, channels),
         0,
         0,
     )
@@ -211,48 +211,13 @@
     parts_ref[...] = parts[...].astype(BF16)
 
 
-def update_kernel(
-    place_ref,
-    pair_ref,
-    mixed_ref,
-    d_proj_ref,
-    proj_weight_ref,
-    out_weight_ref,
-    updated_ref,
-    normed_proj_ref,
-    gain_ref,
-):
-    row_count, width, channels = pair_ref.shape
-    length, first_row = place_ref[0], place_ref[1]
-    token = lax.broadcasted_iota(jnp.int32, (width, channels), 0)
-    gain_sum = jnp.zeros((1, channels), F32)
-    for row in range(row_count):
-        live = token < jnp.where(first_row + row < length, length, 0)
-        output = dot(mixed_ref[row], out_weight_ref[...])
-        updated_ref[row] = (
-            pair_ref[row].astype(F32) + jnp.where(live, output, 0.0)
-        ).astype(BF16)
-        normed_proj = contract(d_proj_ref[row], proj_weight_ref[...], 1, 1)
-        normed_proj_ref[row] = normed_proj
-        x_hat, _ = standardize(pair_ref[row])
-        gain_sum = gain_sum + jnp.sum(normed_proj * x_hat, 0, keepdims=True)
-    gain_ref[...] = gain_sum
-
-
 def bias_kernel(
-    parts_ref,
-    normed_ref,
-    gain_sum_ref,
-    shift_ref,
-    gain_ref,
-    bias_weight_ref,
-    bias_grad_ref,
-    sums_ref,
-    held,
-):
+    parts_ref, normed_ref, shift_ref, mixed_ref, normed_proj_ref, bias_grad_ref, sums_ref, held
+):
+    del mixed_ref, normed_proj_ref
     row_count, width, channels = normed_ref.shape
-    heads = bias_weight_ref.shape[0]
-    shared = heads * row_count
+    shared = bias_grad_ref.shape[0]
+    heads = shared // row_count
     total = parts_ref[0].astype(F32)
     for d in range(1, parts_ref.shape[0]):
         total = total + parts_ref[d].astype(F32)
@@ -267,30 +232,33 @@
     grads = 5 * row_count
     held[:grads] = total[shared : shared + grads]
     held[grads:] = jnp.zeros((held.shape[0] - grads, channels), F32)
-    weight = bias_weight_ref[...].astype(F32)
-    added = jnp.zeros((1, channels), F32)
     for h in range(heads):
-        summed = jnp.sum(grad_bias[h * row_count : (h + 1) * row_count], 0, keepdims=True)
-        held[grads + h : grads + h + 1] = summed
-        added = added + summed * weight[h : h + 1]
-    held[grads + heads : grads + heads + 1] = gain_sum_ref[...] + added / gain_ref[...]
-    held[grads + heads + 1 : grads + heads + 2] = shift_ref[...]
+        held[grads + h : grads + h + 1] = jnp.sum(
+            grad_bias[h * row_count : (h + 1) * row_count], 0, keepdims=True
+        )
+    held[grads + heads : grads + heads + 1] = shift_ref[...]
     block = held[...].astype(BF16)
     for peer in range(sums_ref.shape[0]):
         sums_ref[peer] = block
 
 
 def finish_kernel(
+    place_ref,
     pair_ref,
     cot_ref,
+    mixed_ref,
     normed_proj_ref,
     bias_grad_ref,
     gain_ref,
     bias_weight_ref,
+    out_weight_ref,
+    updated_ref,
     pair_grad_ref,
 ):
     row_count, width, channels = pair_ref.shape
     heads = bias_weight_ref.shape[0]
+    length, first_row = place_ref[0], place_ref[1]
+    token = lax.broadcasted_iota(jnp.int32, (width, channels), 0)
     bias_grad = bias_grad_ref[...].astype(F32)
     of_row = lax.broadcasted_iota(jnp.int32, bias_grad.shape, 0) % row_count
     weight = bias_weight_ref[...].astype(F32)
@@ -298,6 +266,11 @@
         [jnp.broadcast_to(weight[h : h + 1], (row_count, channels)) for h in range(heads)], 0
     ).astype(BF16)
     for row in range(row_count):
+        live = token < jnp.where(first_row + row < length, length, 0)
+        output = dot(mixed_ref[row], out_weight_ref[...])
+        updated_ref[row] = (
+            pair_ref[row].astype(F32) + jnp.where(live, output, 0.0)
+        ).astype(BF16)
         own = jnp.where(of_row == row, bias_grad, 0.0)
         added = dot(own.T.astype(BF16), spread)
         x_hat, inv_std = standardize(pair_ref[row])
@@ -320,25 +293,44 @@
 
 
 def assemble_kernel(
-    heads, scale, blocks_ref, grad_proj_ref, grad_shift_ref, grad_out_ref, grad_bias_ref, grad_gain_ref
+    scale,
+    blocks_ref,
+    proj_weight_ref,
+    bias_weight_ref,
+    gain_ref,
+    grad_proj_ref,
+    grad_shift_ref,
+    grad_out_ref,
+    grad_bias_ref,
+    grad_gain_ref,
 ):
     devices = blocks_ref.shape[0]
     channels = grad_out_ref.shape[0]
+    heads = grad_bias_ref.shape[0]
     row_count = channels // devices
     grads = 5 * row_count
     small = None
+    by_channel = []
     for d in range(devices):
         block = blocks_ref[d].astype(F32) * scale
         own = slice(d * row_count, (d + 1) * row_count)
+        by_lane = None
         for i in range(4):
-            grad_proj_ref[own, i * channels : (i + 1) * channels] = block[
-                i * row_count : (i + 1) * row_count
-            ]
+            columns = slice(i * channels, (i + 1) * channels)
+            piece = block[i * row_count : (i + 1) * row_count]
+            grad_proj_ref[own, columns] = piece
+            term = piece * proj_weight_ref[own, columns].astype(F32)
+            by_lane = term if by_lane is None else by_lane + term
+        by_channel.append(by_lane)
         grad_out_ref[own] = block[4 * row_count : grads]
         small = block[grads:] if small is None else small + block[grads:]
     grad_bias_ref[...] = small[:heads]
-    grad_gain_ref[...] = small[heads : heads + 1]
-    grad_shift_ref[...] = small[heads + 1 : heads + 2]
+    grad_shift_ref[...] = small[heads : heads + 1]
+    gain_sum = jnp.sum(jnp.concatenate(by_channel, 0).T, 0, keepdims=True)
+    gain_sum = gain_sum + jnp.sum(
+        small[:heads] * bias_weight_ref[...].astype(F32), 0, keepdims=True
+    )
+    grad_gain_ref[...] = gain_sum / gain_ref[...]
 
 
 def per_device(
@@ -350,11 +342,10 @@
     gain, bias_weight_t = norm_gain[None], bias_weight.T
     devices, samples = lax.axis_size("dap"), lax.axis_size("dp")
     shared = heads * row_count
-    chunk = -(-(5 * row_count + heads + 2) // 16) * 16
+    chunk = -(-(5 * row_count + heads + 1) // 16) * 16
     vmem = pl.BlockSpec(memory_space=pltpu.VMEM)
     smem = pl.BlockSpec(memory_space=pltpu.SMEM)
     rows_shape = (row_count, width, channels)
-    heads_shape = (row_count, heads * width, width)
     line = ((1, channels), F32)
 
     def call(kernel, name, args, outs, scratch=(), placed=False, flops=0, moved=0):
@@ -381,73 +372,62 @@
     )
     bias_all = exchange(bias_copies, "dap")
     place = jnp.stack([lengths[0], lax.axis_index("dap") * row_count]).astype(jnp.int32)
-    projected = call(
+    narrow, wide = call(
         project_kernel,
         "project",
-        (place, cot, normed, proj_weight, gate_shift[None], out_weight),
+        (place, cot, normed, proj_weight, gate_shift[None], out_weight, bias_weight_t),
         [
-            (rows_shape, BF16),
-            ((row_count, 2 * channels, width), BF16),
-            (rows_shape, F32),
-            (rows_shape, BF16),
-            (rows_shape, F32),
-            (rows_shape, BF16),
-            (heads_shape, F32),
-            (heads_shape, F32),
+            ((row_count, 5 * width + 2 * channels, width), BF16),
+            ((row_count, 2 * width, channels), F32),
         ],
         placed=True,
         flops=3 * 10**9,
         moved=10**7,
     )
-    parts, mixed, d_proj, shift = call(
+    parts, mixed, normed_proj, shift = call(
         attend_kernel,
         "attend",
-        (place, bias_all, normed, *projected),
+        (place, bias_all, normed, narrow, wide, proj_weight),
         [
             ((devices, shared + chunk, width), BF16),
             (rows_shape, BF16),
-            ((row_count, width, 4 * channels), BF16),
+            (rows_shape, F32),
             line,
         ],
         [
             ((heads * width, width), F32),
             ((heads * width, width), F32),
             ((devices, shared + chunk, width), F32),
+            ((row_count, width, 4 * channels), BF16),
+            ((4 * channels, channels), BF16),
         ],
         placed=True,
     )
     parts = exchange(parts, "dap")
-    updated, normed_proj, gain_sum = call(
-        update_kernel,
-        "update",
-        (place, pair, mixed, d_proj, proj_weight, out_weight),
-        [(rows_shape, BF16), (rows_shape, F32), line],
+    bias_grad, sums = call(
+        bias_kernel,
+        "bias_grad",
+        (parts, normed, shift, mixed, normed_proj),
+        [((shared, width), BF16), ((samples, chunk, channels), BF16)],
+        [((chunk, channels), F32)],
+    )
+    sums = exchange(sums, "dp")
+    updated, pair_grad = call(
+        finish_kernel,
+        "finish",
+        (place, pair, cot, mixed, normed_proj, bias_grad, gain, bias_weight_t, out_weight),
+        [(rows_shape, BF16), (rows_shape, BF16)],
         placed=True,
         flops=2 * 10**9,
         moved=6 * 10**6,
     )
-    bias_grad, sums = call(
-        bias_kernel,
-        "bias_grad",
-        (parts, normed, gain_sum, shift, gain, bias_weight_t),
-        [((shared, width), BF16), ((samples, chunk, channels), BF16)],
-        [((chunk, channels), F32)],
-    )
-    sums = exchange(sums, "dp")
-    (pair_grad,) = call(
-        finish_kernel,
-        "finish",
-        (pair, cot, normed_proj, bias_grad, gain, bias_weight_t),
-        [(rows_shape, BF16)],
-        flops=2 * 10**9,
-        moved=6 * 10**6,
-    )
+    sums, pair_grad, updated = lax.optimization_barrier((sums, pair_grad, updated))
     (blocks,) = call(sum_kernel, "sum", (sums,), [((devices, chunk, channels), BF16)])
     blocks = exchange(blocks, "dap")
     grad_proj, grad_shift, grad_out, grad_bias, grad_gain = call(
-        functools.partial(assemble_kernel, heads, 1.0 / width),
+        functools.partial(assemble_kernel, 1.0 / width),
         "assemble",
-        (blocks,),
+        (blocks, proj_weight, bias_weight_t, gain),
         [
             ((channels, 4 * channels), F32),
             line,

time: 97 us -> 86.6 us (0.89)
  local copies, waits for them, and re-layouts: 22.5 us -> 8.25 us
  waiting for transfers between devices: 10.3 us -> 12.6 us
  blocking collectives: 27.7 us -> 29.6 us
    unnamed x56 -> x36, local copies, waits for them, and re-layouts: 22.5 us -> 8.25 us
    all_to_all x3 -> x2, waiting for transfers between devices: 10.3 us -> 12.6 us  [exchange(): return lax.all_to_all(blocks, axis, 0, 0, tiled=True)]
    all_to_all x1 -> x2, blocking collectives: 27.7 us -> 29.6 us  [exchange(): return lax.all_to_all(blocks, axis, 0, 0, tiled=True)]
    all_to_all x3 -> x2, starting transfers between devices: 22 us -> 21.7 us  [exchange(): return lax.all_to_all(blocks, axis, 0, 0, tiled=True)]
    pallas_call x8 -> x7, Pallas kernels: 12.2 us -> 12.4 us  [call(): pl.pallas_call(kernel, out_shape=tuple((jax.ShapeDtypeStruct(shape, dtype...]
  transfers between devices with their start and end apart: 3 -> 2, of which waited for: 2 -> 2; matrix products, arithmetic and copies ran while one was open for 0% -> 0% of each run, Pallas kernels for 7% -> 5%
where the time goes in v4:
time: 86.6 us; the launch traced here: 86 us
  blocking collectives  29.6 us (34%)
  starting transfers between devices  21.7 us (25%)
  waiting for transfers between devices  12.6 us (15%)
  Pallas kernels  12.4 us (14%)
  local copies, waits for them, and re-layouts  8.25 us (10%)
  between operations  1.43 us (2%)
    all_to_all x2, blocking collectives, exchange(): return lax.all_to_all(blocks, axis, 0, 0, tiled=True)  29.6 us
    all_to_all x2, starting transfers between devices, exchange(): return lax.all_to_all(blocks, axis, 0, 0, tiled=True)  21.7 us
    all_to_all x2, waiting for transfers between devices, exchange(): return lax.all_to_all(blocks, axis, 0, 0, tiled=True)  12.6 us
    pallas_call x7, Pallas kernels, call(): pl.pallas_call(kernel, out_shape=tuple((jax.ShapeDtypeStruct(shape, dtype...  12.4 us
    unnamed x36, local copies, waits for them, and re-layouts  8.25 us
  transfers between devices with their start and end apart: 2, of which 2 were waited for; matrix products, arithmetic and copies ran while one was open for 0% of the time, Pallas kernels for 5%

profile of v4, /device:TPU:8, one launch (start us, length us, event | category | flops | bytes accessed | tf_op | source)
XLA Modules:
  0.0 86.0 jit_solution(11128048354998114707)
XLA Ops:
  0.6 0.0 copy-start.6
  0.6 0.9 %copy-done.6 = bf16[1,8,128,128]{3,2,1,0:T(8,128)(2,1)S(1)} copy-done((bf16[1,8,128,128]{3,2,1,0:T(8,128)(2,1)S(1)}, bf16[1,8,128,128]{3,2,1,0:T(8,128)(2,1)}, u32[]{:S(2)}) %copy-start.6) | copy-done | bytes 262168
  1.6 0.7 copy-done.8
  2.3 0.7 copy-done.11
  2.9 1.2 %norm.1 = (bf16[8,128,128]{2,1,0:T(8,128)(2,1)S(1)}, bf16[16,32,128]{2,1,0:T(8,128)(2,1)}) custom-call(bf16[8,128,128]{2,1,0:T(8,128)(2,1)S(1)} %bitcast.11, f32[1,128]{1,0:T(1,128)S(1)} %bitcast.17, bf16[4,128]{1,0:T(4,128)(2,1)S(1)} %bitcast.13), custom_call_target="tpu_custom_call" | custom-call | tf_op jit(solution)/shard_map/norm/pallas_call | solution.py:352
  4.1 9.1 %all-to-all-start = ((bf16[16,32,128]{2,1,0:T(8,128)(2,1)}), bf16[16,32,128]{2,1,0:T(8,128)(2,1)S(1)}, u32[]{:S(2)}, u32[]{:S(2)}) async-start(bf16[16,32,128]{2,1,0:T(8,128)(2,1)} %get-tuple-element.27), calls=%async_computation | async-start | bytes 262144 | tf_op jit(solution)/shard_map/all_to_all | solution.py:364
  13.9 0.1 pad_add_fusion.place_ref
  14.0 0.9 %copy-done.2 = bf16[128,512]{1,0:T(8,128)(2,1)S(1)} copy-done((bf16[128,512]{1,0:T(8,128)(2,1)S(1)}, bf16[128,512]{1,0:T(8,128)(2,1)}, u32[]{:S(2)}) %copy-start.2) | copy-done | bytes 131096
  14.9 0.7 copy-done.9
  15.6 0.9 %copy-done.13 = bf16[1,8,128,128]{3,2,1,0:T(8,128)(2,1)S(1)} copy-done((bf16[1,8,128,128]{3,2,1,0:T(8,128)(2,1)S(1)}, bf16[1,8,128,128]{3,2,1,0:T(8,128)(2,1)}, u32[]{:S(2)}) %copy-start.13) | copy-done | bytes 262168
  16.5 0.8 copy-done.15
  17.3 0.7 copy-done.17
  17.9 1.4 %project.1 = (bf16[8,896,128]{2,1,0:T(8,128)(2,1)S(1)}, f32[8,256,128]{2,1,0:T(8,128)S(1)}) custom-call(s32[2]{0:T(128)S(1)} %pad_add_fusion.place_ref, bf16[8,128,128]{2,1,0:T(8,128)(2,1)S(1)} %bitcast.20, bf16[8,128,128]{2,1,0:T(8,128)(2,1)S(1)} %get-tuple-element.28.normed_ref, bf16[128,512]{1,0:T(8,128)(2,1)S(1)} %copy-done.2, f32[1,128]{1,0:T(1,128)S(1)} %bitcast.22, ...), custom_call_target="tpu_custom_call" | custom-call | flops 3000000000 | bytes 10000000 | tf_op jit(solution)/shard_map/project/pallas_call | solution.py:352
  19.4 1.9 %all-to-all-done.bias_ref = bf16[16,32,128]{2,1,0:T(8,128)(2,1)S(1)} async-done(((bf16[16,32,128]{2,1,0:T(8,128)(2,1)}), bf16[16,32,128]{2,1,0:T(8,128)(2,1)S(1)}, u32[]{:S(2)}, u32[]{:S(2)}) %all-to-all-start) | async-done | bytes 131104 | tf_op jit(solution)/shard_map/all_to_all | solution.py:364
  21.2 5.3 %attend.1 = (bf16[16,80,128]{2,1,0:T(8,128)(2,1)S(1)}, bf16[8,128,128]{2,1,0:T(8,128)(2,1)S(1)}, f32[8,128,128]{2,1,0:T(8,128)S(1)}, f32[1,128]{1,0:T(1,128)S(1)}) custom-call(s32[2]{0:T(128)S(1)} %pad_add_fusion.place_ref, bf16[16,32,128]{2,1,0:T(8,128)(2,1)S(1)} %all-to-all-done.bias_ref, bf16[8,128,128]{2,1,0:T(8,128)(2,1)S(1)} %get-tuple-element.28.normed_ref, ...), custom_call_target="tpu_custom_call" | custom-call | tf_op jit(solution)/shard_map/attend/pallas_call | solution.py:352
  26.6 0.0 copy-start
  26.6 0.0 copy-start.4
  26.6 0.0 copy-start.7
  26.6 0.0 copy-start.10
  26.6 0.0 copy-start.12
  26.6 0.0 copy-start.14
  26.6 0.0 copy-start.16
  26.6 16.5 %all_to_all.20.parts_ref = bf16[16,80,128]{2,1,0:T(8,128)(2,1)S(1)} all-to-all(bf16[16,80,128]{2,1,0:T(8,128)(2,1)S(1)} %get-tuple-element.31), channel_id=1, replica_groups=mesh['dp'=32,'dap'=16] {'dap'}, dimensions={0} | all-to-all | bytes 655360 | tf_op jit(solution)/shard_map/all_to_all | solution.py:364
  43.1 1.0 %bias_grad.1 = (bf16[32,128]{1,0:T(8,128)(2,1)S(1)}, bf16[32,48,128]{2,1,0:T(8,128)(2,1)}) custom-call(bf16[16,80,128]{2,1,0:T(8,128)(2,1)S(1)} %all_to_all.20.parts_ref, bf16[8,128,128]{2,1,0:T(8,128)(2,1)S(1)} %get-tuple-element.28.normed_ref, f32[1,128]{1,0:T(1,128)S(1)} %get-tuple-element.32.shift_ref, ...), custom_call_target="tpu_custom_call" | custom-call | tf_op jit(solution)/shard_map/bias_grad/pallas_call | solution.py:352
  44.1 12.6 %all-to-all-start.2 = ((bf16[32,48,128]{2,1,0:T(8,128)(2,1)}), bf16[32,48,128]{2,1,0:T(8,128)(2,1)S(1)}, u32[]{:S(2)}, u32[]{:S(2)}) async-start(bf16[32,48,128]{2,1,0:T(8,128)(2,1)} %get-tuple-element.35), calls=%async_computation.2 | async-start | bytes 786432 | tf_op jit(solution)/shard_map/all_to_all | solution.py:364
  56.7 1.0 %copy-done.1 = f32[8,128,128]{2,1,0:T(8,128)S(1)} copy-done((f32[8,128,128]{2,1,0:T(8,128)S(1)}, f32[8,128,128]{2,1,0:T(8,128)}, u32[]{:S(2)}) %copy-start.1) | copy-done | bytes 524312
  57.8 0.9 %copy-done.5 = bf16[8,128,128]{2,1,0:T(8,128)(2,1)S(1)} copy-done((bf16[8,128,128]{2,1,0:T(8,128)(2,1)S(1)}, bf16[8,128,128]{2,1,0:T(8,128)(2,1)}, u32[]{:S(2)}) %copy-start.5) | copy-done | bytes 262168
  58.7 2.6 %finish.1 = (bf16[8,128,128]{2,1,0:T(8,128)(2,1)}, bf16[8,128,128]{2,1,0:T(8,128)(2,1)}) custom-call(s32[2]{0:T(128)S(1)} %pad_add_fusion.place_ref, bf16[8,128,128]{2,1,0:T(8,128)(2,1)S(1)} %bitcast.12, bf16[8,128,128]{2,1,0:T(8,128)(2,1)S(1)} %bitcast.21, bf16[8,128,128]{2,1,0:T(8,128)(2,1)S(1)} %copy-done.5, f32[8,128,128]{2,1,0:T(8,128)S(1)} %copy-done.1, ...), custom_call_target="tpu_custom_call" | custom-call | flops 2000000000 | bytes 6000000 | tf_op jit(solution)/shard_map/finish/pallas_call | solution.py:352
  61.3 10.7 %all-to-all-done.2.sums_ref = bf16[32,48,128]{2,1,0:T(8,128)(2,1)S(1)} async-done(((bf16[32,48,128]{2,1,0:T(8,128)(2,1)}), bf16[32,48,128]{2,1,0:T(8,128)(2,1)S(1)}, u32[]{:S(2)}, u32[]{:S(2)}) %all-to-all-start.2) | async-done | bytes 393248 | tf_op jit(solution)/shard_map/all_to_all | solution.py:364
  72.0 0.1 sum.1
  72.1 13.1 %all_to_all.21.blocks_ref = bf16[16,48,128]{2,1,0:T(8,128)(2,1)S(1)} all-to-all(bf16[16,48,128]{2,1,0:T(8,128)(2,1)S(1)} %sum.1), channel_id=1, replica_groups=mesh['dp'=32,'dap'=16] {'dap'}, dimensions={0} | all-to-all | bytes 393216 | tf_op jit(solution)/shard_map/all_to_all | solution.py:364
  85.2 0.8 assemble.1
  (18 shorter events, 0.0 us)
Async XLA Ops:
  0.6 1.0 %copy-start.6 = (bf16[1,8,128,128]{3,2,1,0:T(8,128)(2,1)S(1)}, bf16[1,8,128,128]{3,2,1,0:T(8,128)(2,1)}, u32[]{:S(2)}) copy-start(bf16[1,8,128,128]{3,2,1,0:T(8,128)(2,1)} %param.8) | copy-start | bytes 786436
  1.6 0.7 copy-start.8
  2.3 0.7 copy-start.11
  4.1 17.1 %all-to-all-start = ((bf16[16,32,128]{2,1,0:T(8,128)(2,1)}), bf16[16,32,128]{2,1,0:T(8,128)(2,1)S(1)}, u32[]{:S(2)}, u32[]{:S(2)}) async-start(bf16[16,32,128]{2,1,0:T(8,128)(2,1)} %get-tuple-element.27), calls=%async_computation | async-start | bytes 262144 | tf_op jit(solution)/shard_map/all_to_all | solution.py:364
  14.0 0.9 %copy-start.2 = (bf16[128,512]{1,0:T(8,128)(2,1)S(1)}, bf16[128,512]{1,0:T(8,128)(2,1)}, u32[]{:S(2)}) copy-start(bf16[128,512]{1,0:T(8,128)(2,1)} %proj_weight_ref.5) | copy-start | bytes 393220
  14.9 0.7 copy-start.9
  15.6 0.9 %copy-start.13 = (bf16[1,8,128,128]{3,2,1,0:T(8,128)(2,1)S(1)}, bf16[1,8,128,128]{3,2,1,0:T(8,128)(2,1)}, u32[]{:S(2)}) copy-start(bf16[1,8,128,128]{3,2,1,0:T(8,128)(2,1)} %param.10) | copy-start | bytes 786436
  16.5 0.8 copy-start.15
  17.3 0.7 copy-start.17
  17.9 3.3 %copy-start.3 = (bf16[128,512]{1,0:T(8,128)(2,1)S(1)}, bf16[128,512]{1,0:T(8,128)(2,1)}, u32[]{:S(2)}) copy-start(bf16[128,512]{1,0:T(8,128)(2,1)} %proj_weight_ref.5) | copy-start | bytes 393220
  26.6 17.6 %copy-start = (f32[8,128,128]{2,1,0:T(8,128)}, f32[8,128,128]{2,1,0:T(8,128)S(1)}, u32[]{:S(2)}) copy-start(f32[8,128,128]{2,1,0:T(8,128)S(1)} %get-tuple-element.34.normed_proj_ref) | copy-start | bytes 1572868
  26.6 17.5 %copy-start.4 = (bf16[8,128,128]{2,1,0:T(8,128)(2,1)}, bf16[8,128,128]{2,1,0:T(8,128)(2,1)S(1)}, u32[]{:S(2)}) copy-start(bf16[8,128,128]{2,1,0:T(8,128)(2,1)S(1)} %get-tuple-element.33.mixed_ref) | copy-start | bytes 786436
  26.6 30.1 %copy-start.7 = (bf16[1,8,128,128]{3,2,1,0:T(8,128)(2,1)S(1)}, bf16[1,8,128,128]{3,2,1,0:T(8,128)(2,1)}, u32[]{:S(2)}) copy-start(bf16[1,8,128,128]{3,2,1,0:T(8,128)(2,1)} %param.8) | copy-start | bytes 786436
  26.6 30.1 %copy-start.10 = (bf16[128,4]{0,1:T(4,128)(2,1)S(1)}, bf16[128,4]{0,1:T(4,128)(2,1)}, u32[]{:S(2)}) copy-start(bf16[128,4]{0,1:T(4,128)(2,1)} %param.14) | copy-start | bytes 3076
  26.6 30.1 %copy-start.12 = (f32[128]{0:T(128)S(1)}, f32[128]{0:T(128)}, u32[]{:S(2)}) copy-start(f32[128]{0:T(128)} %param.15) | copy-start | bytes 1540
  26.6 30.1 %copy-start.14 = (bf16[1,8,128,128]{3,2,1,0:T(8,128)(2,1)S(1)}, bf16[1,8,128,128]{3,2,1,0:T(8,128)(2,1)}, u32[]{:S(2)}) copy-start(bf16[1,8,128,128]{3,2,1,0:T(8,128)(2,1)} %param.10) | copy-start | bytes 786436
  26.6 30.1 %copy-start.16 = (bf16[128,128]{1,0:T(8,128)(2,1)S(1)}, bf16[128,128]{1,0:T(8,128)(2,1)}, u32[]{:S(2)}) copy-start(bf16[128,128]{1,0:T(8,128)(2,1)} %out_weight_ref.3) | copy-start | bytes 98308
  44.1 27.9 %all-to-all-start.2 = ((bf16[32,48,128]{2,1,0:T(8,128)(2,1)}), bf16[32,48,128]{2,1,0:T(8,128)(2,1)S(1)}, u32[]{:S(2)}, u32[]{:S(2)}) async-start(bf16[32,48,128]{2,1,0:T(8,128)(2,1)} %get-tuple-element.35), calls=%async_computation.2 | async-start | bytes 786432 | tf_op jit(solution)/shard_map/all_to_all | solution.py:364
  56.7 1.0 %copy-start.1 = (f32[8,128,128]{2,1,0:T(8,128)S(1)}, f32[8,128,128]{2,1,0:T(8,128)}, u32[]{:S(2)}) copy-start(f32[8,128,128]{2,1,0:T(8,128)} %copy-done) | copy-start | bytes 1572868
  57.8 0.9 %copy-start.5 = (bf16[8,128,128]{2,1,0:T(8,128)(2,1)S(1)}, bf16[8,128,128]{2,1,0:T(8,128)(2,1)}, u32[]{:S(2)}) copy-start(bf16[8,128,128]{2,1,0:T(8,128)(2,1)} %copy-done.4) | copy-start | bytes 786436

commit v5 on v4

--- a/solution.py
+++ b/solution.py
@@ -16,6 +16,10 @@
 UNROLL_ATTEND = 4
 
 
+def dot(a, b):
+    return jnp.dot(a, b, preferred_element_type=F32)
+
+
 def contract(a, b, a_axis, b_axis):
     return lax.dot_general(
         a, b, (((a_axis,), (b_axis,)), ((), ())), preferred_element_type=F32
@@ -47,62 +51,106 @@
     return picked
 
 
-def norm_kernel(pair_ref, gain_ref, bias_weight_ref, normed_ref, bias_ref, held):
-    row_count = pair_ref.shape[0]
-    heads = bias_weight_ref.shape[0]
+def begin_all(sources, targets, sems):
+    copies = [
+        pltpu.make_async_copy(source, target, sems.at[n])
+        for n, (source, target) in enumerate(zip(sources, targets, strict=True))
+    ]
+    for copy in copies:
+        copy.start()
+    return copies
+
+
+def norm_kernel(
+    pair_hbm,
+    gain_hbm,
+    bias_weight_hbm,
+    proj_weight_hbm,
+    gate_shift_hbm,
+    normed_ref,
+    bias_ref,
+    proj_weight_ref,
+    gate_shift_ref,
+    pair,
+    gain,
+    bias_weight,
+    held,
+    sems,
+):
+    row_count = pair.shape[0]
+    heads = bias_weight.shape[0]
+    copies = begin_all(
+        (gain_hbm, bias_weight_hbm, pair_hbm, proj_weight_hbm, gate_shift_hbm),
+        (gain, bias_weight, pair, proj_weight_ref, gate_shift_ref),
+        sems,
+    )
+    for copy in copies[:3]:
+        copy.wait()
     for row in range(row_count):
-        x_hat, _ = standardize(pair_ref[row])
-        normed = (x_hat * gain_ref[...]).astype(BF16)
+        x_hat, _ = standardize(pair[row])
+        normed = (x_hat * gain[...]).astype(BF16)
         normed_ref[row] = normed
-        held[pl.ds(row, heads, stride=row_count), :] = contract(
-            bias_weight_ref[...], normed, 1, 1
-        )
+        held[pl.ds(row, heads, stride=row_count), :] = contract(bias_weight[...], normed, 1, 1)
     block = held[...].astype(BF16)
     for peer in range(bias_ref.shape[0]):
         bias_ref[peer] = block
-
-
-def dot(a, b):
-    return jnp.dot(a, b, preferred_element_type=F32)
+    for copy in copies[3:]:
+        copy.wait()
 
 
 def project_kernel(
+    heads,
     place_ref,
-    cot_ref,
     normed_ref,
     proj_weight_ref,
     gate_shift_ref,
-    out_weight_ref,
-    bias_weight_ref,
+    cot_hbm,
+    out_weight_hbm,
     narrow_ref,
     wide_ref,
-):
-    row_count, width, channels = cot_ref.shape
-    heads = bias_weight_ref.shape[0]
+    cot,
+    out_weight,
+    sems,
+):
+    row_count, width, channels = cot.shape
     scaling = (channels // heads) ** (-0.5)
+    copies = begin_all((cot_hbm, out_weight_hbm), (cot, out_weight), sems)
     length, first_row = place_ref[0], place_ref[1]
-    weight_t = proj_weight_ref[:, channels : 3 * channels].T
+    weight_t = proj_weight_ref[...].T
+    share = weight_t.shape[0] // row_count
+    for row in range(row_count):
+        narrow_ref[row, 5 * width + 2 * channels :] = weight_t[row * share : (row + 1) * share]
+    weight_t = weight_t[channels : 3 * channels]
     token = lax.broadcasted_iota(jnp.int32, (width, channels), 0)
 
-    def one_row(row, carry):
+    def place(row, n, block):
+        narrow_ref[row, n * width : (n + 1) * width] = block.astype(BF16)
+
+    def forward(row, carry):
         normed = normed_ref[row]
         projected = dot(normed, proj_weight_ref[...])
-        queries = (projected[:, :channels] * scaling).astype(BF16)
-        keys = projected[:, channels : 2 * channels].astype(BF16)
-        values = projected[:, 2 * channels : 3 * channels].astype(BF16)
-        gating = jax.nn.sigmoid(projected[:, 3 * channels :] + gate_shift_ref[...])
+        place(row, 0, projected[:, :channels] * scaling)
+        place(row, 3, projected[:, channels : 2 * channels])
+        place(row, 4, projected[:, 2 * channels : 3 * channels])
+        wide_ref[row, :width] = jax.nn.sigmoid(projected[:, 3 * channels :] + gate_shift_ref[...])
+        narrow_ref[row, 5 * width : 5 * width + 2 * channels] = contract(
+            weight_t, normed, 1, 1
+        ).astype(BF16)
+        return carry
+
+    def backward(row, carry):
         live = token < jnp.where(first_row + row < length, length, 0)
-        d_output = jnp.where(live, cot_ref[row].astype(F32), 0.0).astype(BF16)
-        d_mixed = contract(d_output, out_weight_ref[...], 1, 1)
-        d_attend = (d_mixed * gating).astype(BF16)
-        for n, block in enumerate((queries, d_attend, d_output, keys, values)):
-            narrow_ref[row, n * width : (n + 1) * width] = block
-        narrow_ref[row, 5 * width :] = contract(weight_t, normed, 1, 1).astype(BF16)
-        wide_ref[row, :width] = gating
+        d_output = jnp.where(live, cot[row].astype(F32), 0.0).astype(BF16)
+        d_mixed = contract(d_output, out_weight[...], 1, 1)
+        place(row, 1, d_mixed * wide_ref[row, :width])
+        place(row, 2, d_output)
         wide_ref[row, width:] = d_mixed
         return carry
 
-    lax.fori_loop(0, row_count, one_row, 0, unroll=UNROLL_PROJECT)
+    lax.fori_loop(0, row_count, forward, 0, unroll=UNROLL_PROJECT)
+    for copy in copies:
+        copy.wait()
+    lax.fori_loop(0, row_count, backward, 0, unroll=UNROLL_PROJECT)
 
 
 def attend_kernel(
@@ -111,7 +159,6 @@
     normed_ref,
     narrow_ref,
     wide_ref,
-    proj_weight_ref,
     parts_ref,
     mixed_ref,
     normed_proj_ref,
@@ -138,7 +185,9 @@
         bias_t[h * width : (h + 1) * width] = jnp.where(key_live, turned, DEAD)
     bias_sum[...] = jnp.zeros_like(bias_sum)
     lane_masks = head_masks((width, channels), 1, heads)
-    weight_t[...] = proj_weight_ref[...].T
+    share = weight_t.shape[0] // row_count
+    for row in range(row_count):
+        weight_t[row * share : (row + 1) * share] = narrow_ref[row, 5 * width + 2 * channels :]
 
     def one_row(row, shift_sum):
         weights, lows, attended_t, d_query_t = [], [], [], []
@@ -244,23 +293,36 @@
 
 def finish_kernel(
     place_ref,
-    pair_ref,
-    cot_ref,
     mixed_ref,
     normed_proj_ref,
     bias_grad_ref,
+    pair_hbm,
+    cot_hbm,
+    gain_hbm,
+    bias_weight_hbm,
+    out_weight_hbm,
+    updated_ref,
+    pair_grad_ref,
+    pair_ref,
+    cot_ref,
     gain_ref,
     bias_weight_ref,
     out_weight_ref,
-    updated_ref,
-    pair_grad_ref,
-):
+    sems,
+):
+    copies = begin_all(
+        (pair_hbm, cot_hbm, gain_hbm, bias_weight_hbm, out_weight_hbm),
+        (pair_ref, cot_ref, gain_ref, bias_weight_ref, out_weight_ref),
+        sems,
+    )
     row_count, width, channels = pair_ref.shape
     heads = bias_weight_ref.shape[0]
     length, first_row = place_ref[0], place_ref[1]
     token = lax.broadcasted_iota(jnp.int32, (width, channels), 0)
     bias_grad = bias_grad_ref[...].astype(F32)
     of_row = lax.broadcasted_iota(jnp.int32, bias_grad.shape, 0) % row_count
+    for copy in copies:
+        copy.wait()
     weight = bias_weight_ref[...].astype(F32)
     spread = jnp.concatenate(
         [jnp.broadcast_to(weight[h : h + 1], (row_count, channels)) for h in range(heads)], 0
@@ -345,49 +407,68 @@
     chunk = -(-(5 * row_count + heads + 1) // 16) * 16
     vmem = pl.BlockSpec(memory_space=pltpu.VMEM)
     smem = pl.BlockSpec(memory_space=pltpu.SMEM)
+    hbm = pl.BlockSpec(memory_space=pltpu.MemorySpace.HBM)
     rows_shape = (row_count, width, channels)
     line = ((1, channels), F32)
 
-    def call(kernel, name, args, outs, scratch=(), placed=False, flops=0, moved=0):
+    def away(array):
+        return pltpu.with_memory_space_constraint(array, pltpu.MemorySpace.HBM)
+
+    def call(kernel, name, args, outs, scratch=(), placed=False, near=0, sems=0, flops=0, moved=0):
         return pl.pallas_call(
             kernel,
             out_shape=tuple(jax.ShapeDtypeStruct(shape, dtype) for shape, dtype in outs),
-            in_specs=[smem] * placed + [vmem] * (len(args) - placed),
+            in_specs=[smem] * placed + [vmem] * near + [hbm] * (len(args) - placed - near),
             out_specs=(vmem,) * len(outs),
-            scratch_shapes=[pltpu.VMEM(shape, dtype) for shape, dtype in scratch],
+            scratch_shapes=[pltpu.VMEM(shape, dtype) for shape, dtype in scratch]
+            + [pltpu.SemaphoreType.DMA((sems,))] * bool(sems),
             compiler_params=pltpu.CompilerParams(vmem_limit_bytes=VMEM_LIMIT),
             cost_estimate=pl.CostEstimate(flops=flops, bytes_accessed=moved, transcendentals=0),
             name=name,
-        )(*args)
+        )(*args[: placed + near], *(away(a) for a in args[placed + near :]))
 
     def exchange(blocks, axis):
         return lax.all_to_all(blocks, axis, 0, 0, tiled=True)
 
-    normed, bias_copies = call(
+    inputs = (pair, gain, bias_weight_t, proj_weight, gate_shift[None])
+    normed, bias_copies, near_proj, near_shift = call(
         norm_kernel,
         "norm",
-        (pair, gain, bias_weight_t),
-        [(rows_shape, BF16), ((devices, shared, width), BF16)],
-        [((shared, width), F32)],
+        inputs,
+        [
+            (rows_shape, BF16),
+            ((devices, shared, width), BF16),
+            *((a.shape, a.dtype) for a in inputs[3:]),
+        ],
+        [
+            (rows_shape, BF16),
+            line,
+            (bias_weight_t.shape, BF16),
+            ((shared, width), F32),
+        ],
+        sems=len(inputs),
     )
     bias_all = exchange(bias_copies, "dap")
     place = jnp.stack([lengths[0], lax.axis_index("dap") * row_count]).astype(jnp.int32)
     narrow, wide = call(
-        project_kernel,
+        functools.partial(project_kernel, heads),
         "project",
-        (place, cot, normed, proj_weight, gate_shift[None], out_weight, bias_weight_t),
-        [
-            ((row_count, 5 * width + 2 * channels, width), BF16),
+        (place, normed, near_proj, near_shift, cot, out_weight),
+        [
+            ((row_count, 5 * width + 2 * channels + 4 * channels // row_count, width), BF16),
             ((row_count, 2 * width, channels), F32),
         ],
+        [(rows_shape, BF16), (out_weight.shape, BF16)],
         placed=True,
+        near=3,
+        sems=2,
         flops=3 * 10**9,
         moved=10**7,
     )
     parts, mixed, normed_proj, shift = call(
         attend_kernel,
         "attend",
-        (place, bias_all, normed, narrow, wide, proj_weight),
+        (place, bias_all, normed, narrow, wide),
         [
             ((devices, shared + chunk, width), BF16),
             (rows_shape, BF16),
@@ -402,6 +483,7 @@
             ((4 * channels, channels), BF16),
         ],
         placed=True,
+        near=4,
     )
     parts = exchange(parts, "dap")
     bias_grad, sums = call(
@@ -410,19 +492,31 @@
         (parts, normed, shift, mixed, normed_proj),
         [((shared, width), BF16), ((samples, chunk, channels), BF16)],
         [((chunk, channels), F32)],
+        near=5,
     )
     sums = exchange(sums, "dp")
     updated, pair_grad = call(
         finish_kernel,
         "finish",
-        (place, pair, cot, mixed, normed_proj, bias_grad, gain, bias_weight_t, out_weight),
+        (place, mixed, normed_proj, bias_grad, pair, cot, gain, bias_weight_t, out_weight),
         [(rows_shape, BF16), (rows_shape, BF16)],
+        [
+            (rows_shape, BF16),
+            (rows_shape, BF16),
+            line,
+            (bias_weight_t.shape, BF16),
+            (out_weight.shape, BF16),
+        ],
         placed=True,
+        near=3,
+        sems=5,
         flops=2 * 10**9,
         moved=6 * 10**6,
     )
     sums, pair_grad, updated = lax.optimization_barrier((sums, pair_grad, updated))
-    (blocks,) = call(sum_kernel, "sum", (sums,), [((devices, chunk, channels), BF16)])
+    (blocks,) = call(
+        sum_kernel, "sum", (sums,), [((devices, chunk, channels), BF16)], near=1
+    )
     blocks = exchange(blocks, "dap")
     grad_proj, grad_shift, grad_out, grad_bias, grad_gain = call(
         functools.partial(assemble_kernel, 1.0 / width),
@@ -435,6 +529,7 @@
             ((heads, channels), F32),
             line,
         ],
+        near=4,
     )
     return (
         updated[None],

time: 86.6 us -> 82.1 us (0.948)
  local copies, waits for them, and re-layouts: 8.25 us -> 2.01 us
  blocking collectives: 29.6 us -> 26.1 us
  Pallas kernels: 12.4 us -> 15 us
  waiting for transfers between devices: 12.6 us -> 14.9 us
    unnamed x36 -> x14, local copies, waits for them, and re-layouts: 8.25 us -> 2.01 us
    all_to_all x2, blocking collectives: 29.6 us -> 26.1 us  [exchange(): return lax.all_to_all(blocks, axis, 0, 0, tiled=True)]
    pallas_call x7, Pallas kernels: 12.4 us -> 15 us  [call(): pl.pallas_call(kernel, out_shape=tuple((jax.ShapeDtypeStruct(shape, dtype...]
    all_to_all x2, waiting for transfers between devices: 12.6 us -> 14.9 us  [exchange(): return lax.all_to_all(blocks, axis, 0, 0, tiled=True)]
  transfers between devices with their start and end apart: 2 -> 2, of which waited for: 2 -> 2; matrix products, arithmetic and copies ran while one was open for 0% -> 0% of each run, Pallas kernels for 5% -> 7%
where the time goes in v5:
time: 82.1 us; the launch traced here: 81.6 us
  blocking collectives  26.1 us (32%)
  starting transfers between devices  22.1 us (27%)
  Pallas kernels  15 us (18%)
  waiting for transfers between devices  14.9 us (18%)
  local copies, waits for them, and re-layouts  2.01 us (2%)
  between operations  1.36 us (2%)
    all_to_all x2, blocking collectives, exchange(): return lax.all_to_all(blocks, axis, 0, 0, tiled=True)  26.1 us
    all_to_all x2, starting transfers between devices, exchange(): return lax.all_to_all(blocks, axis, 0, 0, tiled=True)  22.1 us
    pallas_call x7, Pallas kernels, call(): pl.pallas_call(kernel, out_shape=tuple((jax.ShapeDtypeStruct(shape, dtype...  15 us
    all_to_all x2, waiting for transfers between devices, exchange(): return lax.all_to_all(blocks, axis, 0, 0, tiled=True)  14.9 us
    unnamed x14, local copies, waits for them, and re-layouts  2.01 us
  transfers between devices with their start and end apart: 2, of which 2 were waited for; matrix products, arithmetic and copies ran while one was open for 0% of the time, Pallas kernels for 7%

profile of v5, /device:TPU:8, one launch (start us, length us, event | category | flops | bytes accessed | tf_op | source)
XLA Modules:
  0.0 81.6 jit_solution(2412710738202624380)
XLA Ops:
  0.6 2.2 %norm.1 = (bf16[8,128,128]{2,1,0:T(8,128)(2,1)S(1)}, bf16[16,32,128]{2,1,0:T(8,128)(2,1)}, bf16[128,512]{1,0:T(8,128)(2,1)S(1)}, f32[1,128]{1,0:T(1,128)S(1)}) custom-call(bf16[8,128,128]{2,1,0:T(8,128)(2,1)} %bitcast.17, f32[1,128]{1,0:T(1,128)} %bitcast.14, bf16[4,128]{1,0:T(4,128)(2,1)} %bitcast.11, bf16[128,512]{1,0:T(8,128)(2,1)} %proj_weight_ref.1, ...), custom_call_target="tpu_custom_call" | custom-call | tf_op jit(solution)/shard_map/norm/pallas_call | solution.py:418
  2.9 9.1 %all-to-all-start = ((bf16[16,32,128]{2,1,0:T(8,128)(2,1)}), bf16[16,32,128]{2,1,0:T(8,128)(2,1)S(1)}, u32[]{:S(2)}, u32[]{:S(2)}) async-start(bf16[16,32,128]{2,1,0:T(8,128)(2,1)} %get-tuple-element.29), calls=%async_computation | async-start | bytes 262144 | tf_op jit(solution)/shard_map/all_to_all | solution.py:431
  12.7 0.1 pad_add_fusion.place_ref
  12.7 2.0 %project.1 = (bf16[8,960,128]{2,1,0:T(8,128)(2,1)S(1)}, f32[8,256,128]{2,1,0:T(8,128)S(1)}) custom-call(s32[2]{0:T(128)S(1)} %pad_add_fusion.place_ref, bf16[8,128,128]{2,1,0:T(8,128)(2,1)S(1)} %get-tuple-element.30.normed_ref, bf16[128,512]{1,0:T(8,128)(2,1)S(1)} %get-tuple-element.31.proj_weight_ref, f32[1,128]{1,0:T(1,128)S(1)} %get-tuple-element.32.gate_shift_ref, ...), custom_call_target="tpu_custom_call" | custom-call | flops 3000000000 | bytes 10000000 | tf_op jit(solution)/shard_map/project/pallas_call | solution.py:418
  14.7 5.3 %all-to-all-done.bias_ref = bf16[16,32,128]{2,1,0:T(8,128)(2,1)S(1)} async-done(((bf16[16,32,128]{2,1,0:T(8,128)(2,1)}), bf16[16,32,128]{2,1,0:T(8,128)(2,1)S(1)}, u32[]{:S(2)}, u32[]{:S(2)}) %all-to-all-start) | async-done | bytes 131104 | tf_op jit(solution)/shard_map/all_to_all | solution.py:431
  20.0 5.3 %attend.1 = (bf16[16,80,128]{2,1,0:T(8,128)(2,1)S(1)}, bf16[8,128,128]{2,1,0:T(8,128)(2,1)S(1)}, f32[8,128,128]{2,1,0:T(8,128)S(1)}, f32[1,128]{1,0:T(1,128)S(1)}) custom-call(s32[2]{0:T(128)S(1)} %pad_add_fusion.place_ref, bf16[16,32,128]{2,1,0:T(8,128)(2,1)S(1)} %all-to-all-done.bias_ref, bf16[8,128,128]{2,1,0:T(8,128)(2,1)S(1)} %get-tuple-element.30.normed_ref, ...), custom_call_target="tpu_custom_call" | custom-call | tf_op jit(solution)/shard_map/attend/pallas_call | solution.py:418
  25.3 0.0 copy-start
  25.3 0.0 copy-start.3
  25.3 13.3 %all_to_all.20.parts_ref = bf16[16,80,128]{2,1,0:T(8,128)(2,1)S(1)} all-to-all(bf16[16,80,128]{2,1,0:T(8,128)(2,1)S(1)} %get-tuple-element.35), channel_id=1, replica_groups=mesh['dp'=32,'dap'=16] {'dap'}, dimensions={0} | all-to-all | bytes 655360 | tf_op jit(solution)/shard_map/all_to_all | solution.py:431
  38.6 1.0 %bias_grad.1 = (bf16[32,128]{1,0:T(8,128)(2,1)S(1)}, bf16[32,48,128]{2,1,0:T(8,128)(2,1)}) custom-call(bf16[16,80,128]{2,1,0:T(8,128)(2,1)S(1)} %all_to_all.20.parts_ref, bf16[8,128,128]{2,1,0:T(8,128)(2,1)S(1)} %get-tuple-element.30.normed_ref, f32[1,128]{1,0:T(1,128)S(1)} %get-tuple-element.36.shift_ref, ...), custom_call_target="tpu_custom_call" | custom-call | tf_op jit(solution)/shard_map/bias_grad/pallas_call | solution.py:418
  39.6 0.0 copy-done
  39.6 0.0 copy-done.3
  39.6 13.0 %all-to-all-start.2 = ((bf16[32,48,128]{2,1,0:T(8,128)(2,1)}), bf16[32,48,128]{2,1,0:T(8,128)(2,1)S(1)}, u32[]{:S(2)}, u32[]{:S(2)}) async-start(bf16[32,48,128]{2,1,0:T(8,128)(2,1)} %get-tuple-element.39), calls=%async_computation.2 | async-start | bytes 786432 | tf_op jit(solution)/shard_map/all_to_all | solution.py:431
  52.6 0.0 copy-start.1
  52.6 1.0 %copy-done.1 = f32[8,128,128]{2,1,0:T(8,128)S(1)} copy-done((f32[8,128,128]{2,1,0:T(8,128)S(1)}, f32[8,128,128]{2,1,0:T(8,128)}, u32[]{:S(2)}) %copy-start.1) | copy-done | bytes 524312
  53.6 0.0 copy-start.4
  53.6 0.9 %copy-done.4 = bf16[8,128,128]{2,1,0:T(8,128)(2,1)S(1)} copy-done((bf16[8,128,128]{2,1,0:T(8,128)(2,1)S(1)}, bf16[8,128,128]{2,1,0:T(8,128)(2,1)}, u32[]{:S(2)}) %copy-start.4) | copy-done | bytes 262168
  54.6 0.0 copy-start.2
  54.6 0.0 copy-start.5
  54.6 0.0 copy-start.6
  54.6 3.7 %finish.1 = (bf16[8,128,128]{2,1,0:T(8,128)(2,1)}, bf16[8,128,128]{2,1,0:T(8,128)(2,1)}) custom-call(s32[2]{0:T(128)S(1)} %pad_add_fusion.place_ref, bf16[8,128,128]{2,1,0:T(8,128)(2,1)S(1)} %copy-done.4, f32[8,128,128]{2,1,0:T(8,128)S(1)} %copy-done.1, bf16[32,128]{1,0:T(8,128)(2,1)S(1)} %get-tuple-element.40.bias_grad_ref, bf16[8,128,128]{2,1,0:T(8,128)(2,1)} %bitcast.18, ...), custom_call_target="tpu_custom_call" | custom-call | flops 2000000000 | bytes 6000000 | tf_op jit(solution)/shard_map/finish/pallas_call | solution.py:418
  58.3 9.6 %all-to-all-done.2.sums_ref = bf16[32,48,128]{2,1,0:T(8,128)(2,1)S(1)} async-done(((bf16[32,48,128]{2,1,0:T(8,128)(2,1)}), bf16[32,48,128]{2,1,0:T(8,128)(2,1)S(1)}, u32[]{:S(2)}, u32[]{:S(2)}) %all-to-all-start.2) | async-done | bytes 393248 | tf_op jit(solution)/shard_map/all_to_all | solution.py:431
  67.9 0.1 sum.1
  68.0 12.8 %all_to_all.21.blocks_ref = bf16[16,48,128]{2,1,0:T(8,128)(2,1)S(1)} all-to-all(bf16[16,48,128]{2,1,0:T(8,128)(2,1)S(1)} %sum.1), channel_id=1, replica_groups=mesh['dp'=32,'dap'=16] {'dap'}, dimensions={0} | all-to-all | bytes 393216 | tf_op jit(solution)/shard_map/all_to_all | solution.py:431
  80.8 0.0 copy-done.2
  80.8 0.0 copy-done.5
  80.8 0.0 copy-done.6
  80.8 0.8 assemble.1
Async XLA Ops:
  2.9 17.1 %all-to-all-start = ((bf16[16,32,128]{2,1,0:T(8,128)(2,1)}), bf16[16,32,128]{2,1,0:T(8,128)(2,1)S(1)}, u32[]{:S(2)}, u32[]{:S(2)}) async-start(bf16[16,32,128]{2,1,0:T(8,128)(2,1)} %get-tuple-element.29), calls=%async_computation | async-start | bytes 262144 | tf_op jit(solution)/shard_map/all_to_all | solution.py:431
  25.3 14.3 %copy-start = (f32[8,128,128]{2,1,0:T(8,128)}, f32[8,128,128]{2,1,0:T(8,128)S(1)}, u32[]{:S(2)}) copy-start(f32[8,128,128]{2,1,0:T(8,128)S(1)} %get-tuple-element.38.normed_proj_ref) | copy-start | bytes 1572868
  25.3 14.3 %copy-start.3 = (bf16[8,128,128]{2,1,0:T(8,128)(2,1)}, bf16[8,128,128]{2,1,0:T(8,128)(2,1)S(1)}, u32[]{:S(2)}) copy-start(bf16[8,128,128]{2,1,0:T(8,128)(2,1)S(1)} %get-tuple-element.37.mixed_ref) | copy-start | bytes 786436
  39.6 28.3 %all-to-all-start.2 = ((bf16[32,48,128]{2,1,0:T(8,128)(2,1)}), bf16[32,48,128]{2,1,0:T(8,128)(2,1)S(1)}, u32[]{:S(2)}, u32[]{:S(2)}) async-start(bf16[32,48,128]{2,1,0:T(8,128)(2,1)} %get-tuple-element.39), calls=%async_computation.2 | async-start | bytes 786432 | tf_op jit(solution)/shard_map/all_to_all | solution.py:431
  52.6 1.0 %copy-start.1 = (f32[8,128,128]{2,1,0:T(8,128)S(1)}, f32[8,128,128]{2,1,0:T(8,128)}, u32[]{:S(2)}) copy-start(f32[8,128,128]{2,1,0:T(8,128)} %copy-done) | copy-start | bytes 1572868
  53.6 0.9 %copy-start.4 = (bf16[8,128,128]{2,1,0:T(8,128)(2,1)S(1)}, bf16[8,128,128]{2,1,0:T(8,128)(2,1)}, u32[]{:S(2)}) copy-start(bf16[8,128,128]{2,1,0:T(8,128)(2,1)} %copy-done.3) | copy-start | bytes 786436
  54.6 26.2 %copy-start.2 = (bf16[128,512]{1,0:T(8,128)(2,1)S(1)}, bf16[128,512]{1,0:T(8,128)(2,1)}, u32[]{:S(2)}) copy-start(bf16[128,512]{1,0:T(8,128)(2,1)} %proj_weight_ref.1) | copy-start | bytes 393220
  54.6 26.2 %copy-start.5 = (bf16[128,4]{0,1:T(4,128)(2,1)S(1)}, bf16[128,4]{0,1:T(4,128)(2,1)}, u32[]{:S(2)}) copy-start(bf16[128,4]{0,1:T(4,128)(2,1)} %param.14) | copy-start | bytes 3076
  54.6 26.2 %copy-start.6 = (f32[128]{0:T(128)S(1)}, f32[128]{0:T(128)}, u32[]{:S(2)}) copy-start(f32[128]{0:T(128)} %param.15) | copy-start | bytes 1540

commit v6 on v5

--- a/solution.py
+++ b/solution.py
@@ -12,8 +12,9 @@
 F32 = jnp.float32
 BF16 = jnp.bfloat16
 VMEM_LIMIT = 16 * 1024 * 1024
+PAIR_PIECES = 1
 UNROLL_PROJECT = 4
-UNROLL_ATTEND = 4
+UNROLL_ATTEND = 8
 
 
 def dot(a, b):
@@ -79,14 +80,21 @@
 ):
     row_count = pair.shape[0]
     heads = bias_weight.shape[0]
+    pieces = sems.shape[0] - 4
+    step = row_count // pieces
+    spans = [slice(n * step, (n + 1) * step) for n in range(pieces)]
     copies = begin_all(
-        (gain_hbm, bias_weight_hbm, pair_hbm, proj_weight_hbm, gate_shift_hbm),
-        (gain, bias_weight, pair, proj_weight_ref, gate_shift_ref),
+        (gain_hbm, bias_weight_hbm, *(pair_hbm.at[span] for span in spans))
+        + (proj_weight_hbm, gate_shift_hbm),
+        (gain, bias_weight, *(pair.at[span] for span in spans))
+        + (proj_weight_ref, gate_shift_ref),
         sems,
     )
-    for copy in copies[:3]:
+    for copy in copies[:2]:
         copy.wait()
     for row in range(row_count):
+        if row % step == 0:
+            copies[2 + row // step].wait()
         x_hat, _ = standardize(pair[row])
         normed = (x_hat * gain[...]).astype(BF16)
         normed_ref[row] = normed
@@ -94,7 +102,7 @@
     block = held[...].astype(BF16)
     for peer in range(bias_ref.shape[0]):
         bias_ref[peer] = block
-    for copy in copies[3:]:
+    for copy in copies[2 + pieces :]:
         copy.wait()
 
 
@@ -261,7 +269,7 @@
 
 
 def bias_kernel(
-    parts_ref, normed_ref, shift_ref, mixed_ref, normed_proj_ref, bias_grad_ref, sums_ref, held
+    parts_ref, normed_ref, shift_ref, mixed_ref, normed_proj_ref, bias_grad_ref, held
 ):
     del mixed_ref, normed_proj_ref
     row_count, width, channels = normed_ref.shape
@@ -286,16 +294,19 @@
             grad_bias[h * row_count : (h + 1) * row_count], 0, keepdims=True
         )
     held[grads + heads : grads + heads + 1] = shift_ref[...]
-    block = held[...].astype(BF16)
+
+
+def pair_kernel(own_ref, other_ref, sums_ref):
+    block = (own_ref[...] + other_ref[...]).astype(BF16)
     for peer in range(sums_ref.shape[0]):
         sums_ref[peer] = block
 
 
 def finish_kernel(
     place_ref,
-    mixed_ref,
-    normed_proj_ref,
     bias_grad_ref,
+    mixed_hbm,
+    normed_proj_hbm,
     pair_hbm,
     cot_hbm,
     gain_hbm,
@@ -308,11 +319,29 @@
     gain_ref,
     bias_weight_ref,
     out_weight_ref,
+    mixed_ref,
+    normed_proj_ref,
     sems,
 ):
     copies = begin_all(
-        (pair_hbm, cot_hbm, gain_hbm, bias_weight_hbm, out_weight_hbm),
-        (pair_ref, cot_ref, gain_ref, bias_weight_ref, out_weight_ref),
+        (
+            pair_hbm,
+            cot_hbm,
+            gain_hbm,
+            bias_weight_hbm,
+            out_weight_hbm,
+            mixed_hbm,
+            normed_proj_hbm,
+        ),
+        (
+            pair_ref,
+            cot_ref,
+            gain_ref,
+            bias_weight_ref,
+            out_weight_ref,
+            mixed_ref,
+            normed_proj_ref,
+        ),
         sems,
     )
     row_count, width, channels = pair_ref.shape
@@ -427,8 +456,8 @@
             name=name,
         )(*args[: placed + near], *(away(a) for a in args[placed + near :]))
 
-    def exchange(blocks, axis):
-        return lax.all_to_all(blocks, axis, 0, 0, tiled=True)
+    def exchange(blocks, axis, groups=None):
+        return lax.all_to_all(blocks, axis, 0, 0, axis_index_groups=groups, tiled=True)
 
     inputs = (pair, gain, bias_weight_t, proj_weight, gate_shift[None])
     normed, bias_copies, near_proj, near_shift = call(
@@ -446,7 +475,7 @@
             (bias_weight_t.shape, BF16),
             ((shared, width), F32),
         ],
-        sems=len(inputs),
+        sems=len(inputs) - 1 + PAIR_PIECES,
     )
     bias_all = exchange(bias_copies, "dap")
     place = jnp.stack([lengths[0], lax.axis_index("dap") * row_count]).astype(jnp.int32)
@@ -486,19 +515,28 @@
         near=4,
     )
     parts = exchange(parts, "dap")
-    bias_grad, sums = call(
+    bias_grad, own = call(
         bias_kernel,
         "bias_grad",
         (parts, normed, shift, mixed, normed_proj),
-        [((shared, width), BF16), ((samples, chunk, channels), BF16)],
-        [((chunk, channels), F32)],
+        [((shared, width), BF16), ((chunk, channels), F32)],
         near=5,
     )
-    sums = exchange(sums, "dp")
+    other = lax.ppermute(own, "dp", [(n, n ^ 1) for n in range(samples)])
+    bias_grad, other = lax.optimization_barrier((bias_grad, other))
+    (sums,) = call(
+        pair_kernel,
+        "pair",
+        (own, other),
+        [((samples // 2, chunk, channels), BF16)],
+        near=2,
+    )
+    same_core = [list(range(core, samples, 2)) for core in range(2)]
+    sums = exchange(sums, "dp", same_core)
     updated, pair_grad = call(
         finish_kernel,
         "finish",
-        (place, mixed, normed_proj, bias_grad, pair, cot, gain, bias_weight_t, out_weight),
+        (place, bias_grad, mixed, normed_proj, pair, cot, gain, bias_weight_t, out_weight),
         [(rows_shape, BF16), (rows_shape, BF16)],
         [
             (rows_shape, BF16),
@@ -506,10 +544,12 @@
             line,
             (bias_weight_t.shape, BF16),
             (out_weight.shape, BF16),
+            (rows_shape, BF16),
+            (rows_shape, F32),
         ],
         placed=True,
-        near=3,
-        sems=5,
+        near=1,
+        sems=7,
         flops=2 * 10**9,
         moved=6 * 10**6,
     )

time: 82.1 us -> 81.4 us (level)
  local copies, waits for them, and re-layouts: 2.01 us -> 0.03 us
  starting transfers between devices: 22.1 us -> 23.7 us
    unnamed x14 -> x10, local copies, waits for them, and re-layouts: 2.01 us -> 0.03 us
    ppermute x0 -> x1, starting transfers between devices: none -> 1.92 us  [per_device(): other = lax.ppermute(own, 'dp', [(n, n ^ 1) for n in range(samples)])]
    ppermute x0 -> x1, waiting for transfers between devices: none -> 1.16 us  [per_device(): other = lax.ppermute(own, 'dp', [(n, n ^ 1) for n in range(samples)])]
    all_to_all x2, waiting for transfers between devices: 14.9 us -> 13.9 us  [exchange(): lax.all_to_all(blocks, axis, 0, 0, axis_index_groups=groups, tiled=True)]
    pallas_call x7 -> x8, Pallas kernels: 15 us -> 14.7 us  [call(): pl.pallas_call(kernel, out_shape=tuple((jax.ShapeDtypeStruct(shape, dtype...]
  transfers between devices with their start and end apart: 2 -> 3, of which waited for: 2 -> 3; matrix products, arithmetic and copies ran while one was open for 0% -> 0% of each run, Pallas kernels for 7% -> 7%
where the time goes in v6:
time: 81.4 us; the launch traced here: 81 us
  blocking collectives  26 us (32%)
  starting transfers between devices  23.7 us (29%)
  waiting for transfers between devices  15 us (18%)
  Pallas kernels  14.7 us (18%)
  between operations  1.4 us (2%)
    all_to_all x2, blocking collectives, exchange(): lax.all_to_all(blocks, axis, 0, 0, axis_index_groups=groups, tiled=True)  26 us
    all_to_all x2, starting transfers between devices, exchange(): lax.all_to_all(blocks, axis, 0, 0, axis_index_groups=groups, tiled=True)  21.8 us
    pallas_call x8, Pallas kernels, call(): pl.pallas_call(kernel, out_shape=tuple((jax.ShapeDtypeStruct(shape, dtype...  14.7 us
    all_to_all x2, waiting for transfers between devices, exchange(): lax.all_to_all(blocks, axis, 0, 0, axis_index_groups=groups, tiled=True)  13.9 us
    ppermute x1, starting transfers between devices, per_device(): other = lax.ppermute(own, 'dp', [(n, n ^ 1) for n in range(samples)])  1.92 us
  transfers between devices with their start and end apart: 3, of which 3 were waited for; matrix products, arithmetic and copies ran while one was open for 0% of the time, Pallas kernels for 7%

profile of v6, /device:TPU:8, one launch (start us, length us, event | category | flops | bytes accessed | tf_op | source)
XLA Modules:
  0.0 81.0 jit_solution(6655111362251986098)
XLA Ops:
  0.6 2.2 %norm.1 = (bf16[8,128,128]{2,1,0:T(8,128)(2,1)S(1)}, bf16[16,32,128]{2,1,0:T(8,128)(2,1)}, bf16[128,512]{1,0:T(8,128)(2,1)S(1)}, f32[1,128]{1,0:T(1,128)S(1)}) custom-call(bf16[8,128,128]{2,1,0:T(8,128)(2,1)} %bitcast.17, f32[1,128]{1,0:T(1,128)} %bitcast.14, bf16[4,128]{1,0:T(4,128)(2,1)} %bitcast.11, bf16[128,512]{1,0:T(8,128)(2,1)} %proj_weight_ref.1, ...), custom_call_target="tpu_custom_call" | custom-call | tf_op jit(solution)/shard_map/norm/pallas_call | solution.py:447
  2.9 9.1 %all-to-all-start = ((bf16[16,32,128]{2,1,0:T(8,128)(2,1)}), bf16[16,32,128]{2,1,0:T(8,128)(2,1)S(1)}, u32[]{:S(2)}, u32[]{:S(2)}) async-start(bf16[16,32,128]{2,1,0:T(8,128)(2,1)} %get-tuple-element.31), calls=%async_computation | async-start | bytes 262144 | tf_op jit(solution)/shard_map/all_to_all | solution.py:460
  12.7 0.1 pad_add_fusion.place_ref
  12.7 2.0 %project.1 = (bf16[8,960,128]{2,1,0:T(8,128)(2,1)S(1)}, f32[8,256,128]{2,1,0:T(8,128)S(1)}) custom-call(s32[2]{0:T(128)S(1)} %pad_add_fusion.place_ref, bf16[8,128,128]{2,1,0:T(8,128)(2,1)S(1)} %get-tuple-element.32.normed_ref, bf16[128,512]{1,0:T(8,128)(2,1)S(1)} %get-tuple-element.33.proj_weight_ref, f32[1,128]{1,0:T(1,128)S(1)} %get-tuple-element.34.gate_shift_ref, ...), custom_call_target="tpu_custom_call" | custom-call | flops 3000000000 | bytes 10000000 | tf_op jit(solution)/shard_map/project/pallas_call | solution.py:447
  14.7 5.3 %all-to-all-done.bias_ref = bf16[16,32,128]{2,1,0:T(8,128)(2,1)S(1)} async-done(((bf16[16,32,128]{2,1,0:T(8,128)(2,1)}), bf16[16,32,128]{2,1,0:T(8,128)(2,1)S(1)}, u32[]{:S(2)}, u32[]{:S(2)}) %all-to-all-start) | async-done | bytes 131104 | tf_op jit(solution)/shard_map/all_to_all | solution.py:460
  20.0 4.8 %attend.1 = (bf16[16,80,128]{2,1,0:T(8,128)(2,1)S(1)}, bf16[8,128,128]{2,1,0:T(8,128)(2,1)S(1)}, f32[8,128,128]{2,1,0:T(8,128)S(1)}, f32[1,128]{1,0:T(1,128)S(1)}) custom-call(s32[2]{0:T(128)S(1)} %pad_add_fusion.place_ref, bf16[16,32,128]{2,1,0:T(8,128)(2,1)S(1)} %all-to-all-done.bias_ref, bf16[8,128,128]{2,1,0:T(8,128)(2,1)S(1)} %get-tuple-element.32.normed_ref, ...), custom_call_target="tpu_custom_call" | custom-call | tf_op jit(solution)/shard_map/attend/pallas_call | solution.py:447
  24.8 0.0 copy-start
  24.8 0.0 copy-start.2
  24.9 13.3 %all_to_all.20.parts_ref = bf16[16,80,128]{2,1,0:T(8,128)(2,1)S(1)} all-to-all(bf16[16,80,128]{2,1,0:T(8,128)(2,1)S(1)} %get-tuple-element.37), channel_id=1, replica_groups=mesh['dp'=32,'dap'=16] {'dap'}, dimensions={0} | all-to-all | bytes 655360 | tf_op jit(solution)/shard_map/all_to_all | solution.py:460
  38.2 0.2 bias_grad.1
  38.4 0.0 copy-done
  38.4 0.0 copy-done.2
  38.4 1.9 %collective-permute-start = (f32[48,128]{1,0:T(8,128)S(1)}, f32[48,128]{1,0:T(8,128)S(1)}, u32[]{:S(2)}, u32[]{:S(2)}) collective-permute-start(f32[48,128]{1,0:T(8,128)S(1)} %get-tuple-element.41.own_ref), channel_id=1, source_target_pairs={{0,16},{16,0},{32,48},{48,32},{64,80},{80,64},{96,112},{112,96},{1... | collective-permute-start | bytes 73736 | tf_op jit(solution)/shard_map/ppermute | solution.py:525
  40.3 1.2 %collective-permute-done.other_ref = f32[48,128]{1,0:T(8,128)S(1)} collective-permute-done((f32[48,128]{1,0:T(8,128)S(1)}, f32[48,128]{1,0:T(8,128)S(1)}, u32[]{:S(2)}, u32[]{:S(2)}) %collective-permute-start) | collective-permute-done | bytes 24608 | tf_op jit(solution)/shard_map/ppermute | solution.py:525
  41.5 0.7 pair.1
  42.2 12.7 %all-to-all-start.2 = ((bf16[16,48,128]{2,1,0:T(8,128)(2,1)}), bf16[16,48,128]{2,1,0:T(8,128)(2,1)S(1)}, u32[]{:S(2)}, u32[]{:S(2)}) async-start(bf16[16,48,128]{2,1,0:T(8,128)(2,1)} %pair.1), calls=%async_computation.2 | async-start | bytes 393216 | tf_op jit(solution)/shard_map/all_to_all | solution.py:460
  54.9 0.0 copy-start.1
  54.9 0.0 copy-start.3
  54.9 0.0 copy-start.4
  54.9 4.0 %finish.1 = (bf16[8,128,128]{2,1,0:T(8,128)(2,1)}, bf16[8,128,128]{2,1,0:T(8,128)(2,1)}) custom-call(s32[2]{0:T(128)S(1)} %pad_add_fusion.place_ref, bf16[32,128]{1,0:T(8,128)(2,1)S(1)} %get-tuple-element.44.bias_grad_ref, bf16[8,128,128]{2,1,0:T(8,128)(2,1)} %copy-done.2, f32[8,128,128]{2,1,0:T(8,128)} %copy-done, bf16[8,128,128]{2,1,0:T(8,128)(2,1)} %bitcast.18, ...), custom_call_target="tpu_custom_call" | custom-call | flops 2000000000 | bytes 6000000 | tf_op jit(solution)/shard_map/finish/pallas_call | solution.py:447
  58.9 8.6 %all-to-all-done.2.sums_ref = bf16[16,48,128]{2,1,0:T(8,128)(2,1)S(1)} async-done(((bf16[16,48,128]{2,1,0:T(8,128)(2,1)}), bf16[16,48,128]{2,1,0:T(8,128)(2,1)S(1)}, u32[]{:S(2)}, u32[]{:S(2)}) %all-to-all-start.2) | async-done | bytes 196640 | tf_op jit(solution)/shard_map/all_to_all | solution.py:460
  67.5 12.6 %all_to_all.21.blocks_ref = bf16[16,48,128]{2,1,0:T(8,128)(2,1)S(1)} all-to-all(bf16[16,48,128]{2,1,0:T(8,128)(2,1)S(1)} %sum.1), channel_id=1, replica_groups=mesh['dp'=32,'dap'=16] {'dap'}, dimensions={0} | all-to-all | bytes 393216 | tf_op jit(solution)/shard_map/all_to_all | solution.py:460
  80.2 0.0 copy-done.1
  80.2 0.0 copy-done.3
  80.2 0.0 copy-done.4
  80.2 0.8 assemble.1
  (1 shorter events, 0.0 us)
Async XLA Ops:
  2.9 17.1 %all-to-all-start = ((bf16[16,32,128]{2,1,0:T(8,128)(2,1)}), bf16[16,32,128]{2,1,0:T(8,128)(2,1)S(1)}, u32[]{:S(2)}, u32[]{:S(2)}) async-start(bf16[16,32,128]{2,1,0:T(8,128)(2,1)} %get-tuple-element.31), calls=%async_computation | async-start | bytes 262144 | tf_op jit(solution)/shard_map/all_to_all | solution.py:460
  24.8 13.6 %copy-start = (f32[8,128,128]{2,1,0:T(8,128)}, f32[8,128,128]{2,1,0:T(8,128)S(1)}, u32[]{:S(2)}) copy-start(f32[8,128,128]{2,1,0:T(8,128)S(1)} %get-tuple-element.40.normed_proj_ref.normed_proj_hbm) | copy-start | bytes 1572868
  24.8 13.6 %copy-start.2 = (bf16[8,128,128]{2,1,0:T(8,128)(2,1)}, bf16[8,128,128]{2,1,0:T(8,128)(2,1)S(1)}, u32[]{:S(2)}) copy-start(bf16[8,128,128]{2,1,0:T(8,128)(2,1)S(1)} %get-tuple-element.39.mixed_ref.mixed_hbm) | copy-start | bytes 786436
  38.4 3.1 %collective-permute-start = (f32[48,128]{1,0:T(8,128)S(1)}, f32[48,128]{1,0:T(8,128)S(1)}, u32[]{:S(2)}, u32[]{:S(2)}) collective-permute-start(f32[48,128]{1,0:T(8,128)S(1)} %get-tuple-element.41.own_ref), channel_id=1, source_target_pairs={{0,16},{16,0},{32,48},{48,32},{64,80},{80,64},{96,112},{112,96},{1... | collective-permute-start | bytes 73736 | tf_op jit(solution)/shard_map/ppermute | solution.py:525
  42.2 25.3 %all-to-all-start.2 = ((bf16[16,48,128]{2,1,0:T(8,128)(2,1)}), bf16[16,48,128]{2,1,0:T(8,128)(2,1)S(1)}, u32[]{:S(2)}, u32[]{:S(2)}) async-start(bf16[16,48,128]{2,1,0:T(8,128)(2,1)} %pair.1), calls=%async_computation.2 | async-start | bytes 393216 | tf_op jit(solution)/shard_map/all_to_all | solution.py:460
  54.9 25.3 %copy-start.1 = (bf16[128,512]{1,0:T(8,128)(2,1)S(1)}, bf16[128,512]{1,0:T(8,128)(2,1)}, u32[]{:S(2)}) copy-start(bf16[128,512]{1,0:T(8,128)(2,1)} %proj_weight_ref.1) | copy-start | bytes 393220
  54.9 25.3 %copy-start.3 = (bf16[128,4]{0,1:T(4,128)(2,1)S(1)}, bf16[128,4]{0,1:T(4,128)(2,1)}, u32[]{:S(2)}) copy-start(bf16[128,4]{0,1:T(4,128)(2,1)} %param.14) | copy-start | bytes 3076
  54.9 25.3 %copy-start.4 = (f32[128]{0:T(128)S(1)}, f32[128]{0:T(128)}, u32[]{:S(2)}) copy-start(f32[128]{0:T(128)} %param.15) | copy-start | bytes 1540

commit v7 on v6

--- a/solution.py
+++ b/solution.py
@@ -12,7 +12,6 @@
 F32 = jnp.float32
 BF16 = jnp.bfloat16
 VMEM_LIMIT = 16 * 1024 * 1024
-PAIR_PIECES = 1
 UNROLL_PROJECT = 4
 UNROLL_ATTEND = 8
 
@@ -80,21 +79,14 @@
 ):
     row_count = pair.shape[0]
     heads = bias_weight.shape[0]
-    pieces = sems.shape[0] - 4
-    step = row_count // pieces
-    spans = [slice(n * step, (n + 1) * step) for n in range(pieces)]
     copies = begin_all(
-        (gain_hbm, bias_weight_hbm, *(pair_hbm.at[span] for span in spans))
-        + (proj_weight_hbm, gate_shift_hbm),
-        (gain, bias_weight, *(pair.at[span] for span in spans))
-        + (proj_weight_ref, gate_shift_ref),
+        (gain_hbm, bias_weight_hbm, pair_hbm, proj_weight_hbm, gate_shift_hbm),
+        (gain, bias_weight, pair, proj_weight_ref, gate_shift_ref),
         sems,
     )
-    for copy in copies[:2]:
+    for copy in copies[:3]:
         copy.wait()
     for row in range(row_count):
-        if row % step == 0:
-            copies[2 + row // step].wait()
         x_hat, _ = standardize(pair[row])
         normed = (x_hat * gain[...]).astype(BF16)
         normed_ref[row] = normed
@@ -102,7 +94,7 @@
     block = held[...].astype(BF16)
     for peer in range(bias_ref.shape[0]):
         bias_ref[peer] = block
-    for copy in copies[2 + pieces :]:
+    for copy in copies[3:]:
         copy.wait()
 
 
@@ -237,11 +229,12 @@
             1,
         )
         d_proj[row] = d_row
-        normed_proj_ref[row] = dot(d_row, weight_t[...])
         return shift_sum + jnp.sum(d_gating.astype(F32), 0, keepdims=True)
 
     zero = jnp.zeros((1, channels), F32)
     shift_ref[...] = lax.fori_loop(0, row_count, one_row, zero, unroll=UNROLL_ATTEND)
+    flat = d_proj[...].reshape(row_count * width, 4 * channels)
+    normed_proj_ref[...] = dot(flat, weight_t[...]).reshape(normed_proj_ref.shape)
     shared = heads * row_count
     for h in range(heads):
         turned = bias_sum[h * width : (h + 1) * width].T
@@ -251,7 +244,7 @@
             ]
     tokens = row_count * width
     normed = normed_ref[...].reshape(tokens, channels)
-    grad_proj = contract(normed, d_proj[...].reshape(tokens, 4 * channels), 0, 0)
+    grad_proj = contract(normed, flat, 0, 0)
     grad_out = contract(
         mixed_ref[...].reshape(tokens, channels),
         narrow_ref[:, 2 * width : 3 * width].reshape(tokens, channels),
@@ -263,8 +256,6 @@
         for i, piece in enumerate(pieces):
             start = shared + i * row_count
             parts[d, start : start + row_count] = piece[d * row_count : (d + 1) * row_count]
-    unused = shared + len(pieces) * row_count
-    parts[:, unused:] = jnp.zeros((devices, parts.shape[1] - unused, width), F32)
     parts_ref[...] = parts[...].astype(BF16)
 
 
@@ -475,7 +466,7 @@
             (bias_weight_t.shape, BF16),
             ((shared, width), F32),
         ],
-        sems=len(inputs) - 1 + PAIR_PIECES,
+        sems=len(inputs),
     )
     bias_all = exchange(bias_copies, "dap")
     place = jnp.stack([lengths[0], lax.axis_index("dap") * row_count]).astype(jnp.int32)
@@ -499,7 +490,7 @@
         "attend",
         (place, bias_all, normed, narrow, wide),
         [
-            ((devices, shared + chunk, width), BF16),
+            ((devices, shared + 5 * row_count, width), BF16),
             (rows_shape, BF16),
             (rows_shape, F32),
             line,
@@ -507,7 +498,7 @@
         [
             ((heads * width, width), F32),
             ((heads * width, width), F32),
-            ((devices, shared + chunk, width), F32),
+            ((devices, shared + 5 * row_count, width), F32),
             ((row_count, width, 4 * channels), BF16),
             ((4 * channels, channels), BF16),
         ],

time: 81.4 us -> 79.7 us (0.979)
  Pallas kernels: 14.7 us -> 13.7 us
    pallas_call x8, Pallas kernels: 14.7 us -> 13.7 us  [call(): pl.pallas_call(kernel, out_shape=tuple((jax.ShapeDtypeStruct(shape, dtype...]
  transfers between devices with their start and end apart: 3 -> 3, of which waited for: 3 -> 3; matrix products, arithmetic and copies ran while one was open for 0% -> 0% of each run, Pallas kernels for 7% -> 8%
where the time goes in v7:
time: 79.7 us; the launch traced here: 79.3 us
  blocking collectives  25.6 us (32%)
  starting transfers between devices  23.5 us (29%)
  waiting for transfers between devices  15 us (19%)
  Pallas kernels  13.7 us (17%)
  between operations  1.4 us (2%)
    all_to_all x2, blocking collectives, exchange(): lax.all_to_all(blocks, axis, 0, 0, axis_index_groups=groups, tiled=True)  25.6 us
    all_to_all x2, starting transfers between devices, exchange(): lax.all_to_all(blocks, axis, 0, 0, axis_index_groups=groups, tiled=True)  21.5 us
    all_to_all x2, waiting for transfers between devices, exchange(): lax.all_to_all(blocks, axis, 0, 0, axis_index_groups=groups, tiled=True)  13.9 us
    pallas_call x8, Pallas kernels, call(): pl.pallas_call(kernel, out_shape=tuple((jax.ShapeDtypeStruct(shape, dtype...  13.7 us
    ppermute x1, starting transfers between devices, per_device(): other = lax.ppermute(own, 'dp', [(n, n ^ 1) for n in range(samples)])  1.92 us
  transfers between devices with their start and end apart: 3, of which 3 were waited for; matrix products, arithmetic and copies ran while one was open for 0% of the time, Pallas kernels for 8%

profile of v7, /device:TPU:8, one launch (start us, length us, event | category | flops | bytes accessed | tf_op | source)
XLA Modules:
  0.0 79.3 jit_solution(2918726324379255895)
XLA Ops:
  0.6 2.2 %norm.1 = (bf16[8,128,128]{2,1,0:T(8,128)(2,1)S(1)}, bf16[16,32,128]{2,1,0:T(8,128)(2,1)}, bf16[128,512]{1,0:T(8,128)(2,1)S(1)}, f32[1,128]{1,0:T(1,128)S(1)}) custom-call(bf16[8,128,128]{2,1,0:T(8,128)(2,1)} %bitcast.17, f32[1,128]{1,0:T(1,128)} %bitcast.14, bf16[4,128]{1,0:T(4,128)(2,1)} %bitcast.11, bf16[128,512]{1,0:T(8,128)(2,1)} %proj_weight_ref.1, ...), custom_call_target="tpu_custom_call" | custom-call | tf_op jit(solution)/shard_map/norm/pallas_call | solution.py:438
  2.9 9.1 %all-to-all-start = ((bf16[16,32,128]{2,1,0:T(8,128)(2,1)}), bf16[16,32,128]{2,1,0:T(8,128)(2,1)S(1)}, u32[]{:S(2)}, u32[]{:S(2)}) async-start(bf16[16,32,128]{2,1,0:T(8,128)(2,1)} %get-tuple-element.31), calls=%async_computation | async-start | bytes 262144 | tf_op jit(solution)/shard_map/all_to_all | solution.py:451
  12.7 0.1 pad_add_fusion.place_ref
  12.7 2.0 %project.1 = (bf16[8,960,128]{2,1,0:T(8,128)(2,1)S(1)}, f32[8,256,128]{2,1,0:T(8,128)S(1)}) custom-call(s32[2]{0:T(128)S(1)} %pad_add_fusion.place_ref, bf16[8,128,128]{2,1,0:T(8,128)(2,1)S(1)} %get-tuple-element.32.normed_ref, bf16[128,512]{1,0:T(8,128)(2,1)S(1)} %get-tuple-element.33.proj_weight_ref, f32[1,128]{1,0:T(1,128)S(1)} %get-tuple-element.34.gate_shift_ref, ...), custom_call_target="tpu_custom_call" | custom-call | flops 3000000000 | bytes 10000000 | tf_op jit(solution)/shard_map/project/pallas_call | solution.py:438
  14.7 5.3 %all-to-all-done.bias_ref = bf16[16,32,128]{2,1,0:T(8,128)(2,1)S(1)} async-done(((bf16[16,32,128]{2,1,0:T(8,128)(2,1)}), bf16[16,32,128]{2,1,0:T(8,128)(2,1)S(1)}, u32[]{:S(2)}, u32[]{:S(2)}) %all-to-all-start) | async-done | bytes 131104 | tf_op jit(solution)/shard_map/all_to_all | solution.py:451
  20.0 3.8 %attend.1 = (bf16[16,72,128]{2,1,0:T(8,128)(2,1)S(1)}, bf16[8,128,128]{2,1,0:T(8,128)(2,1)S(1)}, f32[8,128,128]{2,1,0:T(8,128)S(1)}, f32[1,128]{1,0:T(1,128)S(1)}) custom-call(s32[2]{0:T(128)S(1)} %pad_add_fusion.place_ref, bf16[16,32,128]{2,1,0:T(8,128)(2,1)S(1)} %all-to-all-done.bias_ref, bf16[8,128,128]{2,1,0:T(8,128)(2,1)S(1)} %get-tuple-element.32.normed_ref, ...), custom_call_target="tpu_custom_call" | custom-call | tf_op jit(solution)/shard_map/attend/pallas_call | solution.py:438
  23.8 0.0 copy-start
  23.9 0.0 copy-start.2
  23.9 13.0 %all_to_all.20.parts_ref = bf16[16,72,128]{2,1,0:T(8,128)(2,1)S(1)} all-to-all(bf16[16,72,128]{2,1,0:T(8,128)(2,1)S(1)} %get-tuple-element.37), channel_id=1, replica_groups=mesh['dp'=32,'dap'=16] {'dap'}, dimensions={0} | all-to-all | bytes 589824 | tf_op jit(solution)/shard_map/all_to_all | solution.py:451
  36.9 0.2 bias_grad.1
  37.1 0.0 copy-done
  37.1 0.0 copy-done.2
  37.1 1.9 %collective-permute-start = (f32[48,128]{1,0:T(8,128)S(1)}, f32[48,128]{1,0:T(8,128)S(1)}, u32[]{:S(2)}, u32[]{:S(2)}) collective-permute-start(f32[48,128]{1,0:T(8,128)S(1)} %get-tuple-element.41.own_ref), channel_id=1, source_target_pairs={{0,16},{16,0},{32,48},{48,32},{64,80},{80,64},{96,112},{112,96},{1... | collective-permute-start | bytes 73736 | tf_op jit(solution)/shard_map/ppermute | solution.py:516
  39.0 1.2 %collective-permute-done.other_ref = f32[48,128]{1,0:T(8,128)S(1)} collective-permute-done((f32[48,128]{1,0:T(8,128)S(1)}, f32[48,128]{1,0:T(8,128)S(1)}, u32[]{:S(2)}, u32[]{:S(2)}) %collective-permute-start) | collective-permute-done | bytes 24608 | tf_op jit(solution)/shard_map/ppermute | solution.py:516
  40.2 0.7 pair.1
  40.9 12.4 %all-to-all-start.2 = ((bf16[16,48,128]{2,1,0:T(8,128)(2,1)}), bf16[16,48,128]{2,1,0:T(8,128)(2,1)S(1)}, u32[]{:S(2)}, u32[]{:S(2)}) async-start(bf16[16,48,128]{2,1,0:T(8,128)(2,1)} %pair.1), calls=%async_computation.2 | async-start | bytes 393216 | tf_op jit(solution)/shard_map/all_to_all | solution.py:451
  53.3 0.0 copy-start.1
  53.3 0.0 copy-start.3
  53.3 0.0 copy-start.4
  53.3 4.0 %finish.1 = (bf16[8,128,128]{2,1,0:T(8,128)(2,1)}, bf16[8,128,128]{2,1,0:T(8,128)(2,1)}) custom-call(s32[2]{0:T(128)S(1)} %pad_add_fusion.place_ref, bf16[32,128]{1,0:T(8,128)(2,1)S(1)} %get-tuple-element.44.bias_grad_ref, bf16[8,128,128]{2,1,0:T(8,128)(2,1)} %copy-done.2, f32[8,128,128]{2,1,0:T(8,128)} %copy-done, bf16[8,128,128]{2,1,0:T(8,128)(2,1)} %bitcast.18, ...), custom_call_target="tpu_custom_call" | custom-call | flops 2000000000 | bytes 6000000 | tf_op jit(solution)/shard_map/finish/pallas_call | solution.py:438
  57.4 8.6 %all-to-all-done.2.sums_ref = bf16[16,48,128]{2,1,0:T(8,128)(2,1)S(1)} async-done(((bf16[16,48,128]{2,1,0:T(8,128)(2,1)}), bf16[16,48,128]{2,1,0:T(8,128)(2,1)S(1)}, u32[]{:S(2)}, u32[]{:S(2)}) %all-to-all-start.2) | async-done | bytes 196640 | tf_op jit(solution)/shard_map/all_to_all | solution.py:451
  66.0 12.5 %all_to_all.21.blocks_ref = bf16[16,48,128]{2,1,0:T(8,128)(2,1)S(1)} all-to-all(bf16[16,48,128]{2,1,0:T(8,128)(2,1)S(1)} %sum.1), channel_id=1, replica_groups=mesh['dp'=32,'dap'=16] {'dap'}, dimensions={0} | all-to-all | bytes 393216 | tf_op jit(solution)/shard_map/all_to_all | solution.py:451
  78.5 0.0 copy-done.1
  78.5 0.0 copy-done.3
  78.5 0.0 copy-done.4
  78.5 0.8 assemble.1
  (1 shorter events, 0.0 us)
Async XLA Ops:
  2.9 17.1 %all-to-all-start = ((bf16[16,32,128]{2,1,0:T(8,128)(2,1)}), bf16[16,32,128]{2,1,0:T(8,128)(2,1)S(1)}, u32[]{:S(2)}, u32[]{:S(2)}) async-start(bf16[16,32,128]{2,1,0:T(8,128)(2,1)} %get-tuple-element.31), calls=%async_computation | async-start | bytes 262144 | tf_op jit(solution)/shard_map/all_to_all | solution.py:451
  23.8 13.2 %copy-start = (f32[8,128,128]{2,1,0:T(8,128)}, f32[8,128,128]{2,1,0:T(8,128)S(1)}, u32[]{:S(2)}) copy-start(f32[8,128,128]{2,1,0:T(8,128)S(1)} %get-tuple-element.40.normed_proj_ref.normed_proj_hbm) | copy-start | bytes 1572868
  23.9 13.2 %copy-start.2 = (bf16[8,128,128]{2,1,0:T(8,128)(2,1)}, bf16[8,128,128]{2,1,0:T(8,128)(2,1)S(1)}, u32[]{:S(2)}) copy-start(bf16[8,128,128]{2,1,0:T(8,128)(2,1)S(1)} %get-tuple-element.39.mixed_ref.mixed_hbm) | copy-start | bytes 786436
  37.1 3.1 %collective-permute-start = (f32[48,128]{1,0:T(8,128)S(1)}, f32[48,128]{1,0:T(8,128)S(1)}, u32[]{:S(2)}, u32[]{:S(2)}) collective-permute-start(f32[48,128]{1,0:T(8,128)S(1)} %get-tuple-element.41.own_ref), channel_id=1, source_target_pairs={{0,16},{16,0},{32,48},{48,32},{64,80},{80,64},{96,112},{112,96},{1... | collective-permute-start | bytes 73736 | tf_op jit(solution)/shard_map/ppermute | solution.py:516
  40.9 25.0 %all-to-all-start.2 = ((bf16[16,48,128]{2,1,0:T(8,128)(2,1)}), bf16[16,48,128]{2,1,0:T(8,128)(2,1)S(1)}, u32[]{:S(2)}, u32[]{:S(2)}) async-start(bf16[16,48,128]{2,1,0:T(8,128)(2,1)} %pair.1), calls=%async_computation.2 | async-start | bytes 393216 | tf_op jit(solution)/shard_map/all_to_all | solution.py:451
  53.3 25.2 %copy-start.1 = (bf16[128,512]{1,0:T(8,128)(2,1)S(1)}, bf16[128,512]{1,0:T(8,128)(2,1)}, u32[]{:S(2)}) copy-start(bf16[128,512]{1,0:T(8,128)(2,1)} %proj_weight_ref.1) | copy-start | bytes 393220
  53.3 25.2 %copy-start.3 = (bf16[128,4]{0,1:T(4,128)(2,1)S(1)}, bf16[128,4]{0,1:T(4,128)(2,1)}, u32[]{:S(2)}) copy-start(bf16[128,4]{0,1:T(4,128)(2,1)} %param.14) | copy-start | bytes 3076
  53.3 25.2 %copy-start.4 = (f32[128]{0:T(128)S(1)}, f32[128]{0:T(128)}, u32[]{:S(2)}) copy-start(f32[128]{0:T(128)} %param.15) | copy-start | bytes 1540

commit v8 on v7

--- a/solution.py
+++ b/solution.py
@@ -260,7 +260,7 @@
 
 
 def bias_kernel(
-    parts_ref, normed_ref, shift_ref, mixed_ref, normed_proj_ref, bias_grad_ref, held
+    parts_ref, normed_ref, shift_ref, mixed_ref, normed_proj_ref, bias_grad_ref, own_ref, held
 ):
     del mixed_ref, normed_proj_ref
     row_count, width, channels = normed_ref.shape
@@ -285,10 +285,14 @@
             grad_bias[h * row_count : (h + 1) * row_count], 0, keepdims=True
         )
     held[grads + heads : grads + heads + 1] = shift_ref[...]
-
-
-def pair_kernel(own_ref, other_ref, sums_ref):
-    block = (own_ref[...] + other_ref[...]).astype(BF16)
+    own_ref[...] = held[...].astype(BF16)
+
+
+def pair_kernel(near_ref, sums_ref):
+    block = near_ref[0].astype(F32)
+    for n in range(1, near_ref.shape[0]):
+        block = block + near_ref[n].astype(F32)
+    block = block.astype(BF16)
     for peer in range(sums_ref.shape[0]):
         sums_ref[peer] = block
 
@@ -510,20 +514,23 @@
         bias_kernel,
         "bias_grad",
         (parts, normed, shift, mixed, normed_proj),
-        [((shared, width), BF16), ((chunk, channels), F32)],
+        [((shared, width), BF16), ((chunk, channels), BF16)],
+        [((chunk, channels), F32)],
         near=5,
     )
-    other = lax.ppermute(own, "dp", [(n, n ^ 1) for n in range(samples)])
-    bias_grad, other = lax.optimization_barrier((bias_grad, other))
+    near = 4
+    runs = [list(range(n, n + near)) for n in range(0, samples, near)]
+    across = [list(range(n, samples, near)) for n in range(near)]
+    gathered = lax.all_gather(own, "dp", axis=0, axis_index_groups=runs)
+    bias_grad, gathered = lax.optimization_barrier((bias_grad, gathered))
     (sums,) = call(
         pair_kernel,
         "pair",
-        (own, other),
-        [((samples // 2, chunk, channels), BF16)],
-        near=2,
-    )
-    same_core = [list(range(core, samples, 2)) for core in range(2)]
-    sums = exchange(sums, "dp", same_core)
+        (gathered,),
+        [((samples // near, chunk, channels), BF16)],
+        near=1,
+    )
+    sums = exchange(sums, "dp", across)
     updated, pair_grad = call(
         finish_kernel,
         "finish",
@@ -544,7 +551,6 @@
         flops=2 * 10**9,
         moved=6 * 10**6,
     )
-    sums, pair_grad, updated = lax.optimization_barrier((sums, pair_grad, updated))
     (blocks,) = call(
         sum_kernel, "sum", (sums,), [((devices, chunk, channels), BF16)], near=1
     )

time: 79.7 us -> 77.5 us (0.972)
  blocking collectives: 25.6 us -> 38.5 us
  starting transfers between devices: 23.5 us -> 13.6 us
  waiting for transfers between devices: 15 us -> 9.71 us
    all_to_all x2, starting transfers between devices: 21.5 us -> 13.6 us  [exchange(): lax.all_to_all(blocks, axis, 0, 0, axis_index_groups=groups, tiled=True)]
    all_gather x0 -> x1, blocking collectives: none -> 6.73 us  [per_device(): gathered = lax.all_gather(own, 'dp', axis=0, axis_index_groups=runs)]
    all_to_all x2, blocking collectives: 25.6 us -> 31.8 us  [exchange(): lax.all_to_all(blocks, axis, 0, 0, axis_index_groups=groups, tiled=True)]
    all_to_all x2, waiting for transfers between devices: 13.9 us -> 9.71 us  [exchange(): lax.all_to_all(blocks, axis, 0, 0, axis_index_groups=groups, tiled=True)]
    ppermute x1 -> x0, starting transfers between devices: 1.92 us -> none  [per_device(): other = lax.ppermute(own, 'dp', [(n, n ^ 1) for n in range(samples)])]
    ppermute x1 -> x0, waiting for transfers between devices: 1.16 us -> none  [per_device(): other = lax.ppermute(own, 'dp', [(n, n ^ 1) for n in range(samples)])]
  transfers between devices with their start and end apart: 3 -> 2, of which waited for: 3 -> 2; matrix products, arithmetic and copies ran while one was open for 0% -> 0% of each run, Pallas kernels for 8% -> 8%
where the time goes in v8:
time: 77.5 us; the launch traced here: 77.1 us
  blocking collectives  38.5 us (50%)
  Pallas kernels  13.7 us (18%)
  starting transfers between devices  13.6 us (18%)
  waiting for transfers between devices  9.71 us (13%)
  between operations  1.38 us (2%)
    all_to_all x2, blocking collectives, exchange(): lax.all_to_all(blocks, axis, 0, 0, axis_index_groups=groups, tiled=True)  31.8 us
    pallas_call x8, Pallas kernels, call(): pl.pallas_call(kernel, out_shape=tuple((jax.ShapeDtypeStruct(shape, dtype...  13.7 us
    all_to_all x2, starting transfers between devices, exchange(): lax.all_to_all(blocks, axis, 0, 0, axis_index_groups=groups, tiled=True)  13.6 us
    all_to_all x2, waiting for transfers between devices, exchange(): lax.all_to_all(blocks, axis, 0, 0, axis_index_groups=groups, tiled=True)  9.71 us
    all_gather x1, blocking collectives, per_device(): gathered = lax.all_gather(own, 'dp', axis=0, axis_index_groups=runs)  6.73 us
  transfers between devices with their start and end apart: 2, of which 2 were waited for; matrix products, arithmetic and copies ran while one was open for 0% of the time, Pallas kernels for 8%

profile of v8, /device:TPU:8, one launch (start us, length us, event | category | flops | bytes accessed | tf_op | source)
XLA Modules:
  0.0 77.1 jit_solution(2069975055943098778)
XLA Ops:
  0.6 2.2 %norm.1 = (bf16[8,128,128]{2,1,0:T(8,128)(2,1)S(1)}, bf16[16,32,128]{2,1,0:T(8,128)(2,1)}, bf16[128,512]{1,0:T(8,128)(2,1)S(1)}, f32[1,128]{1,0:T(1,128)S(1)}) custom-call(bf16[8,128,128]{2,1,0:T(8,128)(2,1)} %bitcast.19, f32[1,128]{1,0:T(1,128)} %bitcast.16, bf16[4,128]{1,0:T(4,128)(2,1)} %bitcast.13, bf16[128,512]{1,0:T(8,128)(2,1)} %proj_weight_ref.1, ...), custom_call_target="tpu_custom_call" | custom-call | tf_op jit(solution)/shard_map/norm/pallas_call | solution.py:442
  2.9 9.1 %all-to-all-start = ((bf16[16,32,128]{2,1,0:T(8,128)(2,1)}), bf16[16,32,128]{2,1,0:T(8,128)(2,1)S(1)}, u32[]{:S(2)}, u32[]{:S(2)}) async-start(bf16[16,32,128]{2,1,0:T(8,128)(2,1)} %get-tuple-element.28), calls=%async_computation | async-start | bytes 262144 | tf_op jit(solution)/shard_map/all_to_all | solution.py:455
  12.7 0.1 pad_add_fusion.place_ref
  12.7 2.0 %project.1 = (bf16[8,960,128]{2,1,0:T(8,128)(2,1)S(1)}, f32[8,256,128]{2,1,0:T(8,128)S(1)}) custom-call(s32[2]{0:T(128)S(1)} %pad_add_fusion.place_ref, bf16[8,128,128]{2,1,0:T(8,128)(2,1)S(1)} %get-tuple-element.29.normed_ref, bf16[128,512]{1,0:T(8,128)(2,1)S(1)} %get-tuple-element.30.proj_weight_ref, f32[1,128]{1,0:T(1,128)S(1)} %get-tuple-element.31.gate_shift_ref, ...), custom_call_target="tpu_custom_call" | custom-call | flops 3000000000 | bytes 10000000 | tf_op jit(solution)/shard_map/project/pallas_call | solution.py:442
  14.7 5.3 %all-to-all-done.bias_ref = bf16[16,32,128]{2,1,0:T(8,128)(2,1)S(1)} async-done(((bf16[16,32,128]{2,1,0:T(8,128)(2,1)}), bf16[16,32,128]{2,1,0:T(8,128)(2,1)S(1)}, u32[]{:S(2)}, u32[]{:S(2)}) %all-to-all-start) | async-done | bytes 131104 | tf_op jit(solution)/shard_map/all_to_all | solution.py:455
  20.0 3.8 %attend.1 = (bf16[16,72,128]{2,1,0:T(8,128)(2,1)S(1)}, bf16[8,128,128]{2,1,0:T(8,128)(2,1)S(1)}, f32[8,128,128]{2,1,0:T(8,128)S(1)}, f32[1,128]{1,0:T(1,128)S(1)}) custom-call(s32[2]{0:T(128)S(1)} %pad_add_fusion.place_ref, bf16[16,32,128]{2,1,0:T(8,128)(2,1)S(1)} %all-to-all-done.bias_ref, bf16[8,128,128]{2,1,0:T(8,128)(2,1)S(1)} %get-tuple-element.29.normed_ref, ...), custom_call_target="tpu_custom_call" | custom-call | tf_op jit(solution)/shard_map/attend/pallas_call | solution.py:442
  23.8 0.0 copy-start
  23.9 0.0 copy-start.2
  23.9 13.0 %all_to_all.20.parts_ref = bf16[16,72,128]{2,1,0:T(8,128)(2,1)S(1)} all-to-all(bf16[16,72,128]{2,1,0:T(8,128)(2,1)S(1)} %get-tuple-element.34), channel_id=1, replica_groups=mesh['dp'=32,'dap'=16] {'dap'}, dimensions={0} | all-to-all | bytes 589824 | tf_op jit(solution)/shard_map/all_to_all | solution.py:455
  36.9 0.2 bias_grad.1
  37.1 0.0 copy-done
  37.1 6.7 %all-gather = bf16[192,128]{1,0:T(8,128)(2,1)S(1)} all-gather(bf16[48,128]{1,0:T(8,128)(2,1)S(1)} %get-tuple-element.39), channel_id=2, replica_groups={{0,16,32,48},{64,80,96,112},{128,144,160,176},{192,208,224,240},{256,27..., dimensions={0}, use_global_device_ids=true | all-gather | bytes 61440 | tf_op jit(solution)/shard_map/all_gather | solution.py:524
  43.8 0.0 copy-done.2
  43.9 18.8 %all_to_all.21.sums_ref = bf16[8,48,128]{2,1,0:T(8,128)(2,1)S(1)} all-to-all(bf16[8,48,128]{2,1,0:T(8,128)(2,1)S(1)} %pair.1), channel_id=1, replica_groups={{0,64,128,192,256,320,384,448},{16,80,144,208,272,336,400,464},{32,96,1..., dimensions={0} | all-to-all | bytes 196608 | tf_op jit(solution)/shard_map/all_to_all | solution.py:455
  62.7 0.7 sum.1
  63.4 4.5 %all-to-all-start.3 = ((bf16[16,48,128]{2,1,0:T(8,128)(2,1)}), bf16[16,48,128]{2,1,0:T(8,128)(2,1)S(1)}, u32[]{:S(2)}, u32[]{:S(2)}) async-start(bf16[16,48,128]{2,1,0:T(8,128)(2,1)} %sum.1), calls=%async_computation.3 | async-start | bytes 393216 | tf_op jit(solution)/shard_map/all_to_all | solution.py:455
  67.8 0.0 copy-start.1
  67.8 0.0 copy-start.3
  67.8 0.0 copy-start.4
  67.8 4.0 %finish.1 = (bf16[8,128,128]{2,1,0:T(8,128)(2,1)}, bf16[8,128,128]{2,1,0:T(8,128)(2,1)}) custom-call(s32[2]{0:T(128)S(1)} %pad_add_fusion.place_ref, bf16[32,128]{1,0:T(8,128)(2,1)S(1)} %get-tuple-element.40.bias_grad_ref, bf16[8,128,128]{2,1,0:T(8,128)(2,1)} %copy-done.2, f32[8,128,128]{2,1,0:T(8,128)} %copy-done, bf16[8,128,128]{2,1,0:T(8,128)(2,1)} %bitcast.20, ...), custom_call_target="tpu_custom_call" | custom-call | flops 2000000000 | bytes 6000000 | tf_op jit(solution)/shard_map/finish/pallas_call | solution.py:442
  71.9 4.4 %all-to-all-done.3.blocks_ref = bf16[16,48,128]{2,1,0:T(8,128)(2,1)S(1)} async-done(((bf16[16,48,128]{2,1,0:T(8,128)(2,1)}), bf16[16,48,128]{2,1,0:T(8,128)(2,1)S(1)}, u32[]{:S(2)}, u32[]{:S(2)}) %all-to-all-start.3) | async-done | bytes 196640 | tf_op jit(solution)/shard_map/all_to_all | solution.py:455
  76.3 0.0 copy-done.1
  76.3 0.0 copy-done.3
  76.3 0.0 copy-done.4
  76.3 0.8 assemble.1
  (1 shorter events, 0.0 us)
Async XLA Ops:
  2.9 17.1 %all-to-all-start = ((bf16[16,32,128]{2,1,0:T(8,128)(2,1)}), bf16[16,32,128]{2,1,0:T(8,128)(2,1)S(1)}, u32[]{:S(2)}, u32[]{:S(2)}) async-start(bf16[16,32,128]{2,1,0:T(8,128)(2,1)} %get-tuple-element.28), calls=%async_computation | async-start | bytes 262144 | tf_op jit(solution)/shard_map/all_to_all | solution.py:455
  23.8 13.3 %copy-start = (f32[8,128,128]{2,1,0:T(8,128)}, f32[8,128,128]{2,1,0:T(8,128)S(1)}, u32[]{:S(2)}) copy-start(f32[8,128,128]{2,1,0:T(8,128)S(1)} %get-tuple-element.37.normed_proj_ref.normed_proj_hbm) | copy-start | bytes 1572868
  23.9 20.0 %copy-start.2 = (bf16[8,128,128]{2,1,0:T(8,128)(2,1)}, bf16[8,128,128]{2,1,0:T(8,128)(2,1)S(1)}, u32[]{:S(2)}) copy-start(bf16[8,128,128]{2,1,0:T(8,128)(2,1)S(1)} %get-tuple-element.36.mixed_ref.mixed_hbm) | copy-start | bytes 786436
  63.4 12.9 %all-to-all-start.3 = ((bf16[16,48,128]{2,1,0:T(8,128)(2,1)}), bf16[16,48,128]{2,1,0:T(8,128)(2,1)S(1)}, u32[]{:S(2)}, u32[]{:S(2)}) async-start(bf16[16,48,128]{2,1,0:T(8,128)(2,1)} %sum.1), calls=%async_computation.3 | async-start | bytes 393216 | tf_op jit(solution)/shard_map/all_to_all | solution.py:455
  67.8 8.5 %copy-start.1 = (bf16[128,512]{1,0:T(8,128)(2,1)S(1)}, bf16[128,512]{1,0:T(8,128)(2,1)}, u32[]{:S(2)}) copy-start(bf16[128,512]{1,0:T(8,128)(2,1)} %proj_weight_ref.1) | copy-start | bytes 393220
  67.8 8.5 %copy-start.3 = (bf16[128,4]{0,1:T(4,128)(2,1)S(1)}, bf16[128,4]{0,1:T(4,128)(2,1)}, u32[]{:S(2)}) copy-start(bf16[128,4]{0,1:T(4,128)(2,1)} %param.14) | copy-start | bytes 3076
  67.8 8.4 %copy-start.4 = (f32[128]{0:T(128)S(1)}, f32[128]{0:T(128)}, u32[]{:S(2)}) copy-start(f32[128]{0:T(128)} %param.15) | copy-start | bytes 1540

commit v9 on v8

--- a/solution.py
+++ b/solution.py
@@ -91,7 +91,7 @@
         normed = (x_hat * gain[...]).astype(BF16)
         normed_ref[row] = normed
         held[pl.ds(row, heads, stride=row_count), :] = contract(bias_weight[...], normed, 1, 1)
-    block = held[...].astype(BF16)
+    block = held[: heads * row_count].astype(BF16)
     for peer in range(bias_ref.shape[0]):
         bias_ref[peer] = block
     for copy in copies[3:]:
@@ -285,7 +285,7 @@
             grad_bias[h * row_count : (h + 1) * row_count], 0, keepdims=True
         )
     held[grads + heads : grads + heads + 1] = shift_ref[...]
-    own_ref[...] = held[...].astype(BF16)
+    own_ref[...] = held[: own_ref.shape[0]].astype(BF16)
 
 
 def pair_kernel(near_ref, sums_ref):
@@ -468,7 +468,7 @@
             (rows_shape, BF16),
             line,
             (bias_weight_t.shape, BF16),
-            ((shared, width), F32),
+            ((row_count * row_count, width), F32),
         ],
         sems=len(inputs),
     )
@@ -515,7 +515,7 @@
         "bias_grad",
         (parts, normed, shift, mixed, normed_proj),
         [((shared, width), BF16), ((chunk, channels), BF16)],
-        [((chunk, channels), F32)],
+        [((chunk + 8, channels), F32)],
         near=5,
     )
     near = 4

time: 77.5 us -> 77.5 us (level)
  no operation moved by 1% of the time
where the time goes in v9:
time: 77.5 us; the launch traced here: 77.1 us
  blocking collectives  38.5 us (50%)
  Pallas kernels  13.7 us (18%)
  starting transfers between devices  13.6 us (18%)
  waiting for transfers between devices  9.71 us (13%)
  between operations  1.38 us (2%)
    all_to_all x2, blocking collectives, exchange(): lax.all_to_all(blocks, axis, 0, 0, axis_index_groups=groups, tiled=True)  31.8 us
    pallas_call x8, Pallas kernels, call(): pl.pallas_call(kernel, out_shape=tuple((jax.ShapeDtypeStruct(shape, dtype...  13.7 us
    all_to_all x2, starting transfers between devices, exchange(): lax.all_to_all(blocks, axis, 0, 0, axis_index_groups=groups, tiled=True)  13.6 us
    all_to_all x2, waiting for transfers between devices, exchange(): lax.all_to_all(blocks, axis, 0, 0, axis_index_groups=groups, tiled=True)  9.71 us
    all_gather x1, blocking collectives, per_device(): gathered = lax.all_gather(own, 'dp', axis=0, axis_index_groups=runs)  6.73 us
  transfers between devices with their start and end apart: 2, of which 2 were waited for; matrix products, arithmetic and copies ran while one was open for 0% of the time, Pallas kernels for 8%

profile of v9, /device:TPU:8, one launch (start us, length us, event | category | flops | bytes accessed | tf_op | source)
XLA Modules:
  0.0 77.1 jit_solution(9711311679780325571)
XLA Ops:
  0.6 2.2 %norm.1 = (bf16[8,128,128]{2,1,0:T(8,128)(2,1)S(1)}, bf16[16,32,128]{2,1,0:T(8,128)(2,1)}, bf16[128,512]{1,0:T(8,128)(2,1)S(1)}, f32[1,128]{1,0:T(1,128)S(1)}) custom-call(bf16[8,128,128]{2,1,0:T(8,128)(2,1)} %bitcast.19, f32[1,128]{1,0:T(1,128)} %bitcast.16, bf16[4,128]{1,0:T(4,128)(2,1)} %bitcast.13, bf16[128,512]{1,0:T(8,128)(2,1)} %proj_weight_ref.1, ...), custom_call_target="tpu_custom_call" | custom-call | tf_op jit(solution)/shard_map/norm/pallas_call | solution.py:442
  2.9 9.1 %all-to-all-start = ((bf16[16,32,128]{2,1,0:T(8,128)(2,1)}), bf16[16,32,128]{2,1,0:T(8,128)(2,1)S(1)}, u32[]{:S(2)}, u32[]{:S(2)}) async-start(bf16[16,32,128]{2,1,0:T(8,128)(2,1)} %get-tuple-element.28), calls=%async_computation | async-start | bytes 262144 | tf_op jit(solution)/shard_map/all_to_all | solution.py:455
  12.7 0.1 pad_add_fusion.place_ref
  12.7 2.0 %project.1 = (bf16[8,960,128]{2,1,0:T(8,128)(2,1)S(1)}, f32[8,256,128]{2,1,0:T(8,128)S(1)}) custom-call(s32[2]{0:T(128)S(1)} %pad_add_fusion.place_ref, bf16[8,128,128]{2,1,0:T(8,128)(2,1)S(1)} %get-tuple-element.29.normed_ref, bf16[128,512]{1,0:T(8,128)(2,1)S(1)} %get-tuple-element.30.proj_weight_ref, f32[1,128]{1,0:T(1,128)S(1)} %get-tuple-element.31.gate_shift_ref, ...), custom_call_target="tpu_custom_call" | custom-call | flops 3000000000 | bytes 10000000 | tf_op jit(solution)/shard_map/project/pallas_call | solution.py:442
  14.7 5.3 %all-to-all-done.bias_ref = bf16[16,32,128]{2,1,0:T(8,128)(2,1)S(1)} async-done(((bf16[16,32,128]{2,1,0:T(8,128)(2,1)}), bf16[16,32,128]{2,1,0:T(8,128)(2,1)S(1)}, u32[]{:S(2)}, u32[]{:S(2)}) %all-to-all-start) | async-done | bytes 131104 | tf_op jit(solution)/shard_map/all_to_all | solution.py:455
  20.0 3.8 %attend.1 = (bf16[16,72,128]{2,1,0:T(8,128)(2,1)S(1)}, bf16[8,128,128]{2,1,0:T(8,128)(2,1)S(1)}, f32[8,128,128]{2,1,0:T(8,128)S(1)}, f32[1,128]{1,0:T(1,128)S(1)}) custom-call(s32[2]{0:T(128)S(1)} %pad_add_fusion.place_ref, bf16[16,32,128]{2,1,0:T(8,128)(2,1)S(1)} %all-to-all-done.bias_ref, bf16[8,128,128]{2,1,0:T(8,128)(2,1)S(1)} %get-tuple-element.29.normed_ref, ...), custom_call_target="tpu_custom_call" | custom-call | tf_op jit(solution)/shard_map/attend/pallas_call | solution.py:442
  23.8 0.0 copy-start
  23.9 0.0 copy-start.2
  23.9 13.0 %all_to_all.20.parts_ref = bf16[16,72,128]{2,1,0:T(8,128)(2,1)S(1)} all-to-all(bf16[16,72,128]{2,1,0:T(8,128)(2,1)S(1)} %get-tuple-element.34), channel_id=1, replica_groups=mesh['dp'=32,'dap'=16] {'dap'}, dimensions={0} | all-to-all | bytes 589824 | tf_op jit(solution)/shard_map/all_to_all | solution.py:455
  36.9 0.2 bias_grad.1
  37.1 0.0 copy-done
  37.1 6.7 %all-gather = bf16[192,128]{1,0:T(8,128)(2,1)S(1)} all-gather(bf16[48,128]{1,0:T(8,128)(2,1)S(1)} %get-tuple-element.39), channel_id=2, replica_groups={{0,16,32,48},{64,80,96,112},{128,144,160,176},{192,208,224,240},{256,27..., dimensions={0}, use_global_device_ids=true | all-gather | bytes 61440 | tf_op jit(solution)/shard_map/all_gather | solution.py:524
  43.8 0.0 copy-done.2
  43.9 18.8 %all_to_all.21.sums_ref = bf16[8,48,128]{2,1,0:T(8,128)(2,1)S(1)} all-to-all(bf16[8,48,128]{2,1,0:T(8,128)(2,1)S(1)} %pair.1), channel_id=1, replica_groups={{0,64,128,192,256,320,384,448},{16,80,144,208,272,336,400,464},{32,96,1..., dimensions={0} | all-to-all | bytes 196608 | tf_op jit(solution)/shard_map/all_to_all | solution.py:455
  62.7 0.7 sum.1
  63.4 4.5 %all-to-all-start.3 = ((bf16[16,48,128]{2,1,0:T(8,128)(2,1)}), bf16[16,48,128]{2,1,0:T(8,128)(2,1)S(1)}, u32[]{:S(2)}, u32[]{:S(2)}) async-start(bf16[16,48,128]{2,1,0:T(8,128)(2,1)} %sum.1), calls=%async_computation.3 | async-start | bytes 393216 | tf_op jit(solution)/shard_map/all_to_all | solution.py:455
  67.8 0.0 copy-start.1
  67.8 0.0 copy-start.3
  67.8 0.0 copy-start.4
  67.8 4.0 %finish.1 = (bf16[8,128,128]{2,1,0:T(8,128)(2,1)}, bf16[8,128,128]{2,1,0:T(8,128)(2,1)}) custom-call(s32[2]{0:T(128)S(1)} %pad_add_fusion.place_ref, bf16[32,128]{1,0:T(8,128)(2,1)S(1)} %get-tuple-element.40.bias_grad_ref, bf16[8,128,128]{2,1,0:T(8,128)(2,1)} %copy-done.2, f32[8,128,128]{2,1,0:T(8,128)} %copy-done, bf16[8,128,128]{2,1,0:T(8,128)(2,1)} %bitcast.20, ...), custom_call_target="tpu_custom_call" | custom-call | flops 2000000000 | bytes 6000000 | tf_op jit(solution)/shard_map/finish/pallas_call | solution.py:442
  71.9 4.4 %all-to-all-done.3.blocks_ref = bf16[16,48,128]{2,1,0:T(8,128)(2,1)S(1)} async-done(((bf16[16,48,128]{2,1,0:T(8,128)(2,1)}), bf16[16,48,128]{2,1,0:T(8,128)(2,1)S(1)}, u32[]{:S(2)}, u32[]{:S(2)}) %all-to-all-start.3) | async-done | bytes 196640 | tf_op jit(solution)/shard_map/all_to_all | solution.py:455
  76.3 0.0 copy-done.1
  76.3 0.0 copy-done.3
  76.3 0.0 copy-done.4
  76.3 0.8 assemble.1
  (1 shorter events, 0.0 us)
Async XLA Ops:
  2.9 17.1 %all-to-all-start = ((bf16[16,32,128]{2,1,0:T(8,128)(2,1)}), bf16[16,32,128]{2,1,0:T(8,128)(2,1)S(1)}, u32[]{:S(2)}, u32[]{:S(2)}) async-start(bf16[16,32,128]{2,1,0:T(8,128)(2,1)} %get-tuple-element.28), calls=%async_computation | async-start | bytes 262144 | tf_op jit(solution)/shard_map/all_to_all | solution.py:455
  23.8 13.3 %copy-start = (f32[8,128,128]{2,1,0:T(8,128)}, f32[8,128,128]{2,1,0:T(8,128)S(1)}, u32[]{:S(2)}) copy-start(f32[8,128,128]{2,1,0:T(8,128)S(1)} %get-tuple-element.37.normed_proj_ref.normed_proj_hbm) | copy-start | bytes 1572868
  23.9 20.0 %copy-start.2 = (bf16[8,128,128]{2,1,0:T(8,128)(2,1)}, bf16[8,128,128]{2,1,0:T(8,128)(2,1)S(1)}, u32[]{:S(2)}) copy-start(bf16[8,128,128]{2,1,0:T(8,128)(2,1)S(1)} %get-tuple-element.36.mixed_ref.mixed_hbm) | copy-start | bytes 786436
  63.4 12.9 %all-to-all-start.3 = ((bf16[16,48,128]{2,1,0:T(8,128)(2,1)}), bf16[16,48,128]{2,1,0:T(8,128)(2,1)S(1)}, u32[]{:S(2)}, u32[]{:S(2)}) async-start(bf16[16,48,128]{2,1,0:T(8,128)(2,1)} %sum.1), calls=%async_computation.3 | async-start | bytes 393216 | tf_op jit(solution)/shard_map/all_to_all | solution.py:455
  67.8 8.5 %copy-start.1 = (bf16[128,512]{1,0:T(8,128)(2,1)S(1)}, bf16[128,512]{1,0:T(8,128)(2,1)}, u32[]{:S(2)}) copy-start(bf16[128,512]{1,0:T(8,128)(2,1)} %proj_weight_ref.1) | copy-start | bytes 393220
  67.8 8.5 %copy-start.3 = (bf16[128,4]{0,1:T(4,128)(2,1)S(1)}, bf16[128,4]{0,1:T(4,128)(2,1)}, u32[]{:S(2)}) copy-start(bf16[128,4]{0,1:T(4,128)(2,1)} %param.14) | copy-start | bytes 3076
  67.8 8.4 %copy-start.4 = (f32[128]{0:T(128)S(1)}, f32[128]{0:T(128)}, u32[]{:S(2)}) copy-start(f32[128]{0:T(128)} %param.15) | copy-start | bytes 1540

commit v10 on v9

--- a/solution.py
+++ b/solution.py
@@ -107,9 +107,9 @@
     cot_hbm,
     out_weight_hbm,
     narrow_ref,
-    wide_ref,
     cot,
     out_weight,
+    gating,
     sems,
 ):
     row_count, width, channels = cot.shape
@@ -117,9 +117,6 @@
     copies = begin_all((cot_hbm, out_weight_hbm), (cot, out_weight), sems)
     length, first_row = place_ref[0], place_ref[1]
     weight_t = proj_weight_ref[...].T
-    share = weight_t.shape[0] // row_count
-    for row in range(row_count):
-        narrow_ref[row, 5 * width + 2 * channels :] = weight_t[row * share : (row + 1) * share]
     weight_t = weight_t[channels : 3 * channels]
     token = lax.broadcasted_iota(jnp.int32, (width, channels), 0)
 
@@ -132,8 +129,11 @@
         place(row, 0, projected[:, :channels] * scaling)
         place(row, 3, projected[:, channels : 2 * channels])
         place(row, 4, projected[:, 2 * channels : 3 * channels])
-        wide_ref[row, :width] = jax.nn.sigmoid(projected[:, 3 * channels :] + gate_shift_ref[...])
-        narrow_ref[row, 5 * width : 5 * width + 2 * channels] = contract(
+        gate = jax.nn.sigmoid(projected[:, 3 * channels :] + gate_shift_ref[...])
+        gating[row] = gate
+        place(row, 6, gate)
+        place(row, 7, normed)
+        narrow_ref[row, 8 * width :] = contract(
             weight_t, normed, 1, 1
         ).astype(BF16)
         return carry
@@ -142,9 +142,9 @@
         live = token < jnp.where(first_row + row < length, length, 0)
         d_output = jnp.where(live, cot[row].astype(F32), 0.0).astype(BF16)
         d_mixed = contract(d_output, out_weight[...], 1, 1)
-        place(row, 1, d_mixed * wide_ref[row, :width])
+        place(row, 1, d_mixed * gating[row])
         place(row, 2, d_output)
-        wide_ref[row, width:] = d_mixed
+        place(row, 5, d_mixed)
         return carry
 
     lax.fori_loop(0, row_count, forward, 0, unroll=UNROLL_PROJECT)
@@ -156,20 +156,16 @@
 def attend_kernel(
     place_ref,
     bias_ref,
-    normed_ref,
     narrow_ref,
-    wide_ref,
     parts_ref,
     mixed_ref,
-    normed_proj_ref,
+    d_proj_ref,
     shift_ref,
     bias_t,
     bias_sum,
     parts,
-    d_proj,
-    weight_t,
 ):
-    row_count, width, channels = normed_ref.shape
+    row_count, width, channels = mixed_ref.shape
     heads = bias_t.shape[0] // width
     head_size = channels // heads
     scaling = head_size ** (-0.5)
@@ -185,16 +181,13 @@
         bias_t[h * width : (h + 1) * width] = jnp.where(key_live, turned, DEAD)
     bias_sum[...] = jnp.zeros_like(bias_sum)
     lane_masks = head_masks((width, channels), 1, heads)
-    share = weight_t.shape[0] // row_count
-    for row in range(row_count):
-        weight_t[row * share : (row + 1) * share] = narrow_ref[row, 5 * width + 2 * channels :]
 
     def one_row(row, shift_sum):
         weights, lows, attended_t, d_query_t = [], [], [], []
         queries, d_attend, _, keys, values = (
             narrow_ref[row, n * width : (n + 1) * width] for n in range(5)
         )
-        turned = narrow_ref.at[row, 5 * width :]
+        turned = narrow_ref.at[row, 8 * width :]
         scores = contract(stack_heads(keys, lane_masks), queries, 1, 1)
         grads = contract(stack_heads(values, lane_masks), d_attend, 1, 1)
         for h in range(heads):
@@ -215,10 +208,10 @@
         d_query = jnp.concatenate(d_query_t, 0).T
         d_value = pick_heads(dot(jnp.concatenate(weights, 0), d_attend), lane_masks)
         d_key = pick_heads(dot(jnp.concatenate(lows, 0), queries), lane_masks)
-        gating = wide_ref[row, :width]
+        gating = narrow_ref[row, 6 * width : 7 * width].astype(F32)
         mixed = gating * attended
         mixed_ref[row] = mixed.astype(BF16)
-        d_gating = (wide_ref[row, width:] * mixed * (1.0 - gating)).astype(BF16)
+        d_gating = (narrow_ref[row, 5 * width : 6 * width].astype(F32) * mixed * (1.0 - gating)).astype(BF16)
         d_row = jnp.concatenate(
             [
                 (d_query * scaling).astype(BF16),
@@ -228,13 +221,12 @@
             ],
             1,
         )
-        d_proj[row] = d_row
+        d_proj_ref[row] = d_row
         return shift_sum + jnp.sum(d_gating.astype(F32), 0, keepdims=True)
 
     zero = jnp.zeros((1, channels), F32)
     shift_ref[...] = lax.fori_loop(0, row_count, one_row, zero, unroll=UNROLL_ATTEND)
-    flat = d_proj[...].reshape(row_count * width, 4 * channels)
-    normed_proj_ref[...] = dot(flat, weight_t[...]).reshape(normed_proj_ref.shape)
+    flat = d_proj_ref[...].reshape(row_count * width, 4 * channels)
     shared = heads * row_count
     for h in range(heads):
         turned = bias_sum[h * width : (h + 1) * width].T
@@ -243,7 +235,7 @@
                 d * row_count : (d + 1) * row_count
             ]
     tokens = row_count * width
-    normed = normed_ref[...].reshape(tokens, channels)
+    normed = narrow_ref[:, 7 * width : 8 * width].reshape(tokens, channels)
     grad_proj = contract(normed, flat, 0, 0)
     grad_out = contract(
         mixed_ref[...].reshape(tokens, channels),
@@ -260,9 +252,9 @@
 
 
 def bias_kernel(
-    parts_ref, normed_ref, shift_ref, mixed_ref, normed_proj_ref, bias_grad_ref, own_ref, held
+    parts_ref, normed_ref, shift_ref, mixed_ref, d_proj_ref, bias_grad_ref, own_ref, held
 ):
-    del mixed_ref, normed_proj_ref
+    del mixed_ref, d_proj_ref
     row_count, width, channels = normed_ref.shape
     shared = bias_grad_ref.shape[0]
     heads = shared // row_count
@@ -301,7 +293,8 @@
     place_ref,
     bias_grad_ref,
     mixed_hbm,
-    normed_proj_hbm,
+    d_proj_hbm,
+    proj_weight_hbm,
     pair_hbm,
     cot_hbm,
     gain_hbm,
@@ -315,6 +308,8 @@
     bias_weight_ref,
     out_weight_ref,
     mixed_ref,
+    d_proj_ref,
+    proj_weight_ref,
     normed_proj_ref,
     sems,
 ):
@@ -326,7 +321,8 @@
             bias_weight_hbm,
             out_weight_hbm,
             mixed_hbm,
-            normed_proj_hbm,
+            d_proj_hbm,
+            proj_weight_hbm,
         ),
         (
             pair_ref,
@@ -335,7 +331,8 @@
             bias_weight_ref,
             out_weight_ref,
             mixed_ref,
-            normed_proj_ref,
+            d_proj_ref,
+            proj_weight_ref,
         ),
         sems,
     )
@@ -347,6 +344,10 @@
     of_row = lax.broadcasted_iota(jnp.int32, bias_grad.shape, 0) % row_count
     for copy in copies:
         copy.wait()
+    flat = d_proj_ref[...].reshape(row_count * width, 4 * channels)
+    normed_proj_ref[...] = contract(flat, proj_weight_ref[...], 1, 1).reshape(
+        normed_proj_ref.shape
+    )
     weight = bias_weight_ref[...].astype(F32)
     spread = jnp.concatenate(
         [jnp.broadcast_to(weight[h : h + 1], (row_count, channels)) for h in range(heads)], 0
@@ -474,46 +475,43 @@
     )
     bias_all = exchange(bias_copies, "dap")
     place = jnp.stack([lengths[0], lax.axis_index("dap") * row_count]).astype(jnp.int32)
-    narrow, wide = call(
+    (narrow,) = call(
         functools.partial(project_kernel, heads),
         "project",
         (place, normed, near_proj, near_shift, cot, out_weight),
         [
-            ((row_count, 5 * width + 2 * channels + 4 * channels // row_count, width), BF16),
-            ((row_count, 2 * width, channels), F32),
+            ((row_count, 8 * width + 2 * channels, width), BF16),
         ],
-        [(rows_shape, BF16), (out_weight.shape, BF16)],
+        [(rows_shape, BF16), (out_weight.shape, BF16), (rows_shape, F32)],
         placed=True,
         near=3,
         sems=2,
         flops=3 * 10**9,
         moved=10**7,
     )
-    parts, mixed, normed_proj, shift = call(
+    parts, mixed, d_proj, shift = call(
         attend_kernel,
         "attend",
-        (place, bias_all, normed, narrow, wide),
+        (place, bias_all, narrow),
         [
             ((devices, shared + 5 * row_count, width), BF16),
             (rows_shape, BF16),
-            (rows_shape, F32),
+            ((row_count, width, 4 * channels), BF16),
             line,
         ],
         [
             ((heads * width, width), F32),
             ((heads * width, width), F32),
             ((devices, shared + 5 * row_count, width), F32),
-            ((row_count, width, 4 * channels), BF16),
-            ((4 * channels, channels), BF16),
         ],
         placed=True,
-        near=4,
+        near=2,
     )
     parts = exchange(parts, "dap")
     bias_grad, own = call(
         bias_kernel,
         "bias_grad",
-        (parts, normed, shift, mixed, normed_proj),
+        (parts, normed, shift, mixed, d_proj),
         [((shared, width), BF16), ((chunk, channels), BF16)],
         [((chunk + 8, channels), F32)],
         near=5,
@@ -534,7 +532,18 @@
     updated, pair_grad = call(
         finish_kernel,
         "finish",
-        (place, bias_grad, mixed, normed_proj, pair, cot, gain, bias_weight_t, out_weight),
+        (
+            place,
+            bias_grad,
+            mixed,
+            d_proj,
+            proj_weight,
+            pair,
+            cot,
+            gain,
+            bias_weight_t,
+            out_weight,
+        ),
         [(rows_shape, BF16), (rows_shape, BF16)],
         [
             (rows_shape, BF16),
@@ -543,11 +552,13 @@
             (bias_weight_t.shape, BF16),
             (out_weight.shape, BF16),
             (rows_shape, BF16),
+            ((row_count, width, 4 * channels), BF16),
+            (proj_weight.shape, BF16),
             (rows_shape, F32),
         ],
         placed=True,
         near=1,
-        sems=7,
+        sems=8,
         flops=2 * 10**9,
         moved=6 * 10**6,
     )

time: 77.5 us -> 77.3 us (level)
  no operation moved by 1% of the time
where the time goes in v10:
time: 77.3 us; the launch traced here: 76.9 us
  blocking collectives  38.5 us (50%)
  Pallas kernels  13.7 us (18%)
  starting transfers between devices  13.6 us (18%)
  waiting for transfers between devices  9.56 us (12%)
  between operations  1.38 us (2%)
    all_to_all x2, blocking collectives, exchange(): lax.all_to_all(blocks, axis, 0, 0, axis_index_groups=groups, tiled=True)  31.8 us
    pallas_call x8, Pallas kernels, call(): pl.pallas_call(kernel, out_shape=tuple((jax.ShapeDtypeStruct(shape, dtype...  13.7 us
    all_to_all x2, starting transfers between devices, exchange(): lax.all_to_all(blocks, axis, 0, 0, axis_index_groups=groups, tiled=True)  13.6 us
    all_to_all x2, waiting for transfers between devices, exchange(): lax.all_to_all(blocks, axis, 0, 0, axis_index_groups=groups, tiled=True)  9.56 us
    all_gather x1, blocking collectives, per_device(): gathered = lax.all_gather(own, 'dp', axis=0, axis_index_groups=runs)  6.73 us
  transfers between devices with their start and end apart: 2, of which 2 were waited for; matrix products, arithmetic and copies ran while one was open for 0% of the time, Pallas kernels for 8%

profile of v10, /device:TPU:8, one launch (start us, length us, event | category | flops | bytes accessed | tf_op | source)
XLA Modules:
  0.0 76.9 jit_solution(14788215560737634348)
XLA Ops:
  0.6 2.2 %norm.1 = (bf16[8,128,128]{2,1,0:T(8,128)(2,1)S(1)}, bf16[16,32,128]{2,1,0:T(8,128)(2,1)}, bf16[128,512]{1,0:T(8,128)(2,1)S(1)}, f32[1,128]{1,0:T(1,128)S(1)}) custom-call(bf16[8,128,128]{2,1,0:T(8,128)(2,1)} %bitcast.19, f32[1,128]{1,0:T(1,128)} %bitcast.16, bf16[4,128]{1,0:T(4,128)(2,1)} %bitcast.13, bf16[128,512]{1,0:T(8,128)(2,1)} %proj_weight_ref.1, ...), custom_call_target="tpu_custom_call" | custom-call | tf_op jit(solution)/shard_map/norm/pallas_call | solution.py:443
  2.9 9.1 %all-to-all-start = ((bf16[16,32,128]{2,1,0:T(8,128)(2,1)}), bf16[16,32,128]{2,1,0:T(8,128)(2,1)S(1)}, u32[]{:S(2)}, u32[]{:S(2)}) async-start(bf16[16,32,128]{2,1,0:T(8,128)(2,1)} %get-tuple-element.26), calls=%async_computation | async-start | bytes 262144 | tf_op jit(solution)/shard_map/all_to_all | solution.py:456
  12.7 0.1 pad_add_fusion.place_ref
  12.7 2.0 %project.1.narrow_ref = bf16[8,1280,128]{2,1,0:T(8,128)(2,1)S(1)} custom-call(s32[2]{0:T(128)S(1)} %pad_add_fusion.place_ref, bf16[8,128,128]{2,1,0:T(8,128)(2,1)S(1)} %get-tuple-element.27.normed_ref, bf16[128,512]{1,0:T(8,128)(2,1)S(1)} %get-tuple-element.28.proj_weight_ref, f32[1,128]{1,0:T(1,128)S(1)} %get-tuple-element.29.gate_shift_ref, ...), custom_call_target="tpu_custom_call" | custom-call | flops 3000000000 | bytes 10000000 | tf_op jit(solution)/shard_map/project/pallas_call | solution.py:443
  14.7 5.3 %all-to-all-done.bias_ref = bf16[16,32,128]{2,1,0:T(8,128)(2,1)S(1)} async-done(((bf16[16,32,128]{2,1,0:T(8,128)(2,1)}), bf16[16,32,128]{2,1,0:T(8,128)(2,1)S(1)}, u32[]{:S(2)}, u32[]{:S(2)}) %all-to-all-start) | async-done | bytes 131104 | tf_op jit(solution)/shard_map/all_to_all | solution.py:456
  20.0 3.7 %attend.1 = (bf16[16,72,128]{2,1,0:T(8,128)(2,1)S(1)}, bf16[8,128,128]{2,1,0:T(8,128)(2,1)S(1)}, bf16[8,128,512]{2,1,0:T(8,128)(2,1)S(1)}, f32[1,128]{1,0:T(1,128)S(1)}) custom-call(s32[2]{0:T(128)S(1)} %pad_add_fusion.place_ref, bf16[16,32,128]{2,1,0:T(8,128)(2,1)S(1)} %all-to-all-done.bias_ref, bf16[8,1280,128]{2,1,0:T(8,128)(2,1)S(1)} %project.1.narrow_ref), custom_call_target="tpu_custom_call" | custom-call | tf_op jit(solution)/shard_map/attend/pallas_call | solution.py:443
  23.7 0.0 copy-start
  23.7 0.0 copy-start.2
  23.7 13.0 %all_to_all.20.parts_ref = bf16[16,72,128]{2,1,0:T(8,128)(2,1)S(1)} all-to-all(bf16[16,72,128]{2,1,0:T(8,128)(2,1)S(1)} %get-tuple-element.30), channel_id=1, replica_groups=mesh['dp'=32,'dap'=16] {'dap'}, dimensions={0} | all-to-all | bytes 589824 | tf_op jit(solution)/shard_map/all_to_all | solution.py:456
  36.7 0.2 bias_grad.1
  36.9 0.0 copy-done
  36.9 6.7 %all-gather = bf16[192,128]{1,0:T(8,128)(2,1)S(1)} all-gather(bf16[48,128]{1,0:T(8,128)(2,1)S(1)} %get-tuple-element.35), channel_id=2, replica_groups={{0,16,32,48},{64,80,96,112},{128,144,160,176},{192,208,224,240},{256,27..., dimensions={0}, use_global_device_ids=true | all-gather | bytes 61440 | tf_op jit(solution)/shard_map/all_gather | solution.py:522
  43.7 18.8 %all_to_all.21.sums_ref = bf16[8,48,128]{2,1,0:T(8,128)(2,1)S(1)} all-to-all(bf16[8,48,128]{2,1,0:T(8,128)(2,1)S(1)} %pair.1), channel_id=1, replica_groups={{0,64,128,192,256,320,384,448},{16,80,144,208,272,336,400,464},{32,96,1..., dimensions={0} | all-to-all | bytes 196608 | tf_op jit(solution)/shard_map/all_to_all | solution.py:456
  62.5 0.7 sum.1
  63.2 4.5 %all-to-all-start.3 = ((bf16[16,48,128]{2,1,0:T(8,128)(2,1)}), bf16[16,48,128]{2,1,0:T(8,128)(2,1)S(1)}, u32[]{:S(2)}, u32[]{:S(2)}) async-start(bf16[16,48,128]{2,1,0:T(8,128)(2,1)} %sum.1), calls=%async_computation.3 | async-start | bytes 393216 | tf_op jit(solution)/shard_map/all_to_all | solution.py:456
  67.7 0.0 copy-done.2
  67.7 0.0 copy-start.1
  67.7 0.0 copy-start.3
  67.7 0.0 copy-start.4
  67.7 4.1 %finish.1 = (bf16[8,128,128]{2,1,0:T(8,128)(2,1)}, bf16[8,128,128]{2,1,0:T(8,128)(2,1)}) custom-call(s32[2]{0:T(128)S(1)} %pad_add_fusion.place_ref, bf16[32,128]{1,0:T(8,128)(2,1)S(1)} %get-tuple-element.36.bias_grad_ref, bf16[8,128,128]{2,1,0:T(8,128)(2,1)} %copy-done.2, bf16[8,128,512]{2,1,0:T(8,128)(2,1)} %copy-done, bf16[128,512]{1,0:T(8,128)(2,1)} %proj_weight_ref.1, ...), custom_call_target="tpu_custom_call" | custom-call | flops 2000000000 | bytes 6000000 | tf_op jit(solution)/shard_map/finish/pallas_call | solution.py:443
  71.8 4.3 %all-to-all-done.3.blocks_ref = bf16[16,48,128]{2,1,0:T(8,128)(2,1)S(1)} async-done(((bf16[16,48,128]{2,1,0:T(8,128)(2,1)}), bf16[16,48,128]{2,1,0:T(8,128)(2,1)S(1)}, u32[]{:S(2)}, u32[]{:S(2)}) %all-to-all-start.3) | async-done | bytes 196640 | tf_op jit(solution)/shard_map/all_to_all | solution.py:456
  76.1 0.0 copy-done.1
  76.1 0.0 copy-done.3
  76.1 0.0 copy-done.4
  76.1 0.8 assemble.1
  (1 shorter events, 0.0 us)
Async XLA Ops:
  2.9 17.1 %all-to-all-start = ((bf16[16,32,128]{2,1,0:T(8,128)(2,1)}), bf16[16,32,128]{2,1,0:T(8,128)(2,1)S(1)}, u32[]{:S(2)}, u32[]{:S(2)}) async-start(bf16[16,32,128]{2,1,0:T(8,128)(2,1)} %get-tuple-element.26), calls=%async_computation | async-start | bytes 262144 | tf_op jit(solution)/shard_map/all_to_all | solution.py:456
  23.7 13.3 %copy-start = (bf16[8,128,512]{2,1,0:T(8,128)(2,1)}, bf16[8,128,512]{2,1,0:T(8,128)(2,1)S(1)}, u32[]{:S(2)}) copy-start(bf16[8,128,512]{2,1,0:T(8,128)(2,1)S(1)} %get-tuple-element.33.d_proj_ref.d_proj_hbm) | copy-start | bytes 3145732
  23.7 44.0 %copy-start.2 = (bf16[8,128,128]{2,1,0:T(8,128)(2,1)}, bf16[8,128,128]{2,1,0:T(8,128)(2,1)S(1)}, u32[]{:S(2)}) copy-start(bf16[8,128,128]{2,1,0:T(8,128)(2,1)S(1)} %get-tuple-element.32.mixed_ref.mixed_hbm) | copy-start | bytes 786436
  63.2 12.9 %all-to-all-start.3 = ((bf16[16,48,128]{2,1,0:T(8,128)(2,1)}), bf16[16,48,128]{2,1,0:T(8,128)(2,1)S(1)}, u32[]{:S(2)}, u32[]{:S(2)}) async-start(bf16[16,48,128]{2,1,0:T(8,128)(2,1)} %sum.1), calls=%async_computation.3 | async-start | bytes 393216 | tf_op jit(solution)/shard_map/all_to_all | solution.py:456
  67.7 8.5 %copy-start.1 = (bf16[128,512]{1,0:T(8,128)(2,1)S(1)}, bf16[128,512]{1,0:T(8,128)(2,1)}, u32[]{:S(2)}) copy-start(bf16[128,512]{1,0:T(8,128)(2,1)} %proj_weight_ref.1) | copy-start | bytes 393220
  67.7 8.4 %copy-start.3 = (bf16[128,4]{0,1:T(4,128)(2,1)S(1)}, bf16[128,4]{0,1:T(4,128)(2,1)}, u32[]{:S(2)}) copy-start(bf16[128,4]{0,1:T(4,128)(2,1)} %param.14) | copy-start | bytes 3076
  67.7 8.4 %copy-start.4 = (f32[128]{0:T(128)S(1)}, f32[128]{0:T(128)}, u32[]{:S(2)}) copy-start(f32[128]{0:T(128)} %param.15) | copy-start | bytes 1540
